TPU v7x, 512 devices: a whole 4x8x8 slice. The times are simulated.
512 devices in a mesh: plane: 64 (over z, y), dom: 8 (over x, core).
Axes of the slice: x: 4, y: 8, z: 8, core: 2. Of those that a mesh axis runs over, the one named last changes fastest.
Arguments:
- spectral_fields: float32 [4, 256, 512, 128], P(None, 'plane', 'dom')
- deriv_ops: float32 [2, 128, 128], replicated, may hold values from -0.5 to 0.5
- geom: float32 [2, 512, 128], P(None, 'dom'), may hold values from 0.5 to 2
- stiffness: float32 [128, 128], replicated, as said below
- stiff_scale: float32 [512], P('dom'), may hold values from 0.3 to 3
- traces: float32 [4, 16, 128], replicated, may hold values from -0.5 to 0.5
- neighbors: int32 [512, 4], P('dom'), may hold values from -2 to 511, as said below
- rim_lists: int32 [8, 2, 32], P('dom'), may hold values from 0 to 63, as said below
- melt_flags: int32 [256, 512], P(None, ('dom', 'plane')), may hold values 0 or 1
Outputs:
- momentum_terms: float32 [3, 256, 512, 128], P(None, 'plane', 'dom')
- temperature_next: float32 [256, 512, 128], P('plane', 'dom')
Inputs may be any that keep to these rules, and one draw needn't show every extreme that they name: stiffness is symmetric. `neighbors`: elements 64 d to 64 (d + 1) - 1 form partition d, 2 columns around the tube by 32 elements radially. Edges 0 and 2 are radial, -1 at the tube's walls; edges 1 and 3 go around the tube, -2 where the element across lies in the next or previous partition (cyclically), which happens for exactly 32 elements of each partition on each side. Two elements that face each other name each other across edges j and (j + 2) mod 4. Local numbers (0 to 63 within the partition): rim_lists[d, 0] lists the elements of partition d marked -2 across edge 3, rim_lists[d, 1] those marked -2 across edge 1, each once.
All inputs are finite; a program needn't handle non-finite values. No bound on the sum of `melt_flags` on one device may be relied on, other than what follows from the above.
Results may differ from a plain program's by a relative error of at most 0.00011.
Values sent between devices are 32-bit elements; how exact they have to be, the bound alone decides.
No kernel may reach another device: no remote copies, remote signals or barrier semaphores. Data moves between devices by JAX's collectives and lax.ppermute only.
A program may use at most 64 MiB of HBM per device.

v0:
```python
import jax
import jax.numpy as jnp
from jax import lax
from jax.sharding import PartitionSpec as P

ITERS = 2


inverse_step = 0.5
penalty_weight = 1.0
latent_heat = 2.0
axial_wave = 0.01


def padded(cells, sides, width):
    for axis, dim in sides:
        count = lax.axis_size(axis)
        head = lax.slice_in_dim(cells, 0, width, axis=dim)
        tail = lax.slice_in_dim(cells, cells.shape[dim] - width, cells.shape[dim], axis=dim)
        cells = jnp.concatenate(
            [
                lax.ppermute(tail, axis, [(i, (i + 1) % count) for i in range(count)]),
                cells,
                lax.ppermute(head, axis, [((i + 1) % count, i) for i in range(count)]),
            ],
            axis=dim,
        )
    return cells


def axial_tables(planes):
    point_ids = jnp.arange(planes)[:, None]
    plane_ids = jnp.arange(planes)[None, :]
    mode_number = jnp.where(plane_ids == 1, planes // 2, plane_ids // 2)
    phase_index = point_ids * mode_number % planes
    angles = 2.0 * jnp.pi / planes * phase_index.astype(jnp.float32)
    sine_plane = (plane_ids % 2 == 1) & (plane_ids != 1)
    axial_basis = jnp.where(sine_plane, jnp.sin(angles), jnp.cos(angles))
    wave_number = jnp.where(plane_ids >= 2, mode_number, 0).astype(jnp.float32) * axial_wave
    axial_slope = wave_number * jnp.where(sine_plane, jnp.cos(angles), -jnp.sin(angles))
    weights = jnp.where(plane_ids <= 1, 1.0 / planes, 2.0 / planes)
    modal_basis = jnp.transpose(weights * axial_basis)
    return (axial_basis, axial_slope, modal_basis)


def squared_waves(plane_ids, planes):
    mode_number = jnp.where(plane_ids == 1, planes // 2, plane_ids // 2)
    return (mode_number.astype(jnp.float32) * axial_wave) ** 2


def plane_sums(first_field, second_field):
    return jnp.sum(first_field * second_field, axis=(1, 2))


def squares(residual):
    return lax.psum(plane_sums(residual, residual), "dom")


def per_device(
    spectral_fields,
    deriv_ops,
    geom,
    stiffness,
    stiff_scale,
    traces,
    neighbors,
    rim_lists,
    melt_flags,
):
    highest = lax.Precision.HIGHEST
    planes_dev = spectral_fields.shape[1]
    elements = spectral_fields.shape[2]
    points = spectral_fields.shape[3]
    groups = lax.axis_size("plane")
    block_elems = elements // groups
    planes = planes_dev * groups
    plane_rank = lax.axis_index("plane")
    dom_rank = lax.axis_index("dom")
    axial_basis, axial_slope, modal_basis = axial_tables(planes)
    slope_one = geom[0][None, None] * jnp.einsum(
        "cpen,kn->cpek", spectral_fields, deriv_ops[0], precision=highest
    )
    slope_two = geom[1][None, None] * jnp.einsum(
        "cpen,kn->cpek", spectral_fields, deriv_ops[1], precision=highest
    )
    paired = spectral_fields.reshape(4, planes_dev // 2, 2, elements, points)
    pair_wave = (plane_rank * (planes_dev // 2) + jnp.arange(planes_dev // 2)).astype(
        jnp.float32
    ) * axial_wave
    pair_wave = pair_wave[None, :, None, None]
    slope_axial = jnp.stack([pair_wave * paired[:, :, 1], -pair_wave * paired[:, :, 0]], axis=2)
    slope_axial = slope_axial.reshape(4, planes_dev, elements, points)
    stacked = jnp.concatenate([spectral_fields[:3], slope_one, slope_two, slope_axial], axis=0)
    physical = jnp.einsum(
        "mp,fpaen->fmaen",
        axial_basis,
        lax.all_to_all(
            stacked.reshape(stacked.shape[0], planes_dev, groups, block_elems, points),
            "plane",
            split_axis=2,
            concat_axis=1,
            tiled=True,
        ),
        precision=highest,
    )
    physical = physical.reshape(15, planes, block_elems, points)
    velocity = physical[:3]
    grad_one = physical[3:7]
    grad_two = physical[7:11]
    grad_axial = physical[11:15]
    advection = -(
        velocity[0][None] * grad_one + velocity[1][None] * grad_two + velocity[2][None] * grad_axial
    )
    heat_terms = advection[3] / (1.0 + latent_heat * melt_flags.astype(jnp.float32))[:, :, None]
    all_terms = jnp.concatenate([advection[:3], heat_terms[None]], axis=0)
    modal_terms = jnp.einsum("pm,cmen->cpen", modal_basis, all_terms, precision=highest)
    returned = lax.all_to_all(
        modal_terms.reshape(4, planes, 1, block_elems, points),
        "plane",
        split_axis=1,
        concat_axis=2,
        tiled=True,
    )
    modal_local = returned.reshape(4, planes_dev, elements, points)
    rim_count = rim_lists.shape[2]
    element_ids = jnp.arange(elements)
    left_rim = rim_lists[0, 0]
    right_rim = rim_lists[0, 1]

    def rim_position(rim_ids):
        matches = rim_ids[:, None] == element_ids[None, :]
        return jnp.sum(jnp.where(matches, jnp.arange(rim_count)[:, None], 0), axis=0)

    local_ids = neighbors - dom_rank * elements
    indices = []
    presence = []
    for edge_number in range(4):
        column = neighbors[:, edge_number]
        table_index = local_ids[:, edge_number]
        if edge_number == 1:
            table_index = jnp.where(column == -2, elements + rim_position(right_rim), table_index)
        elif edge_number == 3:
            table_index = jnp.where(column == -2, elements + rim_position(left_rim), table_index)
        indices.append(jnp.clip(table_index, 0, elements + rim_count - 1))
        presence.append((column != -1).astype(jnp.float32))
    wave_squares = squared_waves(plane_rank * planes_dev + jnp.arange(planes_dev), planes)[
        :, None, None
    ]

    def helmholtz(vector):
        edge_values = jnp.einsum("jtn,pen->jtpe", traces, vector, precision=highest)
        rim_values = jnp.stack(
            [
                jnp.take(edge_values[3], left_rim, axis=2),
                jnp.take(edge_values[1], right_rim, axis=2),
            ],
            axis=0,
        )
        widened = padded(rim_values, (("dom", 0),), 1)
        before_dom = widened[0]
        after_dom = widened[3]
        facing = []
        for edge_number in range(4):
            source = edge_values[(edge_number + 2) % 4]
            if edge_number == 1:
                source = jnp.concatenate([source, after_dom], axis=2)
            elif edge_number == 3:
                source = jnp.concatenate([source, before_dom], axis=2)
            else:
                source = jnp.concatenate([source, jnp.zeros_like(after_dom)], axis=2)
            picked = jnp.take(source, indices[edge_number], axis=2)
            facing.append(picked * presence[edge_number][None, None, :])
        trace_jumps = edge_values - jnp.stack(facing, axis=0)
        coupling = jnp.einsum("jtn,jtpe->pen", traces, trace_jumps, precision=highest)
        stiff_part = jnp.dot(vector.reshape(-1, points), stiffness, precision=highest).reshape(
            vector.shape
        )
        return (
            (inverse_step + wave_squares) * vector
            + stiff_scale[None, :, None] * stiff_part
            + penalty_weight * coupling
        )

    right_hand = inverse_step * spectral_fields[3] + modal_local[3]
    solution = spectral_fields[3]
    residual = right_hand - helmholtz(solution)
    search = residual
    norm_now = squares(residual)
    for iteration in range(ITERS):
        applied = helmholtz(search)
        step_size = norm_now / lax.psum(plane_sums(search, applied), "dom")
        solution = solution + step_size[:, None, None] * search
        if iteration + 1 < ITERS:
            residual = residual - step_size[:, None, None] * applied
            norm_next = squares(residual)
            search = residual + (norm_next / norm_now)[:, None, None] * search
            norm_now = norm_next
    return (modal_local[:3], solution)


def solution(mesh):
    placed = (
        P(None, "plane", "dom", None),
        P(),
        P(None, "dom", None),
        P(),
        P("dom"),
        P(),
        P("dom", None),
        P("dom", None, None),
        P(None, ("dom", "plane")),
    )
    return jax.shard_map(
        per_device,
        mesh=mesh,
        in_specs=placed,
        out_specs=(P(None, "plane", "dom", None), P("plane", "dom", None)),
        check_vma=False,
    )
```

profile of v0, /device:TPU:1, one launch (start us, length us, event | category | flops | bytes accessed | tf_op | source)
XLA Modules:
  0.0 171.9 jit_solution(11625766064137339756)
XLA Ops:
  0.7 0.8 slice_bitcast_fusion.21
  1.5 1.0 slice.148
  2.6 1.6 convolution_multiply_fusion
  5.2 2.6 %copy.106 = f32[15,4,64,1,128]{4,1,0,3,2:T(4,128)} copy(f32[15,4,64,1,128]{4,2,1,0,3:T(8,128)S(1)} %maximum_bitcast_fusion) | data formatting | bytes 3932160 | tf_op jit(solution)/shard_map/reshape | solution.py:98
  7.8 17.3 %all-to-all-start = ((f32[15,4,64,1,128]{4,1,0,3,2:T(4,128)}), f32[15,4,64,1,128]{4,1,0,3,2:T(4,128)S(1)}, u32[]{:S(2)}, u32[]{:S(2)}) async-start(f32[15,4,64,1,128]{4,1,0,3,2:T(4,128)} %copy.106), calls=%async_computation | async-start | bytes 3932160 | tf_op jit(solution)/shard_map/all_to_all | solution.py:97
  26.5 1.0 collective-permute-start
  28.3 1.1 collective-permute-start.1
  29.7 0.7 gather_fusion.3
  30.5 41.3 %all-to-all-done = f32[15,4,64,1,128]{4,1,0,3,2:T(4,128)S(1)} async-done(((f32[15,4,64,1,128]{4,1,0,3,2:T(4,128)}), f32[15,4,64,1,128]{4,1,0,3,2:T(4,128)S(1)}, u32[]{:S(2)}, u32[]{:S(2)}) %all-to-all-start) | async-done | bytes 1966112 | tf_op jit(solution)/shard_map/all_to_all | solution.py:97
  72.3 4.3 %convolution_bitcast_fusion = f32[15,256,1,1,128]{1,4,0,3,2:T(8,128)S(1)} fusion(f32[15,256,128]{2,1,0:T(8,128)S(1)} %bitcast.320, s32[256]{0:T(256)S(1)} %fusion.79, pred[256]{0:T(512)(128)(4,1)S(1)} %compare_and_fusion.6), kind=kOutput, calls=%fused_computation.19 | convolution fusion | flops 1510932480 | bytes 3933440 | tf_op jit(solution)/shard_map/mp,fpaen->fmaen/dot_general | solution.py:94
  76.9 1.6 convolution_bitcast_fusion.1
  78.5 1.0 copy.109
  79.5 10.7 %all-to-all-start.1 = ((f32[4,256,1,1,128]{4,0,3,2,1:T(4,128)}), f32[4,256,1,1,128]{4,0,3,2,1:T(4,128)S(1)}, u32[]{:S(2)}, u32[]{:S(2)}) async-start(f32[4,256,1,1,128]{4,0,3,2,1:T(4,128)} %copy.109), calls=%async_computation.1 | async-start | bytes 1048576 | tf_op jit(solution)/shard_map/all_to_all | solution.py:117
  90.4 0.7 gather_fusion
  91.4 0.7 gather_fusion.5
  92.3 0.7 gather_fusion.2
  93.5 12.6 %all-to-all-done.1 = f32[4,256,1,1,128]{4,0,3,2,1:T(4,128)S(1)} async-done(((f32[4,256,1,1,128]{4,0,3,2,1:T(4,128)}), f32[4,256,1,1,128]{4,0,3,2,1:T(4,128)S(1)}, u32[]{:S(2)}, u32[]{:S(2)}) %all-to-all-start.1) | async-done | bytes 524320 | tf_op jit(solution)/shard_map/all_to_all | solution.py:117
  107.9 6.0 %collective-permute-start.3 = (f32[1,16,4,32]{3,1,2,0:T(8,128)S(1)}, f32[1,16,4,32]{3,1,2,0:T(8,128)S(1)}, u32[]{:S(2)}, u32[]{:S(2)}) collective-permute-start(f32[1,16,4,32]{3,1,2,0:T(8,128)S(1)} %select_bitcast_fusion.2), channel_id=1, source_target_pairs={{0,1},{1,2},{2,3},{3,4},{4,5},{5,6},{6,7},{7,0},{8,9},{9,10},{10,1... | collective-permute-start | bytes 24584 | tf_op jit(solution)/shard_map/ppermute | solution.py:22
  114.0 0.7 gather_fusion.9
  116.7 0.7 gather_fusion.11
  117.5 1.4 collective-permute-done.2
  119.1 0.7 gather_fusion.8
  120.6 12.2 %all-reduce.6 = (f32[4]{0:T(128)S(1)}, f32[4]{0:T(128)S(1)}) all-reduce(f32[4]{0:T(128)S(1)} %get-tuple-element.5, f32[4]{0:T(128)S(1)} %get-tuple-element.4), channel_id=1, replica_groups=mesh['plane'=64,'dom'=8] {'dom'}, use_global_device_ids=true, to_apply=%region_3.6 | all-reduce | flops 8 | bytes 64 | tf_op jit(solution)/shard_map/psum | solution.py:56
  133.1 15.0 %psum.30 = f32[4]{0:T(128)S(1)} all-reduce(f32[4]{0:T(128)S(1)} %multiply_reduce_fusion), channel_id=1, replica_groups=mesh['plane'=64,'dom'=8] {'dom'}, use_global_device_ids=true, to_apply=%region_7.10 | all-reduce | flops 4 | bytes 32 | tf_op jit(solution)/shard_map/psum | solution.py:56
  149.7 0.7 gather_fusion.15
  151.3 0.7 collective-permute-start.4
  153.1 0.7 gather_fusion.17
  153.8 0.8 collective-permute-done.4
  154.8 0.7 gather_fusion.14
  156.4 0.8 slice_bitcast_fusion.3
  157.2 13.9 %psum.31 = f32[4]{0:T(128)S(1)} all-reduce(f32[4]{0:T(128)S(1)} %fusion.8), channel_id=1, replica_groups=mesh['plane'=64,'dom'=8] {'dom'}, use_global_device_ids=true, to_apply=%region_9.12 | all-reduce | flops 4 | bytes 32 | tf_op jit(solution)/shard_map/psum | solution.py:191
  171.1 0.8 fusion.50
  (139 shorter events, 15.4 us)
Async XLA Ops:
  0.6 105.6 %copy-start = (f32[128,128]{1,0:T(8,128)S(1)}, f32[128,128]{1,0:T(8,128)}, u32[]{:S(2)}) copy-start(f32[128,128]{1,0:T(8,128)} %param.16) | copy-start | bytes 196612
  0.6 3.5 %copy-start.1 = (f32[4,4,64,128]{3,2,1,0:T(8,128)S(1)}, f32[4,4,64,128]{3,2,1,0:T(8,128)}, u32[]{:S(2)}) copy-start(f32[4,4,64,128]{3,2,1,0:T(8,128)} %param.13) | copy-start | bytes 1572868
  0.7 3.5 %copy-start.3 = (f32[2,128,128]{2,1,0:T(8,128)S(1)}, f32[2,128,128]{2,1,0:T(8,128)}, u32[]{:S(2)}) copy-start(f32[2,128,128]{2,1,0:T(8,128)} %param.14) | copy-start | bytes 393220
  7.8 17.3 %copy-start.2 = (f32[4,16,128]{2,1,0:T(8,128)S(1)}, f32[4,16,128]{2,1,0:T(8,128)}, u32[]{:S(2)}) copy-start(f32[4,16,128]{2,1,0:T(8,128)} %param.18) | copy-start | bytes 98308
  7.8 17.9 %copy-start.6 = (s32[1,2,32]{2,1,0:T(2,128)S(1)}, s32[1,2,32]{2,1,0:T(2,128)}, u32[]{:S(2)}) copy-start(s32[1,2,32]{2,1,0:T(2,128)} %param.20) | copy-start | bytes 772
  7.8 21.8 %copy-start.4 = (s32[64,4]{0,1:T(4,128)S(1)}, s32[64,4]{0,1:T(4,128)}, u32[]{:S(2)}) copy-start(s32[64,4]{0,1:T(4,128)} %param.19) | copy-start | bytes 3076
  7.8 64.0 %all-to-all-start = ((f32[15,4,64,1,128]{4,1,0,3,2:T(4,128)}), f32[15,4,64,1,128]{4,1,0,3,2:T(4,128)S(1)}, u32[]{:S(2)}, u32[]{:S(2)}) async-start(f32[15,4,64,1,128]{4,1,0,3,2:T(4,128)} %copy.106), calls=%async_computation | async-start | bytes 3932160 | tf_op jit(solution)/shard_map/all_to_all | solution.py:97
  25.1 5.4 %copy-start.7 = (s32[256,1]{0,1:T(1,128)S(1)}, s32[256,1]{0,1:T(1,128)}, u32[]{:S(2)}) copy-start(s32[256,1]{0,1:T(1,128)} %param.21) | copy-start | bytes 3076
  26.5 64.7 %collective-permute-start = (f32[1,16,4,32]{3,1,2,0:T(8,128)S(1)}, f32[1,16,4,32]{3,1,2,0:T(8,128)S(1)}, u32[]{:S(2)}, u32[]{:S(2)}) collective-permute-start(f32[1,16,4,32]{3,1,2,0:T(8,128)S(1)} %select_bitcast_fusion.5), channel_id=1, source_target_pairs={{1,0},{2,1},{3,2},{4,3},{5,4},{6,5},{7,6},{0,7},{9,8},{10,9},{11,1... | collective-permute-start | bytes 24584 | tf_op jit(solution)/shard_map/ppermute | solution.py:24
  28.3 63.0 %collective-permute-start.1 = (f32[1,16,4,32]{3,1,2,0:T(8,128)S(1)}, f32[1,16,4,32]{3,1,2,0:T(8,128)S(1)}, u32[]{:S(2)}, u32[]{:S(2)}) collective-permute-start(f32[1,16,4,32]{3,1,2,0:T(8,128)S(1)} %select_bitcast_fusion.4), channel_id=1, source_target_pairs={{0,1},{1,2},{2,3},{3,4},{4,5},{5,6},{6,7},{7,0},{8,9},{9,10},{10,1... | collective-permute-start | bytes 24584 | tf_op jit(solution)/shard_map/ppermute | solution.py:22
  79.5 26.5 %all-to-all-start.1 = ((f32[4,256,1,1,128]{4,0,3,2,1:T(4,128)}), f32[4,256,1,1,128]{4,0,3,2,1:T(4,128)S(1)}, u32[]{:S(2)}, u32[]{:S(2)}) async-start(f32[4,256,1,1,128]{4,0,3,2,1:T(4,128)} %copy.109), calls=%async_computation.1 | async-start | bytes 1048576 | tf_op jit(solution)/shard_map/all_to_all | solution.py:117
  90.2 16.0 %copy-start.5 = (f32[64]{0:T(128)S(1)}, f32[64]{0:T(128)}, u32[]{:S(2)}) copy-start(f32[64]{0:T(128)} %param.17) | copy-start | bytes 772
  107.9 8.6 %collective-permute-start.3 = (f32[1,16,4,32]{3,1,2,0:T(8,128)S(1)}, f32[1,16,4,32]{3,1,2,0:T(8,128)S(1)}, u32[]{:S(2)}, u32[]{:S(2)}) collective-permute-start(f32[1,16,4,32]{3,1,2,0:T(8,128)S(1)} %select_bitcast_fusion.2), channel_id=1, source_target_pairs={{0,1},{1,2},{2,3},{3,4},{4,5},{5,6},{6,7},{7,0},{8,9},{9,10},{10,1... | collective-permute-start | bytes 24584 | tf_op jit(solution)/shard_map/ppermute | solution.py:22
  115.6 3.4 %collective-permute-start.2 = (f32[1,16,4,32]{3,1,2,0:T(8,128)S(1)}, f32[1,16,4,32]{3,1,2,0:T(8,128)S(1)}, u32[]{:S(2)}, u32[]{:S(2)}) collective-permute-start(f32[1,16,4,32]{3,1,2,0:T(8,128)S(1)} %select_bitcast_fusion.3), channel_id=1, source_target_pairs={{1,0},{2,1},{3,2},{4,3},{5,4},{6,5},{7,6},{0,7},{9,8},{10,9},{11,1... | collective-permute-start | bytes 24584 | tf_op jit(solution)/shard_map/ppermute | solution.py:24
  149.5 3.3 %collective-permute-start.5 = (f32[1,16,4,32]{3,1,2,0:T(8,128)S(1)}, f32[1,16,4,32]{3,1,2,0:T(8,128)S(1)}, u32[]{:S(2)}, u32[]{:S(2)}) collective-permute-start(f32[1,16,4,32]{3,1,2,0:T(8,128)S(1)} %select_bitcast_fusion), channel_id=1, source_target_pairs={{0,1},{1,2},{2,3},{3,4},{4,5},{5,6},{6,7},{7,0},{8,9},{9,10},{10,1... | collective-permute-start | bytes 24584 | tf_op jit(solution)/shard_map/ppermute | solution.py:22
  151.3 3.4 %collective-permute-start.4 = (f32[1,16,4,32]{3,1,2,0:T(8,128)S(1)}, f32[1,16,4,32]{3,1,2,0:T(8,128)S(1)}, u32[]{:S(2)}, u32[]{:S(2)}) collective-permute-start(f32[1,16,4,32]{3,1,2,0:T(8,128)S(1)} %select_bitcast_fusion.1), channel_id=1, source_target_pairs={{1,0},{2,1},{3,2},{4,3},{5,4},{6,5},{7,6},{0,7},{9,8},{10,9},{11,1... | collective-permute-start | bytes 24584 | tf_op jit(solution)/shard_map/ppermute | solution.py:24
where the time goes:
time: 174 us; the launch traced here: 172 us
  waiting for transfers between devices  56.1 us (32%)
  blocking collectives  41.2 us (24%)
  starting transfers between devices  36.7 us (21%)
  local copies, waits for them, and re-layouts  22.3 us (13%)
  matrix products  12 us (7%)
  other arithmetic  2.28 us (1%)
    all_to_all x1, waiting for transfers between devices, per_device(): lax.all_to_all(stacked.reshape(stacked.shape[0], planes_dev, groups, bloc...  41.3 us
    psum x2, blocking collectives, squares(): return lax.psum(plane_sums(residual, residual), 'dom')  27.2 us
    all_to_all x1, starting transfers between devices, per_device(): lax.all_to_all(stacked.reshape(stacked.shape[0], planes_dev, groups, bloc...  17.3 us
    psum x1, blocking collectives, per_device(): step_size = norm_now / lax.psum(plane_sums(search, applied), 'dom')  13.9 us
    all_to_all x1, waiting for transfers between devices, per_device(): lax.all_to_all(modal_terms.reshape(4, planes, 1, block_elems, points), 'p...  12.6 us
    all_to_all x1, starting transfers between devices, per_device(): lax.all_to_all(modal_terms.reshape(4, planes, 1, block_elems, points), 'p...  10.7 us
    gather x24, local copies, waits for them, and re-layouts, helmholtz(): picked = jnp.take(source, indices[edge_number], axis=2)  8.83 us
    ppermute x3, starting transfers between devices, padded(): lax.ppermute(tail, axis, [(i, (i + 1) % count) for i in range(count)])  7.1 us
  transfers between devices with their start and end apart: 8, of which 4 were waited for; matrix products, arithmetic and copies ran while one was open for 12% of the time, Pallas kernels for 0%

commit v1 on v0

v1 whole, which is shorter than its diff:
```python
import functools

import jax
import jax.numpy as jnp
import numpy as np
from jax import lax
from jax.experimental import pallas as pl
from jax.experimental.pallas import tpu as pltpu
from jax.sharding import PartitionSpec as P

PLANES = 256
POINTS = 128
ELEMS = 64
OWN = 4
EDGES = 4
TRACE = 16
RIM = 32
ROWS = OWN * ELEMS
AXIAL_WAVE = 0.01
INVERSE_STEP = 0.5
LATENT = 2.0
F32 = jnp.float32
BF16 = jnp.bfloat16


def halves_np(table):
    high = table.astype(np.float32).astype(jnp.bfloat16)
    low = (table - high.astype(np.float64)).astype(np.float32).astype(jnp.bfloat16)
    return high, low


@functools.cache
def axial_tables():
    points = np.arange(PLANES)[:, None]
    planes = np.arange(PLANES)[None, :]
    mode = np.where(planes == 1, PLANES // 2, planes // 2)
    angles = 2.0 * np.pi / PLANES * ((points * mode) % PLANES)
    sine = (planes % 2 == 1) & (planes != 1)
    basis = np.where(sine, np.sin(angles), np.cos(angles))
    wave = np.where(planes >= 2, mode, 0) * AXIAL_WAVE
    slope = wave * np.where(sine, np.cos(angles), -np.sin(angles))
    weights = np.where(planes <= 1, 1.0 / PLANES, 2.0 / PLANES)
    modal = -np.transpose(weights * basis)
    return halves_np(np.concatenate([basis, slope], axis=0)) + halves_np(modal)


def halves(value):
    high = value.astype(BF16)
    return high, (value - high.astype(F32)).astype(BF16)


def product(left, right):
    return jnp.dot(left, right, preferred_element_type=F32)


def product3(left, right):
    return product(left[0], right[0]) + (product(left[1], right[0]) + product(left[0], right[1]))


def lanes(rows):
    return lax.broadcasted_iota(jnp.int32, (rows, POINTS), 1)


def edge_of(lane):
    return (lane % (EDGES * TRACE)) // TRACE


def call(kernel, outs, *args, flops=0):
    return pl.pallas_call(
        kernel,
        out_shape=[jax.ShapeDtypeStruct(shape, kind) for shape, kind in outs],
        in_specs=[pl.BlockSpec(memory_space=pltpu.VMEM)] * len(args),
        out_specs=[pl.BlockSpec(memory_space=pltpu.VMEM)] * len(outs),
        compiler_params=pltpu.CompilerParams(vmem_limit_bytes=24 * 1024 * 1024),
        cost_estimate=pl.CostEstimate(
            flops=flops or 10**6,
            bytes_accessed=sum(a.size * a.dtype.itemsize for a in args),
            transcendentals=0,
        ),
    )(*args)


def pack_kernel(fields, out):
    for plane in range(OWN):
        for field in range(4):
            out[pl.ds(plane * 4 + field, ELEMS, stride=16), :] = fields[field, plane]


def physical_kernel(fields, factors, flags, deriv, both_h, both_l, modal_h, modal_l, out):
    spectral = jnp.concatenate([fields[pl.ds(c, PLANES, stride=4), :] for c in range(4)], axis=1)
    points = product3((both_h[...], both_l[...]), halves(spectral))
    values = [points[:PLANES, c * POINTS : (c + 1) * POINTS] for c in range(4)]
    first = values[0] * factors[0:1, :]
    second = values[1] * factors[1:2, :]
    third = values[2]
    deriv_halves = halves(deriv[...])
    melting = 1.0 / (1.0 + LATENT * flags[...].astype(F32))
    terms = []
    for c in range(4):
        slopes = product3(halves(values[c]), deriv_halves)
        term = (
            first * slopes[:, :POINTS]
            + second * slopes[:, POINTS:]
            + third * points[PLANES:, c * POINTS : (c + 1) * POINTS]
        )
        terms.append(term * melting if c == 3 else term)
    modal = product3((modal_h[...], modal_l[...]), halves(jnp.concatenate(terms, axis=1)))
    for c in range(4):
        out[pl.ds(c, PLANES, stride=4), :] = modal[:, c * POINTS : (c + 1) * POINTS]


def prepare_kernel(
    weights, edge_back, near, rim_column, rim_row, columns,
    weights_h, weights_l, back_h, back_l, gather, to_rim, from_rim, rim_mask, scale_one, scale_two,
):
    weights_h[...], weights_l[...] = halves(weights[...])
    back_h[...], back_l[...] = halves(edge_back[...])
    wide = lax.broadcasted_iota(jnp.int32, (ROWS, ROWS), 1)
    tall = lax.broadcasted_iota(jnp.int32, (ROWS, ROWS), 0)
    for edge in range(EDGES):
        hit = wide == near[:, edge : edge + 1]
        gather[:, edge * ROWS : (edge + 1) * ROWS] = jnp.where(hit, 1.0, 0.0).astype(BF16)
    to_rim[...] = jnp.where(wide == rim_column[...], 1.0, 0.0).astype(BF16)
    from_rim[...] = jnp.where(tall == rim_row[...], 1.0, 0.0).astype(BF16)
    lane = lanes(ROWS)
    edge = edge_of(lane)
    forward = (edge == 1) & (near[:, 1:2] == -2)
    backward = (edge == 3) & (near[:, 3:4] == -2)
    upper = lane >= EDGES * TRACE
    rim_mask[...] = jnp.where((forward | backward) & upper, 1.0, 0.0)
    scale_one[...] = jnp.broadcast_to(columns[:, 0:1], (ROWS, POINTS))
    scale_two[...] = jnp.broadcast_to(columns[:, 1:2], (ROWS, POINTS))


def two_halves(doubled):
    high = doubled.astype(BF16).astype(F32)
    return jnp.where(lanes(doubled.shape[0]) < EDGES * TRACE, high, doubled - high)


def facing_local(split_traces, gather):
    edge = edge_of(lanes(ROWS))
    stack = [jnp.where(edge == j, split_traces, 0.0).astype(BF16) for j in range(EDGES)]
    return product(gather[...], jnp.concatenate(stack, axis=0))


def start_helmholtz(vector, weights_h, weights_l, back_h, back_l, gather, to_rim, scale_one, scale_two):
    weights = (weights_h[...], weights_l[...])
    images = product3(halves(vector), weights)
    stiff, own, doubled, crossing = (images[:, k * POINTS : (k + 1) * POINTS] for k in range(4))
    traces_split = two_halves(doubled)
    facing = facing_local(traces_split, gather).astype(BF16)
    coupling = product(facing, back_h[...]) + product(facing, back_l[...])
    part = scale_one[...] * vector + scale_two[...] * stiff + own - coupling
    trace_weights = tuple(w[:, 2 * POINTS : 3 * POINTS] for w in weights)
    part_split = two_halves(product3(halves(part), trace_weights))
    rims = product(to_rim[...], jnp.concatenate([traces_split, part_split], axis=1).astype(BF16))
    first, second = rims[:, :POINTS], rims[:, POINTS:]
    first = first + pltpu.roll(first, EDGES * TRACE, 1)
    second = second + pltpu.roll(second, EDGES * TRACE, 1)
    return part, jnp.where(lanes(ROWS) < EDGES * TRACE, first, second), crossing


def first_kernel(
    fields, weights_h, weights_l, back_h, back_l, gather, to_rim, scale_one, scale_two,
    part_out, left_out, right_out,
):
    vector = fields[3].reshape(ROWS, POINTS)
    part, rims, _ = start_helmholtz(
        vector, weights_h, weights_l, back_h, back_l, gather, to_rim, scale_one, scale_two
    )
    part_out[...] = part
    left_out[...] = rims[: OWN * RIM]
    right_out[...] = rims[OWN * RIM :]


def arrived(left, right, from_rim):
    half = OWN * RIM
    edge = edge_of(lanes(half))
    both = jnp.concatenate(
        [jnp.where(edge == 3, left[...], 0.0), jnp.where(edge == 1, right[...], 0.0)], axis=0
    )
    high, low = halves(both)
    spread = product(from_rim[...], jnp.concatenate([high, low], axis=1))
    return spread[:, :POINTS], spread[:, POINTS:]


def rim_coupling(high, low, back_h, back_l):
    lower = lanes(ROWS) < EDGES * TRACE
    high = jnp.where(lower, high, 0.0).astype(BF16)
    low = jnp.where(lower, low, 0.0).astype(BF16)
    return product(high, back_h[...]) + (product(low, back_h[...]) + product(high, back_l[...]))


def base_kernel(fields, part, left, right, from_rim, back_h, back_l, out):
    high, low = arrived(left, right, from_rim)
    image = part[...] - rim_coupling(high, low, back_h, back_l)
    out[...] = INVERSE_STEP * fields[3].reshape(ROWS, POINTS) - image


def residual_kernel(
    modal, base, weights_h, weights_l, back_h, back_l, gather, to_rim, scale_one, scale_two,
    residual_out, part_out, left_out, right_out, crossing_out,
):
    heat = [modal[pl.ds(plane * 4 + 3, ELEMS, stride=16), :] for plane in range(OWN)]
    residual = base[...] + jnp.concatenate(heat, axis=0)
    part, rims, crossing = start_helmholtz(
        residual, weights_h, weights_l, back_h, back_l, gather, to_rim, scale_one, scale_two
    )
    residual_out[...] = residual
    part_out[...] = part
    left_out[...] = rims[: OWN * RIM]
    right_out[...] = rims[OWN * RIM :]
    crossing_out[...] = crossing


def momentum_kernel(modal, out):
    for field in range(3):
        for plane in range(OWN):
            out[field, plane] = modal[pl.ds(plane * 4 + field, ELEMS, stride=16), :]


def moments_kernel(
    residual_ref, part, left, right, crossing, from_rim, weights_h, weights_l, back_h, back_l, gather,
    rim_mask, scale_one, scale_two, image_out, sums_out,
):
    high, low = arrived(left, right, from_rim)
    image = part[...] - rim_coupling(high, low, back_h, back_l)
    image_out[...] = image
    residual = residual_ref[...]
    weights = (
        jnp.concatenate([weights_h[:, :POINTS], weights_h[:, 2 * POINTS : 3 * POINTS]], axis=1),
        jnp.concatenate([weights_l[:, :POINTS], weights_l[:, 2 * POINTS : 3 * POINTS]], axis=1),
    )
    images = product3(halves(image), weights)
    stiff, doubled = images[:, :POINTS], images[:, POINTS:]
    facing = facing_local(two_halves(doubled), gather)
    facing = facing + pltpu.roll(facing, EDGES * TRACE, 1)
    facing = facing + (high + low) - crossing[...] * rim_mask[...]
    own = pltpu.roll(doubled, 2 * TRACE, 1)
    jumps = jnp.where(lanes(ROWS) >= EDGES * TRACE, own * (own - facing), 0.0)
    square = image * image
    cubic = scale_one[...] * square + scale_two[...] * (image * stiff) + jumps
    for number, value in enumerate((residual * residual, residual * image, square, cubic)):
        for plane in range(OWN):
            total = jnp.sum(value[plane * ELEMS : (plane + 1) * ELEMS], axis=0, keepdims=True)
            for peer in range(8):
                row = peer * 16 + number * OWN + plane
                sums_out[row : row + 1, :] = total


def final_kernel(sums, fields, residual, image, out):
    total = sums[0:16, :]
    for peer in range(1, 8):
        total = total + sums[peer * 16 : (peer + 1) * 16, :]
    total = jnp.sum(total, axis=1, keepdims=True)
    m0, m1, m2, m3 = (total[k * OWN : (k + 1) * OWN] for k in range(4))
    step = m0 / m1
    after = m0 + step * (step * m2 - 2.0 * m1)
    after_image = m1 + step * (step * m3 - 2.0 * m2)
    ratio = after / m0
    second = after / (after_image - ratio * after / step)
    on_residual = step + second * (1.0 + ratio)
    on_image = -second * step
    for plane in range(OWN):
        rows = pl.ds(plane * ELEMS, ELEMS)
        out[plane] = (
            fields[3, plane]
            + on_residual[plane : plane + 1] * residual[rows, :]
            + on_image[plane : plane + 1] * image[rows, :]
        )


def per_device(
    spectral_fields,
    deriv_ops,
    geom,
    stiffness,
    stiff_scale,
    traces,
    neighbors,
    rim_lists,
    melt_flags,
):
    highest = lax.Precision.HIGHEST
    plane_rank = lax.axis_index("plane")
    dom_rank = lax.axis_index("dom")
    count = lax.axis_size("dom")
    groups = lax.axis_size("plane")
    whole = ((ROWS, POINTS), F32)
    rims = ((OWN * RIM, POINTS), F32)

    with jax.named_scope("to_points"):
        (packed,) = call(pack_kernel, [((ELEMS * 16, POINTS), F32)], spectral_fields)
        gathered = lax.all_to_all(
            packed.reshape(groups, 16, POINTS), "plane", split_axis=0, concat_axis=0, tiled=True
        ).reshape(groups * 16, POINTS)

    with jax.named_scope("operator_tables"):
        edges = traces.reshape(EDGES * TRACE, POINTS)
        turned = jnp.concatenate([edges[2 * TRACE :], edges[: 2 * TRACE]], axis=0)
        own = jnp.dot(edges.T, edges, precision=highest)
        square_one = jnp.dot(traces[1], traces[1].T, precision=highest)
        square_three = jnp.dot(traces[3], traces[3].T, precision=highest)
        empty = jnp.zeros((POINTS, TRACE), F32)
        crossing = jnp.concatenate(
            [
                empty,
                jnp.dot(traces[1].T, square_three, precision=highest),
                empty,
                jnp.dot(traces[3].T, square_one, precision=highest),
            ],
            axis=1,
        )
        weights = jnp.concatenate(
            [stiffness, own, turned.T, turned.T, jnp.zeros((POINTS, EDGES * TRACE), F32), crossing],
            axis=1,
        )
        edge_back = jnp.concatenate([edges, edges], axis=0)
        shift = (jnp.arange(OWN, dtype=jnp.int32) * ELEMS)[:, None]
        local = jnp.where(neighbors >= 0, neighbors - dom_rank * ELEMS, neighbors)
        near = jnp.where(local[None] >= 0, local[None] + shift[:, :, None], local[None]).reshape(ROWS, EDGES)
        rim = (rim_lists[0][:, None, :] + shift[None]).reshape(2 * OWN * RIM)
        wave = (plane_rank * OWN + jnp.arange(OWN)).astype(jnp.int32)
        wave = jnp.where(wave == 1, PLANES // 2, wave // 2).astype(F32) * AXIAL_WAVE
        columns = jnp.stack(
            [jnp.repeat(INVERSE_STEP + wave**2, ELEMS), jnp.tile(stiff_scale, OWN)], axis=1
        )
        (
            weights_h, weights_l, back_h, back_l, gather, to_rim, from_rim, rim_mask, scale_one, scale_two,
        ) = call(
            prepare_kernel,
            [
                ((POINTS, 4 * POINTS), BF16),
                ((POINTS, 4 * POINTS), BF16),
                ((POINTS, POINTS), BF16),
                ((POINTS, POINTS), BF16),
                ((ROWS, EDGES * ROWS), BF16),
                ((ROWS, ROWS), BF16),
                ((ROWS, ROWS), BF16),
                whole,
                whole,
                whole,
            ],
            weights,
            edge_back,
            near,
            rim[:, None],
            rim[None, :],
            columns,
        )
        tables = (weights_h, weights_l, back_h, back_l, gather, to_rim, scale_one, scale_two)

    def exchange(left, right):
        from_left = lax.ppermute(right, "dom", [(i, (i + 1) % count) for i in range(count)])
        from_right = lax.ppermute(left, "dom", [((i + 1) % count, i) for i in range(count)])
        return from_left, from_right

    with jax.named_scope("base"):
        part, left, right = call(first_kernel, [whole, rims, rims], spectral_fields, *tables)
        left, right = exchange(left, right)
        (base,) = call(
            base_kernel, [whole], spectral_fields, part, left, right, from_rim, back_h, back_l
        )

    with jax.named_scope("advection"):
        factors = lax.dynamic_slice_in_dim(geom, plane_rank, 1, axis=1)[:, 0]
        deriv = jnp.concatenate([deriv_ops[0].T, deriv_ops[1].T], axis=1)
        (modal,) = call(
            physical_kernel,
            [((groups * 16, POINTS), F32)],
            gathered,
            factors,
            melt_flags,
            deriv,
            *(jnp.asarray(t) for t in axial_tables()),
            flops=10**9,
        )
        returned = lax.all_to_all(
            modal.reshape(groups, 16, POINTS), "plane", split_axis=0, concat_axis=0, tiled=True
        ).reshape(ELEMS * 16, POINTS)

    with jax.named_scope("solve"):
        residual, part, left, right, crossing_part = call(
            residual_kernel, [whole, whole, rims, rims, whole], returned, base, *tables
        )
        left, right = exchange(left, right)
        (momentum,) = call(momentum_kernel, [((3, OWN, ELEMS, POINTS), F32)], returned)
        image, sums = call(
            moments_kernel,
            [whole, ((8 * 16, POINTS), F32)],
            residual,
            part,
            left,
            right,
            crossing_part,
            from_rim,
            weights_h,
            weights_l,
            back_h,
            back_l,
            gather,
            rim_mask,
            scale_one,
            scale_two,
        )
        sums = lax.all_to_all(
            sums.reshape(8, 16, POINTS), "dom", split_axis=0, concat_axis=0, tiled=True
        ).reshape(8 * 16, POINTS)
        (temperature,) = call(
            final_kernel, [((OWN, ELEMS, POINTS), F32)], sums, spectral_fields, residual, image
        )
    return momentum, temperature


def solution(mesh):
    placed = (
        P(None, "plane", "dom", None),
        P(),
        P(None, "dom", None),
        P(),
        P("dom"),
        P(),
        P("dom", None),
        P("dom", None, None),
        P(None, ("dom", "plane")),
    )
    return jax.shard_map(
        per_device,
        mesh=mesh,
        in_specs=placed,
        out_specs=(P(None, "plane", "dom", None), P("plane", "dom", None)),
        check_vma=False,
    )
```

time: 174 us -> 85 us (0.49)
  blocking collectives: 41.2 us -> 0 us
  waiting for transfers between devices: 56.1 us -> 27.4 us
  local copies, waits for them, and re-layouts: 22.3 us -> 7.98 us
  matrix products: 12 us -> 1.13 us
  Pallas kernels: 0 us -> 9.98 us
  other arithmetic: 2.28 us -> 0.3 us
    psum x3 -> x0, blocking collectives: 41.2 us -> none  [the longest x2 27.2 us: squares(): return lax.psum(plane_sums(residual, residual), 'dom')]
    all_to_all x2 -> x3, waiting for transfers between devices: 53.8 us -> 19.7 us  [the longest x1 11.1 us: per_device(): lax.all_to_all(packed.reshape(groups, 16, POINTS), 'plane', split_axis=0,...]
    gather x36 -> x0, local copies, waits for them, and re-layouts: 12.9 us -> none  [the longest x24 8.83 us: helmholtz(): picked = jnp.take(source, indices[edge_number], axis=2)]
    dot_general x13 -> x5, matrix products: 12 us -> 1.13 us  [the longest x1 0.31 us: per_device(): jnp.dot(traces[3].T, square_one, precision=highest)]
    pallas_call x0 -> x9, Pallas kernels: none -> 9.98 us  [call(): pl.pallas_call(kernel, out_shape=[jax.ShapeDtypeStruct(shape, kind) for s...]
    unnamed x22 -> x31, local copies, waits for them, and re-layouts: 0.68 us -> 6.63 us
    ppermute x6 -> x4, waiting for transfers between devices: 2.26 us -> 7.67 us  [the longest x2 5.01 us: exchange(): lax.ppermute(left, 'dom', [((i + 1) % count, i) for i in range(count)])]
    reshape x2 -> x1, local copies, waits for them, and re-layouts: 3.58 us -> 0.08 us  [per_device(): jnp.stack([jnp.repeat(INVERSE_STEP + wave ** 2, ELEMS), jnp.tile(stiff_sc...]
  transfers between devices with their start and end apart: 8 -> 7, of which waited for: 4 -> 7; matrix products, arithmetic and copies ran while one was open for 12% -> 4% of each run, Pallas kernels for 0% -> 3%
where the time goes in v1:
time: 85 us; the launch traced here: 84.4 us
  starting transfers between devices  36.7 us (43%)
  waiting for transfers between devices  27.4 us (32%)
  Pallas kernels  9.98 us (12%)
  local copies, waits for them, and re-layouts  7.98 us (9%)
  matrix products  1.13 us (1%)
  between operations  0.93 us (1%)
    all_to_all x1, starting transfers between devices, per_device(): lax.all_to_all(packed.reshape(groups, 16, POINTS), 'plane', split_axis=0,...  17.1 us
    all_to_all x1, waiting for transfers between devices, per_device(): lax.all_to_all(packed.reshape(groups, 16, POINTS), 'plane', split_axis=0,...  11.1 us
    pallas_call x9, Pallas kernels, call(): pl.pallas_call(kernel, out_shape=[jax.ShapeDtypeStruct(shape, kind) for s...  9.98 us
    ppermute x2, starting transfers between devices, exchange(): lax.ppermute(right, 'dom', [(i, (i + 1) % count) for i in range(count)])  8.49 us
    all_to_all x1, starting transfers between devices, per_device(): lax.all_to_all(modal.reshape(groups, 16, POINTS), 'plane', split_axis=0,...  6.75 us
    unnamed x31, local copies, waits for them, and re-layouts  6.63 us
    ppermute x2, waiting for transfers between devices, exchange(): lax.ppermute(left, 'dom', [((i + 1) % count, i) for i in range(count)])  5.01 us
    all_to_all x1, waiting for transfers between devices, per_device(): lax.all_to_all(modal.reshape(groups, 16, POINTS), 'plane', split_axis=0,...  4.6 us
  transfers between devices with their start and end apart: 7, of which 7 were waited for; matrix products, arithmetic and copies ran while one was open for 4% of the time, Pallas kernels for 3%

profile of v1, /device:TPU:1, one launch (start us, length us, event | category | flops | bytes accessed | tf_op | source)
XLA Modules:
  0.0 84.4 jit_solution(3298617642431624151)
XLA Ops:
  0.7 1.1 %copy-done.1 = f32[4,4,64,128]{3,2,1,0:T(8,128)S(1)} copy-done((f32[4,4,64,128]{3,2,1,0:T(8,128)S(1)}, f32[4,4,64,128]{3,2,1,0:T(8,128)}, u32[]{:S(2)}) %copy-start.1) | copy-done | bytes 524312
  1.7 1.1 %to_points.1 = f32[1024,128]{1,0:T(8,128)} custom-call(f32[4,4,64,128]{3,2,1,0:T(8,128)S(1)} %copy-done.1), custom_call_target="tpu_custom_call" | custom-call | flops 1000000 | bytes 524288 | tf_op jit(solution)/shard_map/to_points/pallas_call | solution.py:69
  2.8 17.1 %all-to-all-start = ((f32[64,16,128]{2,1,0:T(8,128)}), f32[64,16,128]{2,1,0:T(8,128)S(1)}, u32[]{:S(2)}, u32[]{:S(2)}) async-start(f32[64,16,128]{2,1,0:T(8,128)} %bitcast), calls=%async_computation | async-start | bytes 1048576 | tf_op jit(solution)/shard_map/to_points/all_to_all | solution.py:294
  20.0 0.7 copy-done.10
  20.7 0.7 copy-done.12
  22.2 0.6 copy-done.13
  23.0 0.6 copy-done.7
  23.8 0.7 copy-done.8
  24.7 0.6 copy-done.11
  26.0 11.1 %all-to-all-done = f32[64,16,128]{2,1,0:T(8,128)S(1)} async-done(((f32[64,16,128]{2,1,0:T(8,128)}), f32[64,16,128]{2,1,0:T(8,128)S(1)}, u32[]{:S(2)}, u32[]{:S(2)}) %all-to-all-start) | async-done | bytes 524320 | tf_op jit(solution)/shard_map/to_points/all_to_all | solution.py:294
  37.1 2.2 %advection.1 = f32[1024,128]{1,0:T(8,128)} custom-call(f32[1024,128]{1,0:T(8,128)S(1)} %bitcast.48, f32[2,128]{1,0:T(2,128)S(1)} %bitcast.50, s32[256,1]{1,0:T(8,128)S(1)} %copy.40.flags, f32[128,256]{1,0:T(8,128)S(1)} %pad_maximum_fusion.deriv, bf16[512,256]{1,0:T(8,128)(2,1)S(1)} %copy-done.3, bf16[512,256]{1,0:T(8,128)(2,1)S(1)} %copy-done.4, ...), custom_call_target="tpu_custom_call" | custom-call | flops 1000000000 | bytes 1443840 | tf_op jit(solution)/shard_map/advection/pallas_call | solution.py:69
  39.3 6.8 %all-to-all-start.1 = ((f32[64,16,128]{2,1,0:T(8,128)}), f32[64,16,128]{2,1,0:T(8,128)S(1)}, u32[]{:S(2)}, u32[]{:S(2)}) async-start(f32[64,16,128]{2,1,0:T(8,128)} %bitcast.7), calls=%async_computation.1 | async-start | bytes 1048576 | tf_op jit(solution)/shard_map/advection/all_to_all | solution.py:378
  46.3 0.3 convolution_bitcast_fusion
  46.6 0.3 convolution_bitcast_fusion.1
  47.0 0.8 copy-done.9
  48.0 0.4 operator_tables.1
  48.4 0.6 copy-done.2
  49.0 1.2 %base.2 = (f32[256,128]{1,0:T(8,128)S(1)}, f32[128,128]{1,0:T(8,128)S(1)}, f32[128,128]{1,0:T(8,128)S(1)}) custom-call(f32[4,4,64,128]{3,2,1,0:T(8,128)S(1)} %copy-done.2, bf16[128,512]{1,0:T(8,128)(2,1)S(1)} %get-tuple-element.22.weights_h, bf16[128,512]{1,0:T(8,128)(2,1)S(1)} %get-tuple-element.23.weights_l, ...), custom_call_target="tpu_custom_call" | custom-call | flops 1000000 | bytes 1769472 | tf_op jit(solution)/shard_map/base/pallas_call | solution.py:69
  50.2 2.8 %collective-permute-start = (f32[128,128]{1,0:T(8,128)S(1)}, f32[128,128]{1,0:T(8,128)S(1)}, u32[]{:S(2)}, u32[]{:S(2)}) collective-permute-start(f32[128,128]{1,0:T(8,128)S(1)} %get-tuple-element.31), channel_id=1, source_target_pairs={{0,1},{1,2},{2,3},{3,4},{4,5},{5,6},{6,7},{7,0},{8,9},{9,10},{10,1... | collective-permute-start | bytes 196616 | tf_op jit(solution)/shard_map/base/ppermute | solution.py:354
  53.1 1.3 %collective-permute-done.left = f32[128,128]{1,0:T(8,128)S(1)} collective-permute-done((f32[128,128]{1,0:T(8,128)S(1)}, f32[128,128]{1,0:T(8,128)S(1)}, u32[]{:S(2)}, u32[]{:S(2)}) %collective-permute-start) | collective-permute-done | bytes 65568 | tf_op jit(solution)/shard_map/base/ppermute | solution.py:354
  54.4 2.7 %collective-permute-done.1.right = f32[128,128]{1,0:T(8,128)S(1)} collective-permute-done((f32[128,128]{1,0:T(8,128)S(1)}, f32[128,128]{1,0:T(8,128)S(1)}, u32[]{:S(2)}, u32[]{:S(2)}) %collective-permute-start.1) | collective-permute-done | bytes 65568 | tf_op jit(solution)/shard_map/base/ppermute | solution.py:355
  57.1 0.4 base.3
  57.5 4.6 %all-to-all-done.1 = f32[64,16,128]{2,1,0:T(8,128)S(1)} async-done(((f32[64,16,128]{2,1,0:T(8,128)}), f32[64,16,128]{2,1,0:T(8,128)S(1)}, u32[]{:S(2)}, u32[]{:S(2)}) %all-to-all-start.1) | async-done | bytes 524320 | tf_op jit(solution)/shard_map/advection/all_to_all | solution.py:378
  62.1 1.2 %solve.5 = (f32[256,128]{1,0:T(8,128)S(1)}, f32[256,128]{1,0:T(8,128)S(1)}, f32[128,128]{1,0:T(8,128)S(1)}, f32[128,128]{1,0:T(8,128)S(1)}, f32[256,128]{1,0:T(8,128)S(1)}) custom-call(f32[1024,128]{1,0:T(8,128)S(1)} %bitcast.46, f32[256,128]{1,0:T(8,128)S(1)} %base.3, bf16[128,512]{1,0:T(8,128)(2,1)S(1)} %get-tuple-element.22.weights_h, ...), custom_call_target="tpu_custom_call" | custom-call | flops 1000000 | bytes 1900544 | tf_op jit(solution)/shard_map/solve/pallas_call | solution.py:69
  63.3 5.6 %collective-permute-start.2 = (f32[128,128]{1,0:T(8,128)S(1)}, f32[128,128]{1,0:T(8,128)S(1)}, u32[]{:S(2)}, u32[]{:S(2)}) collective-permute-start(f32[128,128]{1,0:T(8,128)S(1)} %get-tuple-element.36), channel_id=1, source_target_pairs={{0,1},{1,2},{2,3},{3,4},{4,5},{5,6},{6,7},{7,0},{8,9},{9,10},{10,1... | collective-permute-start | bytes 196616 | tf_op jit(solution)/shard_map/solve/ppermute | solution.py:354
  69.0 1.3 %collective-permute-done.2.left = f32[128,128]{1,0:T(8,128)S(1)} collective-permute-done((f32[128,128]{1,0:T(8,128)S(1)}, f32[128,128]{1,0:T(8,128)S(1)}, u32[]{:S(2)}, u32[]{:S(2)}) %collective-permute-start.2) | collective-permute-done | bytes 65568 | tf_op jit(solution)/shard_map/solve/ppermute | solution.py:354
  70.3 2.4 %collective-permute-done.3.right = f32[128,128]{1,0:T(8,128)S(1)} collective-permute-done((f32[128,128]{1,0:T(8,128)S(1)}, f32[128,128]{1,0:T(8,128)S(1)}, u32[]{:S(2)}, u32[]{:S(2)}) %collective-permute-start.3) | collective-permute-done | bytes 65568 | tf_op jit(solution)/shard_map/solve/ppermute | solution.py:355
  72.7 1.7 %solve.6 = (f32[256,128]{1,0:T(8,128)S(1)}, f32[128,128]{1,0:T(8,128)}) custom-call(f32[256,128]{1,0:T(8,128)S(1)} %get-tuple-element.34.residual_ref.residual, f32[256,128]{1,0:T(8,128)S(1)} %get-tuple-element.35.part, f32[128,128]{1,0:T(8,128)S(1)} %collective-permute-done.2.left, f32[128,128]{1,0:T(8,128)S(1)} %collective-permute-done.3.right, ...), custom_call_target="tpu_custom_call" | custom-call | flops 1000000 | bytes 1900544 | tf_op jit(solution)/shard_map/solve/pallas_call | solution.py:69
  74.4 4.3 %all-to-all-start.2 = ((f32[8,16,128]{2,1,0:T(8,128)}), f32[8,16,128]{2,1,0:T(8,128)S(1)}, u32[]{:S(2)}, u32[]{:S(2)}) async-start(f32[8,16,128]{2,1,0:T(8,128)} %bitcast.21), calls=%async_computation.2 | async-start | bytes 131072 | tf_op jit(solution)/shard_map/solve/all_to_all | solution.py:406
  78.7 0.9 %solve.4 = f32[3,4,64,128]{3,2,1,0:T(8,128)} custom-call(f32[1024,128]{1,0:T(8,128)S(1)} %bitcast.47), custom_call_target="tpu_custom_call" | custom-call | flops 1000000 | bytes 524288 | tf_op jit(solution)/shard_map/solve/pallas_call | solution.py:69
  79.6 4.0 %all-to-all-done.2 = f32[8,16,128]{2,1,0:T(8,128)S(1)} async-done(((f32[8,16,128]{2,1,0:T(8,128)}), f32[8,16,128]{2,1,0:T(8,128)S(1)}, u32[]{:S(2)}, u32[]{:S(2)}) %all-to-all-start.2) | async-done | bytes 65568 | tf_op jit(solution)/shard_map/solve/all_to_all | solution.py:406
  83.6 0.8 solve.7
  (55 shorter events, 2.6 us)
Async XLA Ops:
  0.6 24.9 %copy-start = (f32[2,64,128]{2,1,0:T(8,128)S(1)}, f32[2,64,128]{2,1,0:T(8,128)}, u32[]{:S(2)}) copy-start(f32[2,64,128]{2,1,0:T(8,128)} %param.15) | copy-start | bytes 196612
  0.6 1.1 %copy-start.1 = (f32[4,4,64,128]{3,2,1,0:T(8,128)S(1)}, f32[4,4,64,128]{3,2,1,0:T(8,128)}, u32[]{:S(2)}) copy-start(f32[4,4,64,128]{3,2,1,0:T(8,128)} %fields.7) | copy-start | bytes 1572868
  2.8 34.3 %all-to-all-start = ((f32[64,16,128]{2,1,0:T(8,128)}), f32[64,16,128]{2,1,0:T(8,128)S(1)}, u32[]{:S(2)}, u32[]{:S(2)}) async-start(f32[64,16,128]{2,1,0:T(8,128)} %bitcast), calls=%async_computation | async-start | bytes 1048576 | tf_op jit(solution)/shard_map/to_points/all_to_all | solution.py:294
  20.0 0.7 copy-start.10
  20.6 0.7 copy-start.12
  22.1 0.7 copy-start.13
  22.8 0.8 copy-start.7
  23.6 0.9 %copy-start.8 = (f32[2,128,128]{2,1,0:T(8,128)S(1)}, f32[2,128,128]{2,1,0:T(8,128)}, u32[]{:S(2)}) copy-start(f32[2,128,128]{2,1,0:T(8,128)} %param.14) | copy-start | bytes 393220
  24.6 0.7 copy-start.11
  25.3 11.8 %copy-start.6 = (bf16[256,256]{1,0:T(8,128)(2,1)S(1)}, bf16[256,256]{1,0:T(8,128)(2,1)}, u32[]{:S(2)}) copy-start(bf16[256,256]{1,0:T(8,128)(2,1)} %constant.52.clone.modal_l) | copy-start | bytes 393220
  25.4 11.7 %copy-start.5 = (bf16[256,256]{1,0:T(8,128)(2,1)S(1)}, bf16[256,256]{1,0:T(8,128)(2,1)}, u32[]{:S(2)}) copy-start(bf16[256,256]{1,0:T(8,128)(2,1)} %constant.51.clone.modal_h) | copy-start | bytes 393220
  25.6 11.5 %copy-start.3 = (bf16[512,256]{1,0:T(8,128)(2,1)S(1)}, bf16[512,256]{1,0:T(8,128)(2,1)}, u32[]{:S(2)}) copy-start(bf16[512,256]{1,0:T(8,128)(2,1)} %constant.49.clone.both_h) | copy-start | bytes 786436
  25.6 11.5 %copy-start.4 = (bf16[512,256]{1,0:T(8,128)(2,1)S(1)}, bf16[512,256]{1,0:T(8,128)(2,1)}, u32[]{:S(2)}) copy-start(bf16[512,256]{1,0:T(8,128)(2,1)} %constant.50.clone.both_l) | copy-start | bytes 786436
  39.3 22.8 %all-to-all-start.1 = ((f32[64,16,128]{2,1,0:T(8,128)}), f32[64,16,128]{2,1,0:T(8,128)S(1)}, u32[]{:S(2)}, u32[]{:S(2)}) async-start(f32[64,16,128]{2,1,0:T(8,128)} %bitcast.7), calls=%async_computation.1 | async-start | bytes 1048576 | tf_op jit(solution)/shard_map/advection/all_to_all | solution.py:378
  46.9 0.8 copy-start.9
  47.9 1.0 %copy-start.2 = (f32[4,4,64,128]{3,2,1,0:T(8,128)S(1)}, f32[4,4,64,128]{3,2,1,0:T(8,128)}, u32[]{:S(2)}) copy-start(f32[4,4,64,128]{3,2,1,0:T(8,128)} %fields.7) | copy-start | bytes 1572868
  50.2 4.2 %collective-permute-start = (f32[128,128]{1,0:T(8,128)S(1)}, f32[128,128]{1,0:T(8,128)S(1)}, u32[]{:S(2)}, u32[]{:S(2)}) collective-permute-start(f32[128,128]{1,0:T(8,128)S(1)} %get-tuple-element.31), channel_id=1, source_target_pairs={{0,1},{1,2},{2,3},{3,4},{4,5},{5,6},{6,7},{7,0},{8,9},{9,10},{10,1... | collective-permute-start | bytes 196616 | tf_op jit(solution)/shard_map/base/ppermute | solution.py:354
  53.1 4.0 %collective-permute-start.1 = (f32[128,128]{1,0:T(8,128)S(1)}, f32[128,128]{1,0:T(8,128)S(1)}, u32[]{:S(2)}, u32[]{:S(2)}) collective-permute-start(f32[128,128]{1,0:T(8,128)S(1)} %get-tuple-element.32), channel_id=1, source_target_pairs={{1,0},{2,1},{3,2},{4,3},{5,4},{6,5},{7,6},{0,7},{9,8},{10,9},{11,1... | collective-permute-start | bytes 196616 | tf_op jit(solution)/shard_map/base/ppermute | solution.py:355
  63.3 7.0 %collective-permute-start.2 = (f32[128,128]{1,0:T(8,128)S(1)}, f32[128,128]{1,0:T(8,128)S(1)}, u32[]{:S(2)}, u32[]{:S(2)}) collective-permute-start(f32[128,128]{1,0:T(8,128)S(1)} %get-tuple-element.36), channel_id=1, source_target_pairs={{0,1},{1,2},{2,3},{3,4},{4,5},{5,6},{6,7},{7,0},{8,9},{9,10},{10,1... | collective-permute-start | bytes 196616 | tf_op jit(solution)/shard_map/solve/ppermute | solution.py:354
  69.0 3.7 %collective-permute-start.3 = (f32[128,128]{1,0:T(8,128)S(1)}, f32[128,128]{1,0:T(8,128)S(1)}, u32[]{:S(2)}, u32[]{:S(2)}) collective-permute-start(f32[128,128]{1,0:T(8,128)S(1)} %get-tuple-element.37), channel_id=1, source_target_pairs={{1,0},{2,1},{3,2},{4,3},{5,4},{6,5},{7,6},{0,7},{9,8},{10,9},{11,1... | collective-permute-start | bytes 196616 | tf_op jit(solution)/shard_map/solve/ppermute | solution.py:355
  74.4 9.2 %all-to-all-start.2 = ((f32[8,16,128]{2,1,0:T(8,128)}), f32[8,16,128]{2,1,0:T(8,128)S(1)}, u32[]{:S(2)}, u32[]{:S(2)}) async-start(f32[8,16,128]{2,1,0:T(8,128)} %bitcast.21), calls=%async_computation.2 | async-start | bytes 131072 | tf_op jit(solution)/shard_map/solve/all_to_all | solution.py:406

commit v2 on v1

v2 whole, which is shorter than its diff:
```python
import functools

import jax
import jax.numpy as jnp
import numpy as np
from jax import lax
from jax.experimental import pallas as pl
from jax.experimental.pallas import tpu as pltpu
from jax.sharding import PartitionSpec as P

PLANES = 256
POINTS = 128
ELEMS = 64
OWN = 4
EDGES = 4
TRACE = 16
RIM = 32
ROWS = OWN * ELEMS
AXIAL_WAVE = 0.01
INVERSE_STEP = 0.5
LATENT = 2.0
F32 = jnp.float32
BF16 = jnp.bfloat16


def halves_np(table):
    high = table.astype(np.float32).astype(jnp.bfloat16)
    low = (table - high.astype(np.float64)).astype(np.float32).astype(jnp.bfloat16)
    return high, low


@functools.cache
def axial_tables():
    points = np.arange(PLANES)[:, None]
    planes = np.arange(PLANES)[None, :]
    mode = np.where(planes == 1, PLANES // 2, planes // 2)
    angles = 2.0 * np.pi / PLANES * ((points * mode) % PLANES)
    sine = (planes % 2 == 1) & (planes != 1)
    basis = np.where(sine, np.sin(angles), np.cos(angles))
    wave = np.where(planes >= 2, mode, 0) * AXIAL_WAVE
    slope = wave * np.where(sine, np.cos(angles), -np.sin(angles))
    weights = np.where(planes <= 1, 1.0 / PLANES, 2.0 / PLANES)
    modal = -np.transpose(weights * basis)
    both_h, both_l = halves_np(np.concatenate([basis, slope], axis=0))
    modal_h, modal_l = halves_np(modal)
    return np.concatenate([both_h, both_l, modal_h, modal_l], axis=0)


def halves(value):
    high = value.astype(BF16)
    return high, (value - high.astype(F32)).astype(BF16)


def product(left, right):
    return jnp.dot(left, right, preferred_element_type=F32)


def product3(left, right):
    return product(left[0], right[0]) + (product(left[1], right[0]) + product(left[0], right[1]))


def lanes(rows):
    return lax.broadcasted_iota(jnp.int32, (rows, POINTS), 1)


def edge_of(lane):
    return (lane % (EDGES * TRACE)) // TRACE


def call(kernel, outs, *args, flops=0, specs=None):
    return pl.pallas_call(
        kernel,
        grid=(1,) if specs else (),
        out_shape=[jax.ShapeDtypeStruct(shape, kind) for shape, kind in outs],
        in_specs=specs or [pl.BlockSpec(memory_space=pltpu.VMEM)] * len(args),
        out_specs=[pl.BlockSpec(memory_space=pltpu.VMEM)] * len(outs),
        compiler_params=pltpu.CompilerParams(vmem_limit_bytes=24 * 1024 * 1024),
        cost_estimate=pl.CostEstimate(
            flops=flops or 10**7,
            bytes_accessed=sum(a.size * a.dtype.itemsize for a in args),
            transcendentals=0,
        ),
    )(*args)


def stacked(value):
    return jnp.concatenate(halves(value), axis=1)


def product_stacked(value, twice_h, low):
    pair = stacked(value)
    return product(pair, twice_h) + product(pair[:, : low.shape[0]], low)


def pack_kernel(fields, out):
    for plane in range(OWN):
        for field in range(4):
            out[pl.ds(plane * 4 + field, ELEMS, stride=16), :] = fields[field, plane]


def physical_kernel(fields, factors, melting, deriv_h, deriv_l, tables, out):
    spectral = jnp.concatenate([fields[pl.ds(c, PLANES, stride=4), :] for c in range(4)], axis=1)
    both_h, both_l, modal_h, modal_l = (
        tables[start : start + size]
        for start, size in ((0, 512), (512, 512), (1024, 256), (1280, 256))
    )
    points = product3((both_h, both_l), halves(spectral))
    values = [points[:PLANES, c * POINTS : (c + 1) * POINTS] for c in range(4)]
    first = values[0] * factors[0:1, :]
    second = values[1] * factors[1:2, :]
    third = values[2]
    terms = []
    for c in range(4):
        slopes = product_stacked(values[c], deriv_h[...], deriv_l[...])
        term = (
            first * slopes[:, :POINTS]
            + second * slopes[:, POINTS:]
            + third * points[PLANES:, c * POINTS : (c + 1) * POINTS]
        )
        terms.append(term * melting[...] if c == 3 else term)
    modal = product3((modal_h, modal_l), halves(jnp.concatenate(terms, axis=1)))
    for c in range(4):
        out[pl.ds(c, PLANES, stride=4), :] = modal[:, c * POINTS : (c + 1) * POINTS]


def upright(row):
    size = row.shape[1]
    down = lax.broadcasted_iota(jnp.int32, (size, size), 0)
    along = lax.broadcasted_iota(jnp.int32, (size, size), 1)
    return jnp.sum(jnp.where(down == along, row, 0.0), axis=1, keepdims=True)


def exact(left, right):
    return jnp.dot(left, right, preferred_element_type=F32, precision=lax.Precision.HIGHEST)


def two_halves(doubled):
    high = doubled.astype(BF16).astype(F32)
    return jnp.where(lanes(doubled.shape[0]) < EDGES * TRACE, high, doubled - high)


def facing_local(split_traces, gather):
    edge = edge_of(lanes(ELEMS))
    parts = []
    for plane in range(OWN):
        own = split_traces[plane * ELEMS : (plane + 1) * ELEMS]
        stack = [jnp.where(edge == j, own, 0.0).astype(BF16) for j in range(EDGES)]
        parts.append(product(gather, jnp.concatenate(stack, axis=0)))
    return jnp.concatenate(parts, axis=0)


def packed_rims(rims, edge):
    lane = lanes(RIM)
    total = jnp.zeros((RIM, POINTS), F32)
    for plane in range(OWN):
        rows = rims[plane * RIM : (plane + 1) * RIM]
        for which in range(2):
            at = plane * 2 * TRACE + which * TRACE
            moved = pltpu.roll(rows, (at - which * EDGES * TRACE - edge * TRACE) % POINTS, 1)
            total = jnp.where((lane >= at) & (lane < at + TRACE), moved, total)
    return total


def unpacked_rims(packed, edge):
    lane = lanes(RIM)
    parts = []
    for plane in range(OWN):
        total = jnp.zeros((RIM, POINTS), F32)
        for which in range(2):
            at = which * EDGES * TRACE + edge * TRACE
            moved = pltpu.roll(packed, (at - plane * 2 * TRACE - which * TRACE) % POINTS, 1)
            total = jnp.where((lane >= at) & (lane < at + TRACE), moved, total)
        parts.append(total)
    return jnp.concatenate(parts, axis=0)


def doubled_sum(value):
    return value + pltpu.roll(value, EDGES * TRACE, 1)


def start_helmholtz(vector, weights_h, weights_l, back, gather, to_rim, scale_one, scale_two):
    images = product_stacked(vector, weights_h, weights_l)
    stiff, own, doubled, crossing, stiff_trace, own_trace = (
        images[:, k * POINTS : (k + 1) * POINTS] for k in range(6)
    )
    traces_split = two_halves(doubled)
    facing = facing_local(traces_split, gather).astype(BF16)
    coupling = product(jnp.concatenate([facing, facing], axis=1), back)
    part = scale_one * vector + scale_two * stiff + own - coupling[:, :POINTS]
    part_trace = scale_one * doubled + scale_two * stiff_trace + own_trace - coupling[:, POINTS:]
    split = jnp.concatenate([traces_split, two_halves(part_trace)], axis=1).astype(BF16)
    rims = product(to_rim, split)
    first, second = doubled_sum(rims[:, :POINTS]), doubled_sum(rims[:, POINTS:])
    rims = jnp.where(lanes(ROWS) < EDGES * TRACE, first, second)
    half = OWN * RIM
    return part, packed_rims(rims[:half], 1), packed_rims(rims[half:], 3), crossing


def arrived(left, right, from_rim):
    both = jnp.concatenate([unpacked_rims(left[...], 3), unpacked_rims(right[...], 1)], axis=0)
    spread = product(from_rim[...], stacked(both))
    return spread[:, :POINTS], spread[:, POINTS:]


def rim_coupling(high, low, back):
    facing = jnp.where(
        lanes(ROWS) < EDGES * TRACE, high, pltpu.roll(low, EDGES * TRACE, 1)
    ).astype(BF16)
    return product(jnp.concatenate([facing, facing], axis=1), back[:, :POINTS])


def prepare_kernel(
    stiffness, traces, scale_row, near_rows, rim_rows, flags, deriv, geom, fields,
    weights_h, weights_l, back, gather, to_rim, from_rim, rim_mask, scale_one, scale_two,
    melting, factors, deriv_h, deriv_l, part_out, left_out, right_out,
):
    plane_rank = lax.axis_index("plane")
    dom_rank = lax.axis_index("dom")
    edges = traces[...].reshape(EDGES * TRACE, POINTS)
    turned = jnp.concatenate([edges[2 * TRACE :], edges[: 2 * TRACE]], axis=0)
    edges = jnp.concatenate([edges, edges], axis=0)
    turned = jnp.concatenate([turned, turned], axis=0)
    edges_up = jnp.transpose(edges)
    turned_up = jnp.transpose(turned)
    stiff = stiffness[...]
    own = 0.5 * exact(edges_up, edges)
    down = lax.broadcasted_iota(jnp.int32, (POINTS, POINTS), 0)
    along = lanes(POINTS)
    lower = EDGES * TRACE
    kept = (
        (down < lower)
        & (along >= lower)
        & (edge_of(down) == edge_of(along))
        & (edge_of(along) % 2 == 1)
    )
    crossing = exact(edges_up, jnp.where(kept, exact(turned, turned_up), 0.0))
    weights = jnp.concatenate(
        [stiff, own, turned_up, crossing, exact(stiff, turned_up), exact(own, turned_up)], axis=1
    )
    high, low = halves(weights)
    weights_h[...] = jnp.concatenate([high, high], axis=0)
    weights_l[...] = low
    high, low = halves(jnp.concatenate([edges, exact(edges, turned_up)], axis=1))
    back[...] = jnp.concatenate([high, low], axis=0)

    rows = near_rows[...]
    rows = jnp.where(rows >= 0, rows - dom_rank * ELEMS, rows).astype(F32)
    near = [upright(rows[edge : edge + 1]).astype(jnp.int32) for edge in range(EDGES)]
    cell = lax.broadcasted_iota(jnp.int32, (ELEMS, EDGES * ELEMS), 1)
    wanted = near[EDGES - 1]
    for edge in range(EDGES - 1):
        wanted = jnp.where(cell // ELEMS == edge, near[edge], wanted)
    gather[...] = jnp.where(cell % ELEMS == wanted, 1.0, 0.0).astype(BF16)
    wide = lax.broadcasted_iota(jnp.int32, (ROWS, ROWS), 1)
    rims = [upright(rim_rows[side : side + 1, :].astype(F32)).astype(jnp.int32) for side in range(2)]
    column = jnp.concatenate([rims[side] + plane * ELEMS for side in range(2) for plane in range(OWN)], axis=0)
    picked = jnp.where(wide == column, 1.0, 0.0)
    to_rim[...] = picked.astype(BF16)
    from_rim[...] = jnp.transpose(picked).astype(BF16)
    lane = lanes(ELEMS)
    edge = edge_of(lane)
    beyond = ((edge == 1) & (near[1] == -2)) | ((edge == 3) & (near[3] == -2))
    mask = jnp.where(beyond & (lane >= lower), 1.0, 0.0)
    scale = jnp.broadcast_to(upright(scale_row[...]), (ELEMS, POINTS))
    plane = plane_rank * OWN + lax.broadcasted_iota(jnp.int32, (ROWS, POINTS), 0) // ELEMS
    wave = jnp.where(plane == 1, PLANES // 2, plane // 2).astype(F32) * AXIAL_WAVE
    one = INVERSE_STEP + wave * wave
    two = jnp.concatenate([scale] * OWN, axis=0)
    rim_mask[...] = jnp.concatenate([mask] * OWN, axis=0)
    scale_one[...] = one
    scale_two[...] = two

    melted = upright(flags[...].astype(F32))
    melting[...] = jnp.broadcast_to(1.0 / (1.0 + LATENT * melted), (PLANES, POINTS))
    for side in range(2):
        factors[side : side + 1, :] = geom[side, pl.ds(plane_rank, 1), :]
    high, low = halves(jnp.concatenate([jnp.transpose(deriv[0]), jnp.transpose(deriv[1])], axis=1))
    deriv_h[...] = jnp.concatenate([high, high], axis=0)
    deriv_l[...] = low

    vector = fields[0].reshape(ROWS, POINTS)
    part, left, right, _ = start_helmholtz(
        vector, weights_h[...], weights_l[...], back[...], gather[...], to_rim[...], one, two
    )
    part_out[...] = part
    left_out[...] = left
    right_out[...] = right


def base_kernel(fields, part, left, right, from_rim, back, out):
    high, low = arrived(left, right, from_rim)
    image = part[...] - rim_coupling(high, low, back[...])
    out[...] = INVERSE_STEP * fields[0].reshape(ROWS, POINTS) - image


def residual_kernel(
    modal, base, weights_h, weights_l, back, gather, to_rim, scale_one, scale_two,
    residual_out, part_out, left_out, right_out, crossing_out,
):
    heat = [modal[pl.ds(plane * 4 + 3, ELEMS, stride=16), :] for plane in range(OWN)]
    residual = base[...] + jnp.concatenate(heat, axis=0)
    part, left, right, crossing = start_helmholtz(
        residual,
        weights_h[...],
        weights_l[...],
        back[...],
        gather[...],
        to_rim[...],
        scale_one[...],
        scale_two[...],
    )
    left_out[...] = left
    right_out[...] = right
    residual_out[...] = residual
    part_out[...] = part
    crossing_out[...] = crossing


def momentum_kernel(modal, out):
    for field in range(3):
        for plane in range(OWN):
            out[field, plane] = modal[pl.ds(plane * 4 + field, ELEMS, stride=16), :]


def moments_kernel(
    residual_ref, part, left, right, crossing, from_rim, weights_h, weights_l, back, gather,
    rim_mask, scale_one, scale_two, image_out, sums_out,
):
    high, low = arrived(left, right, from_rim)
    image = part[...] - rim_coupling(high, low, back[...])
    image_out[...] = image
    residual = residual_ref[...]
    weights = [
        jnp.concatenate([w[:, :POINTS], w[:, 2 * POINTS : 3 * POINTS]], axis=1)
        for w in (weights_h, weights_l)
    ]
    images = product_stacked(image, *weights)
    stiff, doubled = images[:, :POINTS], images[:, POINTS:]
    facing = doubled_sum(facing_local(two_halves(doubled), gather[...]))
    facing = facing + (high + low) - crossing[...] * rim_mask[...]
    own = pltpu.roll(doubled, 2 * TRACE, 1)
    jumps = jnp.where(lanes(ROWS) >= EDGES * TRACE, own * (own - facing), 0.0)
    square = image * image
    cubic = scale_one[...] * square + scale_two[...] * (image * stiff) + jumps
    for number, value in enumerate((residual * residual, residual * image, square, cubic)):
        for plane in range(OWN):
            total = jnp.sum(value[plane * ELEMS : (plane + 1) * ELEMS], axis=0, keepdims=True)
            for peer in range(8):
                row = peer * 16 + number * OWN + plane
                sums_out[row : row + 1, :] = total


def final_kernel(sums, fields, residual, image, out):
    total = sums[0:16, :]
    for peer in range(1, 8):
        total = total + sums[peer * 16 : (peer + 1) * 16, :]
    total = jnp.sum(total, axis=1, keepdims=True)
    m0, m1, m2, m3 = (total[k * OWN : (k + 1) * OWN] for k in range(4))
    step = m0 / m1
    after = m0 + step * (step * m2 - 2.0 * m1)
    after_image = m1 + step * (step * m3 - 2.0 * m2)
    ratio = after / m0
    second = after / (after_image - ratio * after / step)
    on_residual = step + second * (1.0 + ratio)
    on_image = -second * step
    for plane in range(OWN):
        rows = pl.ds(plane * ELEMS, ELEMS)
        out[plane] = (
            fields[0, plane]
            + on_residual[plane : plane + 1] * residual[rows, :]
            + on_image[plane : plane + 1] * image[rows, :]
        )


def per_device(
    spectral_fields,
    deriv_ops,
    geom,
    stiffness,
    stiff_scale,
    traces,
    neighbors,
    rim_lists,
    melt_flags,
):
    count = lax.axis_size("dom")
    groups = lax.axis_size("plane")
    whole = ((ROWS, POINTS), F32)
    rims = ((RIM, POINTS), F32)
    plain = pl.BlockSpec(memory_space=pltpu.VMEM)
    heat_only = pl.BlockSpec((1, OWN, ELEMS, POINTS), lambda *_: (3, 0, 0, 0), memory_space=pltpu.VMEM)

    with jax.named_scope("to_points"):
        (packed,) = call(pack_kernel, [((ELEMS * 16, POINTS), F32)], spectral_fields)
        gathered = lax.all_to_all(
            packed.reshape(groups, 16, POINTS), "plane", split_axis=0, concat_axis=0, tiled=True
        ).reshape(groups * 16, POINTS)

    def exchange(left, right):
        from_left = lax.ppermute(right, "dom", [(i, (i + 1) % count) for i in range(count)])
        from_right = lax.ppermute(left, "dom", [((i + 1) % count, i) for i in range(count)])
        return from_left, from_right

    with jax.named_scope("base"):
        (
            weights_h, weights_l, back, gather, to_rim, from_rim, rim_mask, scale_one, scale_two,
            melting, factors, deriv_h, deriv_l, part, left, right,
        ) = call(
            prepare_kernel,
            [
                ((2 * POINTS, 6 * POINTS), BF16),
                ((POINTS, 6 * POINTS), BF16),
                ((2 * POINTS, 2 * POINTS), BF16),
                ((ELEMS, EDGES * ELEMS), BF16),
                ((ROWS, ROWS), BF16),
                ((ROWS, ROWS), BF16),
                whole,
                whole,
                whole,
                whole,
                ((2, POINTS), F32),
                ((2 * POINTS, 2 * POINTS), BF16),
                ((POINTS, 2 * POINTS), BF16),
                whole,
                rims,
                rims,
            ],
            stiffness,
            traces,
            stiff_scale.reshape(1, ELEMS),
            neighbors.T,
            rim_lists[0],
            melt_flags.reshape(1, PLANES),
            deriv_ops,
            geom,
            spectral_fields,
            specs=[plain] * 8 + [heat_only],
        )
        left, right = exchange(left, right)
        (base,) = call(
            base_kernel,
            [whole],
            spectral_fields,
            part,
            left,
            right,
            from_rim,
            back,
            specs=[heat_only] + [plain] * 5,
        )

    with jax.named_scope("advection"):
        gathered, base = lax.optimization_barrier((gathered, base))
        (modal,) = call(
            physical_kernel,
            [((groups * 16, POINTS), F32)],
            gathered,
            factors,
            melting,
            deriv_h,
            deriv_l,
            jnp.asarray(axial_tables()),
            flops=10**9,
        )
        returned = lax.all_to_all(
            modal.reshape(groups, 16, POINTS), "plane", split_axis=0, concat_axis=0, tiled=True
        ).reshape(ELEMS * 16, POINTS)

    with jax.named_scope("solve"):
        residual, part, left, right, crossing = call(
            residual_kernel,
            [whole, whole, rims, rims, whole],
            returned,
            base,
            weights_h,
            weights_l,
            back,
            gather,
            to_rim,
            scale_one,
            scale_two,
        )
        left, right = exchange(left, right)
        (momentum,) = call(momentum_kernel, [((3, OWN, ELEMS, POINTS), F32)], returned)
        left, right, momentum = lax.optimization_barrier((left, right, momentum))
        image, sums = call(
            moments_kernel,
            [whole, ((8 * 16, POINTS), F32)],
            residual,
            part,
            left,
            right,
            crossing,
            from_rim,
            weights_h,
            weights_l,
            back,
            gather,
            rim_mask,
            scale_one,
            scale_two,
        )
        sums = lax.all_to_all(
            sums.reshape(8, 16, POINTS), "dom", split_axis=0, concat_axis=0, tiled=True
        ).reshape(8 * 16, POINTS)
        (temperature,) = call(
            final_kernel,
            [((OWN, ELEMS, POINTS), F32)],
            sums,
            spectral_fields,
            residual,
            image,
            specs=[plain, heat_only, plain, plain],
        )
    return momentum, temperature


def solution(mesh):
    placed = (
        P(None, "plane", "dom", None),
        P(),
        P(None, "dom", None),
        P(),
        P("dom"),
        P(),
        P("dom", None),
        P("dom", None, None),
        P(None, ("dom", "plane")),
    )
    return jax.shard_map(
        per_device,
        mesh=mesh,
        in_specs=placed,
        out_specs=(P(None, "plane", "dom", None), P("plane", "dom", None)),
        check_vma=False,
    )
```

time: 85 us -> 83 us (0.976)
  blocking collectives: 0 us -> 31.4 us
  waiting for transfers between devices: 27.4 us -> 14.7 us
  starting transfers between devices: 36.7 us -> 25.1 us
  local copies, waits for them, and re-layouts: 7.98 us -> 2.81 us
  Pallas kernels: 9.98 us -> 7.7 us
  matrix products: 1.13 us -> 0 us
    all_to_all x0 -> x2, blocking collectives: none -> 31.4 us  [the longest x1 22.4 us: per_device(): lax.all_to_all(modal.reshape(groups, 16, POINTS), 'plane', split_axis=0,...]
    all_to_all x2 -> x0, starting transfers between devices: 11.1 us -> none  [the longest x1 6.75 us: per_device(): lax.all_to_all(modal.reshape(groups, 16, POINTS), 'plane', split_axis=0,...]
    all_to_all x2 -> x0, waiting for transfers between devices: 8.59 us -> none  [the longest x1 4.6 us: per_device(): lax.all_to_all(modal.reshape(groups, 16, POINTS), 'plane', split_axis=0,...]
    unnamed x31 -> x22, local copies, waits for them, and re-layouts: 6.63 us -> 2.81 us
    pallas_call x9 -> x8, Pallas kernels: 9.98 us -> 7.7 us  [call(): pl.pallas_call(kernel, grid=(1,) if specs else (), out_shape=[jax.ShapeDt...]
    all_to_all x1, waiting for transfers between devices: 11.1 us -> 9 us  [per_device(): lax.all_to_all(packed.reshape(groups, 16, POINTS), 'plane', split_axis=0,...]
    ppermute x2, waiting for transfers between devices: 2.66 us -> 0.87 us  [exchange(): lax.ppermute(right, 'dom', [(i, (i + 1) % count) for i in range(count)])]
    dot_general x5 -> x0, matrix products: 1.13 us -> none  [the longest x1 0.31 us: per_device(): jnp.dot(traces[3].T, square_one, precision=highest)]
  transfers between devices with their start and end apart: 7 -> 5, of which waited for: 7 -> 4; matrix products, arithmetic and copies ran while one was open for 4% -> 0% of each run, Pallas kernels for 3% -> 3%
where the time goes in v2:
time: 83 us; the launch traced here: 82.6 us
  blocking collectives  31.4 us (38%)
  starting transfers between devices  25.1 us (30%)
  waiting for transfers between devices  14.7 us (18%)
  Pallas kernels  7.7 us (9%)
  local copies, waits for them, and re-layouts  2.81 us (3%)
    all_to_all x1, blocking collectives, per_device(): lax.all_to_all(modal.reshape(groups, 16, POINTS), 'plane', split_axis=0,...  22.4 us
    all_to_all x1, starting transfers between devices, per_device(): lax.all_to_all(packed.reshape(groups, 16, POINTS), 'plane', split_axis=0,...  17.3 us
    all_to_all x1, waiting for transfers between devices, per_device(): lax.all_to_all(packed.reshape(groups, 16, POINTS), 'plane', split_axis=0,...  9 us
    all_to_all x1, blocking collectives, per_device(): lax.all_to_all(sums.reshape(8, 16, POINTS), 'dom', split_axis=0, concat_a...  8.99 us
    ppermute x2, starting transfers between devices, exchange(): lax.ppermute(right, 'dom', [(i, (i + 1) % count) for i in range(count)])  7.84 us
    pallas_call x8, Pallas kernels, call(): pl.pallas_call(kernel, grid=(1,) if specs else (), out_shape=[jax.ShapeDt...  7.7 us
    ppermute x2, waiting for transfers between devices, exchange(): lax.ppermute(left, 'dom', [((i + 1) % count, i) for i in range(count)])  4.88 us
    unnamed x22, local copies, waits for them, and re-layouts  2.81 us
  transfers between devices with their start and end apart: 5, of which 4 were waited for; matrix products, arithmetic and copies ran while one was open for 0% of the time, Pallas kernels for 3%

profile of v2, /device:TPU:1, one launch (start us, length us, event | category | flops | bytes accessed | tf_op | source)
XLA Modules:
  0.0 82.6 jit_solution(245352468325602893)
XLA Ops:
  0.6 0.0 copy-start
  0.6 1.0 %copy-done = f32[4,4,64,128]{3,2,1,0:T(8,128)S(1)} copy-done((f32[4,4,64,128]{3,2,1,0:T(8,128)S(1)}, f32[4,4,64,128]{3,2,1,0:T(8,128)}, u32[]{:S(2)}) %copy-start) | copy-done | bytes 524312
  1.7 1.0 %to_points.1 = f32[1024,128]{1,0:T(8,128)} custom-call(f32[4,4,64,128]{3,2,1,0:T(8,128)S(1)} %copy-done), custom_call_target="tpu_custom_call" | custom-call | flops 10000000 | bytes 524288 | tf_op jit(solution)/shard_map/to_points/pallas_call | solution.py:71
  2.7 0.0 copy-start.5
  2.7 0.0 copy-start.8
  2.8 17.3 %all-to-all-start = ((f32[64,16,128]{2,1,0:T(8,128)}), f32[64,16,128]{2,1,0:T(8,128)S(1)}, u32[]{:S(2)}, u32[]{:S(2)}) async-start(f32[64,16,128]{2,1,0:T(8,128)} %bitcast), calls=%async_computation | async-start | bytes 1048576 | tf_op jit(solution)/shard_map/to_points/all_to_all | solution.py:395
  20.0 0.0 copy-start.6
  20.1 0.0 copy-start.7
  20.1 0.0 copy-start.9
  20.1 0.0 copy-done.1
  20.1 0.0 copy-done.2
  20.1 0.6 copy-done.6
  20.7 0.0 copy-done.7
  20.7 1.4 %base.2 = (bf16[256,768]{1,0:T(8,128)(2,1)S(1)}, bf16[128,768]{1,0:T(8,128)(2,1)S(1)}, bf16[256,256]{1,0:T(8,128)(2,1)S(1)}, bf16[64,256]{1,0:T(8,128)(2,1)S(1)}...) custom-call(f32[128,128]{1,0:T(8,128)S(1)} %copy-done.3, ...), custom_call_target="tpu_custom_call" | custom-call | flops 10000000 | bytes 821760 | tf_op jit(solution)/shard_map/base/pallas_call | solution.py:71
  22.2 2.1 %collective-permute-start = (f32[32,128]{1,0:T(8,128)S(1)}, f32[32,128]{1,0:T(8,128)S(1)}, u32[]{:S(2)}, u32[]{:S(2)}) collective-permute-start(f32[32,128]{1,0:T(8,128)S(1)} %get-tuple-element.31), channel_id=1, source_target_pairs={{0,1},{1,2},{2,3},{3,4},{4,5},{5,6},{6,7},{7,0},{8,9},{9,10},{10,1... | collective-permute-start | bytes 49160 | tf_op jit(solution)/shard_map/base/ppermute | solution.py:400
  24.3 0.0 collective-permute-start.1
  24.3 0.9 %collective-permute-done.left = f32[32,128]{1,0:T(8,128)S(1)} collective-permute-done((f32[32,128]{1,0:T(8,128)S(1)}, f32[32,128]{1,0:T(8,128)S(1)}, u32[]{:S(2)}, u32[]{:S(2)}) %collective-permute-start) | collective-permute-done | bytes 16416 | tf_op jit(solution)/shard_map/base/ppermute | solution.py:400
  25.1 2.6 %collective-permute-done.1.right = f32[32,128]{1,0:T(8,128)S(1)} collective-permute-done((f32[32,128]{1,0:T(8,128)S(1)}, f32[32,128]{1,0:T(8,128)S(1)}, u32[]{:S(2)}, u32[]{:S(2)}) %collective-permute-start.1) | collective-permute-done | bytes 16416 | tf_op jit(solution)/shard_map/base/ppermute | solution.py:401
  27.7 0.5 base.3
  28.2 9.0 %all-to-all-done = f32[64,16,128]{2,1,0:T(8,128)S(1)} async-done(((f32[64,16,128]{2,1,0:T(8,128)}), f32[64,16,128]{2,1,0:T(8,128)S(1)}, u32[]{:S(2)}, u32[]{:S(2)}) %all-to-all-start) | async-done | bytes 524320 | tf_op jit(solution)/shard_map/to_points/all_to_all | solution.py:395
  37.2 1.1 %copy-done.10 = bf16[1536,256]{1,0:T(8,128)(2,1)S(1)} copy-done((bf16[1536,256]{1,0:T(8,128)(2,1)S(1)}, bf16[1536,256]{1,0:T(8,128)(2,1)}, u32[]{:S(2)}) %copy-start.10) | copy-done | bytes 786456
  38.4 1.2 %advection.1 = f32[1024,128]{1,0:T(8,128)S(1)} custom-call(f32[1024,128]{1,0:T(8,128)S(1)} %bitcast.12, f32[2,128]{1,0:T(2,128)S(1)} %get-tuple-element.36.factors, f32[256,128]{1,0:T(8,128)S(1)} %get-tuple-element.37.melting, bf16[256,256]{1,0:T(8,128)(2,1)S(1)} %get-tuple-element.38.deriv_h, bf16[128,256]{1,0:T(8,128)(2,1)S(1)} %get-tuple-element.39.deriv_l, ...), custom_call_target="tpu_custom_call" | custom-call | flops 1000000000 | bytes 1639424 | tf_op jit(solution)/shard_map/advection/pallas_call | solution.py:71
  39.6 22.4 %all_to_all.15 = f32[64,16,128]{2,1,0:T(8,128)S(1)} all-to-all(f32[64,16,128]{2,1,0:T(8,128)S(1)} %bitcast.13), channel_id=1, replica_groups=mesh['plane'=64,'dom'=8] {'plane'}, dimensions={0} | all-to-all | bytes 1048576 | tf_op jit(solution)/shard_map/advection/all_to_all | solution.py:465
  62.0 0.9 %solve.4 = (f32[256,128]{1,0:T(8,128)S(1)}, f32[256,128]{1,0:T(8,128)S(1)}, f32[32,128]{1,0:T(8,128)S(1)}, f32[32,128]{1,0:T(8,128)S(1)}, f32[256,128]{1,0:T(8,128)S(1)}) custom-call(f32[1024,128]{1,0:T(8,128)S(1)} %bitcast.10, f32[256,128]{1,0:T(8,128)S(1)} %base.3, bf16[256,768]{1,0:T(8,128)(2,1)S(1)} %get-tuple-element.41.weights_h, ...), custom_call_target="tpu_custom_call" | custom-call | flops 10000000 | bytes 1802240 | tf_op jit(solution)/shard_map/solve/pallas_call | solution.py:71
  62.9 5.8 %collective-permute-start.2 = (f32[32,128]{1,0:T(8,128)S(1)}, f32[32,128]{1,0:T(8,128)S(1)}, u32[]{:S(2)}, u32[]{:S(2)}) collective-permute-start(f32[32,128]{1,0:T(8,128)S(1)} %get-tuple-element.47), channel_id=1, source_target_pairs={{0,1},{1,2},{2,3},{3,4},{4,5},{5,6},{6,7},{7,0},{8,9},{9,10},{10,1... | collective-permute-start | bytes 49160 | tf_op jit(solution)/shard_map/solve/ppermute | solution.py:400
  68.7 0.0 collective-permute-start.3
  68.7 0.9 %solve.5 = f32[3,4,64,128]{3,2,1,0:T(8,128)} custom-call(f32[1024,128]{1,0:T(8,128)S(1)} %bitcast.11), custom_call_target="tpu_custom_call" | custom-call | flops 10000000 | bytes 524288 | tf_op jit(solution)/shard_map/solve/pallas_call | solution.py:71
  69.6 0.0 collective-permute-done.2.left
  69.6 2.3 %collective-permute-done.3.right = f32[32,128]{1,0:T(8,128)S(1)} collective-permute-done((f32[32,128]{1,0:T(8,128)S(1)}, f32[32,128]{1,0:T(8,128)S(1)}, u32[]{:S(2)}, u32[]{:S(2)}) %collective-permute-start.3) | collective-permute-done | bytes 16416 | tf_op jit(solution)/shard_map/solve/ppermute | solution.py:401
  71.9 0.9 %solve.6 = (f32[256,128]{1,0:T(8,128)S(1)}, f32[128,128]{1,0:T(8,128)S(1)}) custom-call(f32[256,128]{1,0:T(8,128)S(1)} %get-tuple-element.50.residual_ref.residual, f32[256,128]{1,0:T(8,128)S(1)} %get-tuple-element.51.part, f32[32,128]{1,0:T(8,128)S(1)} %collective-permute-done.2.left, f32[32,128]{1,0:T(8,128)S(1)} %collective-permute-done.3.right, ...), custom_call_target="tpu_custom_call" | custom-call | flops 10000000 | bytes 1703936 | tf_op jit(solution)/shard_map/solve/pallas_call | solution.py:71
  72.8 9.0 %all_to_all.16 = f32[8,16,128]{2,1,0:T(8,128)S(1)} all-to-all(f32[8,16,128]{2,1,0:T(8,128)S(1)} %bitcast.15), channel_id=1, replica_groups=mesh['plane'=64,'dom'=8] {'dom'}, dimensions={0} | all-to-all | bytes 131072 | tf_op jit(solution)/shard_map/solve/all_to_all | solution.py:503
  81.8 0.8 solve.7
  (10 shorter events, 0.0 us)
Async XLA Ops:
  0.6 1.0 %copy-start = (f32[4,4,64,128]{3,2,1,0:T(8,128)S(1)}, f32[4,4,64,128]{3,2,1,0:T(8,128)}, u32[]{:S(2)}) copy-start(f32[4,4,64,128]{3,2,1,0:T(8,128)} %fields.7) | copy-start | bytes 1572868
  2.7 17.4 %copy-start.1 = (f32[4,4,64,128]{3,2,1,0:T(8,128)S(1)}, f32[4,4,64,128]{3,2,1,0:T(8,128)}, u32[]{:S(2)}) copy-start(f32[4,4,64,128]{3,2,1,0:T(8,128)} %fields.7) | copy-start | bytes 1572868
  2.7 17.4 %copy-start.2 = (f32[2,128,128]{2,1,0:T(8,128)S(1)}, f32[2,128,128]{2,1,0:T(8,128)}, u32[]{:S(2)}) copy-start(f32[2,128,128]{2,1,0:T(8,128)} %deriv.1) | copy-start | bytes 393220
  2.7 17.4 %copy-start.3 = (f32[128,128]{1,0:T(8,128)S(1)}, f32[128,128]{1,0:T(8,128)}, u32[]{:S(2)}) copy-start(f32[128,128]{1,0:T(8,128)} %stiffness.1) | copy-start | bytes 196612
  2.7 17.4 %copy-start.4 = (f32[2,64,128]{2,1,0:T(8,128)S(1)}, f32[2,64,128]{2,1,0:T(8,128)}, u32[]{:S(2)}) copy-start(f32[2,64,128]{2,1,0:T(8,128)} %geom.1) | copy-start | bytes 196612
  2.7 17.4 %copy-start.5 = (f32[4,16,128]{2,1,0:T(8,128)S(1)}, f32[4,16,128]{2,1,0:T(8,128)}, u32[]{:S(2)}) copy-start(f32[4,16,128]{2,1,0:T(8,128)} %traces.1) | copy-start | bytes 98308
  2.7 17.4 %copy-start.8 = (s32[256,1]{0,1:T(1,128)S(1)}, s32[256,1]{0,1:T(1,128)}, u32[]{:S(2)}) copy-start(s32[256,1]{0,1:T(1,128)} %param.18) | copy-start | bytes 3076
  2.8 34.5 %all-to-all-start = ((f32[64,16,128]{2,1,0:T(8,128)}), f32[64,16,128]{2,1,0:T(8,128)S(1)}, u32[]{:S(2)}, u32[]{:S(2)}) async-start(f32[64,16,128]{2,1,0:T(8,128)} %bitcast), calls=%async_computation | async-start | bytes 1048576 | tf_op jit(solution)/shard_map/to_points/all_to_all | solution.py:395
  20.0 0.7 copy-start.6
  20.1 0.7 copy-start.7
  20.1 0.7 copy-start.9
  22.2 2.9 %collective-permute-start = (f32[32,128]{1,0:T(8,128)S(1)}, f32[32,128]{1,0:T(8,128)S(1)}, u32[]{:S(2)}, u32[]{:S(2)}) collective-permute-start(f32[32,128]{1,0:T(8,128)S(1)} %get-tuple-element.31), channel_id=1, source_target_pairs={{0,1},{1,2},{2,3},{3,4},{4,5},{5,6},{6,7},{7,0},{8,9},{9,10},{10,1... | collective-permute-start | bytes 49160 | tf_op jit(solution)/shard_map/base/ppermute | solution.py:400
  24.3 3.5 %collective-permute-start.1 = (f32[32,128]{1,0:T(8,128)S(1)}, f32[32,128]{1,0:T(8,128)S(1)}, u32[]{:S(2)}, u32[]{:S(2)}) collective-permute-start(f32[32,128]{1,0:T(8,128)S(1)} %get-tuple-element.32), channel_id=1, source_target_pairs={{1,0},{2,1},{3,2},{4,3},{5,4},{6,5},{7,6},{0,7},{9,8},{10,9},{11,1... | collective-permute-start | bytes 49160 | tf_op jit(solution)/shard_map/base/ppermute | solution.py:401
  37.2 1.1 %copy-start.10 = (bf16[1536,256]{1,0:T(8,128)(2,1)S(1)}, bf16[1536,256]{1,0:T(8,128)(2,1)}, u32[]{:S(2)}) copy-start(bf16[1536,256]{1,0:T(8,128)(2,1)} %constant.2.clone.tables) | copy-start | bytes 2359300
  62.9 6.7 %collective-permute-start.2 = (f32[32,128]{1,0:T(8,128)S(1)}, f32[32,128]{1,0:T(8,128)S(1)}, u32[]{:S(2)}, u32[]{:S(2)}) collective-permute-start(f32[32,128]{1,0:T(8,128)S(1)} %get-tuple-element.47), channel_id=1, source_target_pairs={{0,1},{1,2},{2,3},{3,4},{4,5},{5,6},{6,7},{7,0},{8,9},{9,10},{10,1... | collective-permute-start | bytes 49160 | tf_op jit(solution)/shard_map/solve/ppermute | solution.py:400
  68.7 3.2 %collective-permute-start.3 = (f32[32,128]{1,0:T(8,128)S(1)}, f32[32,128]{1,0:T(8,128)S(1)}, u32[]{:S(2)}, u32[]{:S(2)}) collective-permute-start(f32[32,128]{1,0:T(8,128)S(1)} %get-tuple-element.48), channel_id=1, source_target_pairs={{1,0},{2,1},{3,2},{4,3},{5,4},{6,5},{7,6},{0,7},{9,8},{10,9},{11,1... | collective-permute-start | bytes 49160 | tf_op jit(solution)/shard_map/solve/ppermute | solution.py:401

commit v3 on v2

--- a/solution.py
+++ b/solution.py
@@ -30,20 +30,12 @@
 
 
 @functools.cache
-def axial_tables():
+def axial_table():
     points = np.arange(PLANES)[:, None]
-    planes = np.arange(PLANES)[None, :]
-    mode = np.where(planes == 1, PLANES // 2, planes // 2)
-    angles = 2.0 * np.pi / PLANES * ((points * mode) % PLANES)
-    sine = (planes % 2 == 1) & (planes != 1)
-    basis = np.where(sine, np.sin(angles), np.cos(angles))
-    wave = np.where(planes >= 2, mode, 0) * AXIAL_WAVE
-    slope = wave * np.where(sine, np.cos(angles), -np.sin(angles))
-    weights = np.where(planes <= 1, 1.0 / PLANES, 2.0 / PLANES)
-    modal = -np.transpose(weights * basis)
-    both_h, both_l = halves_np(np.concatenate([basis, slope], axis=0))
-    modal_h, modal_l = halves_np(modal)
-    return np.concatenate([both_h, both_l, modal_h, modal_l], axis=0)
+    modes = np.arange(PLANES // 2)[None, :]
+    angles = 2.0 * np.pi / PLANES * ((points * modes) % PLANES)
+    others = np.where(modes == 0, 1.0 - 2.0 * (points % 2), np.sin(angles))
+    return np.concatenate(halves_np(np.concatenate([np.cos(angles), others], axis=1)), axis=0)
 
 
 def halves(value):
@@ -53,6 +45,10 @@
 
 def product(left, right):
     return jnp.dot(left, right, preferred_element_type=F32)
+
+
+def across(left, right):
+    return lax.dot_general(left, right, (((0,), (0,)), ((), ())), preferred_element_type=F32)
 
 
 def product3(left, right):
@@ -87,9 +83,10 @@
     return jnp.concatenate(halves(value), axis=1)
 
 
-def product_stacked(value, twice_h, low):
+def product_stacked(value, high, low):
     pair = stacked(value)
-    return product(pair, twice_h) + product(pair[:, : low.shape[0]], low)
+    twice = jnp.concatenate([high, high], axis=0)
+    return product(pair, twice) + product(pair[:, : low.shape[0]], low)
 
 
 def pack_kernel(fields, out):
@@ -98,29 +95,35 @@
             out[pl.ds(plane * 4 + field, ELEMS, stride=16), :] = fields[field, plane]
 
 
-def physical_kernel(fields, factors, melting, deriv_h, deriv_l, tables, out):
-    spectral = jnp.concatenate([fields[pl.ds(c, PLANES, stride=4), :] for c in range(4)], axis=1)
-    both_h, both_l, modal_h, modal_l = (
-        tables[start : start + size]
-        for start, size in ((0, 512), (512, 512), (1024, 256), (1280, 256))
-    )
-    points = product3((both_h, both_l), halves(spectral))
-    values = [points[:PLANES, c * POINTS : (c + 1) * POINTS] for c in range(4)]
+def physical_kernel(fields, factors, melting, deriv_h, deriv_l, table, out):
+    half = PLANES // 2
+    even = [fields[pl.ds(c, half, stride=8), :] for c in range(4)]
+    odd = [fields[pl.ds(4 + c, half, stride=8), :] for c in range(4)]
+    even, odd = jnp.concatenate(even, axis=1), jnp.concatenate(odd, axis=1)
+    mode = lax.broadcasted_iota(jnp.int32, (half, 4 * POINTS), 0)
+    wave = mode.astype(F32) * AXIAL_WAVE
+    spectral = jnp.concatenate(
+        [jnp.concatenate([even, wave * odd], axis=1), jnp.concatenate([odd, -wave * even], axis=1)], axis=0
+    )
+    basis = (table[:PLANES], table[PLANES:])
+    points = product3(basis, halves(spectral))
+    values = [points[:, c * POINTS : (c + 1) * POINTS] for c in range(4)]
+    axial = [points[:, c * POINTS : (c + 1) * POINTS] for c in range(4, 8)]
     first = values[0] * factors[0:1, :]
     second = values[1] * factors[1:2, :]
     third = values[2]
     terms = []
     for c in range(4):
         slopes = product_stacked(values[c], deriv_h[...], deriv_l[...])
-        term = (
-            first * slopes[:, :POINTS]
-            + second * slopes[:, POINTS:]
-            + third * points[PLANES:, c * POINTS : (c + 1) * POINTS]
-        )
+        term = first * slopes[:, :POINTS] + second * slopes[:, POINTS:] + third * axial[c]
         terms.append(term * melting[...] if c == 3 else term)
-    modal = product3((modal_h, modal_l), halves(jnp.concatenate(terms, axis=1)))
+    terms = halves(jnp.concatenate(terms, axis=1))
+    modal = across(basis[0], terms[0]) + (across(basis[1], terms[0]) + across(basis[0], terms[1]))
+    row = lax.broadcasted_iota(jnp.int32, (PLANES, 4 * POINTS), 0)
+    modal = modal * jnp.where(row % half == 0, -1.0 / PLANES, -2.0 / PLANES)
     for c in range(4):
-        out[pl.ds(c, PLANES, stride=4), :] = modal[:, c * POINTS : (c + 1) * POINTS]
+        out[pl.ds(c, half, stride=8), :] = modal[:half, c * POINTS : (c + 1) * POINTS]
+        out[pl.ds(4 + c, half, stride=8), :] = modal[half:, c * POINTS : (c + 1) * POINTS]
 
 
 def upright(row):
@@ -178,7 +181,18 @@
     return value + pltpu.roll(value, EDGES * TRACE, 1)
 
 
+def by_plane(rows):
+    return jnp.concatenate(
+        [jnp.broadcast_to(rows[plane : plane + 1], (ELEMS, POINTS)) for plane in range(OWN)], axis=0
+    )
+
+
+def by_element(rows):
+    return jnp.concatenate([rows] * OWN, axis=0)
+
+
 def start_helmholtz(vector, weights_h, weights_l, back, gather, to_rim, scale_one, scale_two):
+    scale_one, scale_two = by_plane(scale_one), by_element(scale_two)
     images = product_stacked(vector, weights_h, weights_l)
     stiff, own, doubled, crossing, stiff_trace, own_trace = (
         images[:, k * POINTS : (k + 1) * POINTS] for k in range(6)
@@ -238,7 +252,7 @@
         [stiff, own, turned_up, crossing, exact(stiff, turned_up), exact(own, turned_up)], axis=1
     )
     high, low = halves(weights)
-    weights_h[...] = jnp.concatenate([high, high], axis=0)
+    weights_h[...] = high
     weights_l[...] = low
     high, low = halves(jnp.concatenate([edges, exact(edges, turned_up)], axis=1))
     back[...] = jnp.concatenate([high, low], axis=0)
@@ -262,32 +276,32 @@
     beyond = ((edge == 1) & (near[1] == -2)) | ((edge == 3) & (near[3] == -2))
     mask = jnp.where(beyond & (lane >= lower), 1.0, 0.0)
     scale = jnp.broadcast_to(upright(scale_row[...]), (ELEMS, POINTS))
-    plane = plane_rank * OWN + lax.broadcasted_iota(jnp.int32, (ROWS, POINTS), 0) // ELEMS
+    plane = plane_rank * OWN + lax.broadcasted_iota(jnp.int32, (OWN, POINTS), 0)
     wave = jnp.where(plane == 1, PLANES // 2, plane // 2).astype(F32) * AXIAL_WAVE
     one = INVERSE_STEP + wave * wave
-    two = jnp.concatenate([scale] * OWN, axis=0)
-    rim_mask[...] = jnp.concatenate([mask] * OWN, axis=0)
+    rim_mask[...] = mask
     scale_one[...] = one
-    scale_two[...] = two
+    scale_two[...] = scale
 
     melted = upright(flags[...].astype(F32))
     melting[...] = jnp.broadcast_to(1.0 / (1.0 + LATENT * melted), (PLANES, POINTS))
     for side in range(2):
         factors[side : side + 1, :] = geom[side, pl.ds(plane_rank, 1), :]
     high, low = halves(jnp.concatenate([jnp.transpose(deriv[0]), jnp.transpose(deriv[1])], axis=1))
-    deriv_h[...] = jnp.concatenate([high, high], axis=0)
+    deriv_h[...] = high
     deriv_l[...] = low
 
     vector = fields[0].reshape(ROWS, POINTS)
     part, left, right, _ = start_helmholtz(
-        vector, weights_h[...], weights_l[...], back[...], gather[...], to_rim[...], one, two
+        vector, weights_h[...], weights_l[...], back[...], gather[...], to_rim[...], one, scale
     )
     part_out[...] = part
     left_out[...] = left
     right_out[...] = right
 
 
-def base_kernel(fields, part, left, right, from_rim, back, out):
+def base_kernel(fields, part, left, right, from_rim, back, table, out, table_out):
+    table_out[...] = table[...]
     high, low = arrived(left, right, from_rim)
     image = part[...] - rim_coupling(high, low, back[...])
     out[...] = INVERSE_STEP * fields[0].reshape(ROWS, POINTS) - image
@@ -337,25 +351,25 @@
     images = product_stacked(image, *weights)
     stiff, doubled = images[:, :POINTS], images[:, POINTS:]
     facing = doubled_sum(facing_local(two_halves(doubled), gather[...]))
-    facing = facing + (high + low) - crossing[...] * rim_mask[...]
+    facing = facing + (high + low) - crossing[...] * by_element(rim_mask[...])
     own = pltpu.roll(doubled, 2 * TRACE, 1)
     jumps = jnp.where(lanes(ROWS) >= EDGES * TRACE, own * (own - facing), 0.0)
     square = image * image
-    cubic = scale_one[...] * square + scale_two[...] * (image * stiff) + jumps
-    for number, value in enumerate((residual * residual, residual * image, square, cubic)):
-        for plane in range(OWN):
-            total = jnp.sum(value[plane * ELEMS : (plane + 1) * ELEMS], axis=0, keepdims=True)
-            for peer in range(8):
-                row = peer * 16 + number * OWN + plane
-                sums_out[row : row + 1, :] = total
+    cubic = by_plane(scale_one[...]) * square + by_element(scale_two[...]) * (image * stiff) + jumps
+    rows = [
+        jnp.sum(value[plane * ELEMS : (plane + 1) * ELEMS], axis=0, keepdims=True)
+        for value in (residual * residual, residual * image, square, cubic)
+        for plane in range(OWN)
+    ]
+    totals = jnp.sum(jnp.concatenate(rows, axis=0), axis=1, keepdims=True)
+    down = lax.broadcasted_iota(jnp.int32, (EDGES * OWN, POINTS), 0)
+    row = jnp.sum(jnp.where(down == lanes(EDGES * OWN), totals, 0.0), axis=0, keepdims=True)
+    sums_out[...] = jnp.broadcast_to(row, sums_out.shape)
 
 
 def final_kernel(sums, fields, residual, image, out):
-    total = sums[0:16, :]
-    for peer in range(1, 8):
-        total = total + sums[peer * 16 : (peer + 1) * 16, :]
-    total = jnp.sum(total, axis=1, keepdims=True)
-    m0, m1, m2, m3 = (total[k * OWN : (k + 1) * OWN] for k in range(4))
+    total = jnp.sum(sums[...], axis=0, keepdims=True)
+    m0, m1, m2, m3 = (pltpu.roll(total, (-k * OWN) % POINTS, 1) for k in range(4))
     step = m0 / m1
     after = m0 + step * (step * m2 - 2.0 * m1)
     after_image = m1 + step * (step * m3 - 2.0 * m2)
@@ -367,8 +381,8 @@
         rows = pl.ds(plane * ELEMS, ELEMS)
         out[plane] = (
             fields[0, plane]
-            + on_residual[plane : plane + 1] * residual[rows, :]
-            + on_image[plane : plane + 1] * image[rows, :]
+            + on_residual[:, plane : plane + 1] * residual[rows, :]
+            + on_image[:, plane : plane + 1] * image[rows, :]
         )
 
 
@@ -408,18 +422,18 @@
         ) = call(
             prepare_kernel,
             [
-                ((2 * POINTS, 6 * POINTS), BF16),
+                ((POINTS, 6 * POINTS), BF16),
                 ((POINTS, 6 * POINTS), BF16),
                 ((2 * POINTS, 2 * POINTS), BF16),
                 ((ELEMS, EDGES * ELEMS), BF16),
                 ((ROWS, ROWS), BF16),
                 ((ROWS, ROWS), BF16),
-                whole,
-                whole,
-                whole,
+                ((ELEMS, POINTS), F32),
+                ((OWN, POINTS), F32),
+                ((ELEMS, POINTS), F32),
                 whole,
                 ((2, POINTS), F32),
-                ((2 * POINTS, 2 * POINTS), BF16),
+                ((POINTS, 2 * POINTS), BF16),
                 ((POINTS, 2 * POINTS), BF16),
                 whole,
                 rims,
@@ -437,20 +451,22 @@
             specs=[plain] * 8 + [heat_only],
         )
         left, right = exchange(left, right)
-        (base,) = call(
+        table = jnp.asarray(axial_table())
+        base, table = call(
             base_kernel,
-            [whole],
+            [whole, (table.shape, BF16)],
             spectral_fields,
             part,
             left,
             right,
             from_rim,
             back,
-            specs=[heat_only] + [plain] * 5,
+            table,
+            specs=[heat_only] + [plain] * 6,
         )
 
     with jax.named_scope("advection"):
-        gathered, base = lax.optimization_barrier((gathered, base))
+        gathered, base, table = lax.optimization_barrier((gathered, base, table))
         (modal,) = call(
             physical_kernel,
             [((groups * 16, POINTS), F32)],
@@ -459,7 +475,7 @@
             melting,
             deriv_h,
             deriv_l,
-            jnp.asarray(axial_tables()),
+            table,
             flops=10**9,
         )
         returned = lax.all_to_all(
@@ -485,7 +501,7 @@
         left, right, momentum = lax.optimization_barrier((left, right, momentum))
         image, sums = call(
             moments_kernel,
-            [whole, ((8 * 16, POINTS), F32)],
+            [whole, ((count, POINTS), F32)],
             residual,
             part,
             left,
@@ -501,8 +517,8 @@
             scale_two,
         )
         sums = lax.all_to_all(
-            sums.reshape(8, 16, POINTS), "dom", split_axis=0, concat_axis=0, tiled=True
-        ).reshape(8 * 16, POINTS)
+            sums.reshape(count, 1, POINTS), "dom", split_axis=0, concat_axis=0, tiled=True
+        ).reshape(count, POINTS)
         (temperature,) = call(
             final_kernel,
             [((OWN, ELEMS, POINTS), F32)],

time: 83 us -> 81.7 us (0.984)
  local copies, waits for them, and re-layouts: 2.81 us -> 1.68 us
    unnamed x22, local copies, waits for them, and re-layouts: 2.81 us -> 1.68 us
where the time goes in v3:
time: 81.7 us; the launch traced here: 81.4 us
  blocking collectives  31.2 us (38%)
  starting transfers between devices  25.1 us (31%)
  waiting for transfers between devices  14.8 us (18%)
  Pallas kernels  7.9 us (10%)
  local copies, waits for them, and re-layouts  1.68 us (2%)
    all_to_all x1, blocking collectives, per_device(): lax.all_to_all(modal.reshape(groups, 16, POINTS), 'plane', split_axis=0,...  22.4 us
    all_to_all x1, starting transfers between devices, per_device(): lax.all_to_all(packed.reshape(groups, 16, POINTS), 'plane', split_axis=0,...  17.3 us
    all_to_all x1, waiting for transfers between devices, per_device(): lax.all_to_all(packed.reshape(groups, 16, POINTS), 'plane', split_axis=0,...  9.02 us
    all_to_all x1, blocking collectives, per_device(): lax.all_to_all(sums.reshape(count, 1, POINTS), 'dom', split_axis=0, conca...  8.72 us
    pallas_call x8, Pallas kernels, call(): pl.pallas_call(kernel, grid=(1,) if specs else (), out_shape=[jax.ShapeDt...  7.9 us
    ppermute x2, starting transfers between devices, exchange(): lax.ppermute(right, 'dom', [(i, (i + 1) % count) for i in range(count)])  7.82 us
    ppermute x2, waiting for transfers between devices, exchange(): lax.ppermute(left, 'dom', [((i + 1) % count, i) for i in range(count)])  4.88 us
    unnamed x22, local copies, waits for them, and re-layouts  1.68 us
  transfers between devices with their start and end apart: 5, of which 4 were waited for; matrix products, arithmetic and copies ran while one was open for 0% of the time, Pallas kernels for 3%

profile of v3, /device:TPU:1, one launch (start us, length us, event | category | flops | bytes accessed | tf_op | source)
XLA Modules:
  0.0 81.4 jit_solution(1826744905432751600)
XLA Ops:
  0.6 0.0 copy-start
  0.6 1.0 %copy-done = f32[4,4,64,128]{3,2,1,0:T(8,128)S(1)} copy-done((f32[4,4,64,128]{3,2,1,0:T(8,128)S(1)}, f32[4,4,64,128]{3,2,1,0:T(8,128)}, u32[]{:S(2)}) %copy-start) | copy-done | bytes 524312
  1.7 1.0 %to_points.1 = f32[1024,128]{1,0:T(8,128)} custom-call(f32[4,4,64,128]{3,2,1,0:T(8,128)S(1)} %copy-done), custom_call_target="tpu_custom_call" | custom-call | flops 10000000 | bytes 524288 | tf_op jit(solution)/shard_map/to_points/pallas_call | solution.py:67
  2.7 0.0 copy-start.6
  2.7 0.0 copy-start.9
  2.7 17.3 %all-to-all-start = ((f32[64,16,128]{2,1,0:T(8,128)}), f32[64,16,128]{2,1,0:T(8,128)S(1)}, u32[]{:S(2)}, u32[]{:S(2)}) async-start(f32[64,16,128]{2,1,0:T(8,128)} %bitcast), calls=%async_computation | async-start | bytes 1048576 | tf_op jit(solution)/shard_map/to_points/all_to_all | solution.py:409
  20.0 0.0 copy-start.7
  20.0 0.0 copy-start.8
  20.1 0.0 copy-start.10
  20.1 0.0 copy-done.1
  20.1 0.0 copy-done.3
  20.1 0.0 copy-done.4
  20.1 0.6 copy-done.7
  20.7 0.0 copy-done.8
  20.7 1.4 %base.2 = (bf16[128,768]{1,0:T(8,128)(2,1)S(1)}, bf16[128,768]{1,0:T(8,128)(2,1)S(1)}, bf16[256,256]{1,0:T(8,128)(2,1)S(1)}, bf16[64,256]{1,0:T(8,128)(2,1)S(1)}...) custom-call(f32[128,128]{1,0:T(8,128)S(1)} %copy-done.4, ...), custom_call_target="tpu_custom_call" | custom-call | flops 10000000 | bytes 821760 | tf_op jit(solution)/shard_map/base/pallas_call | solution.py:67
  22.2 2.1 %collective-permute-start = (f32[32,128]{1,0:T(8,128)S(1)}, f32[32,128]{1,0:T(8,128)S(1)}, u32[]{:S(2)}, u32[]{:S(2)}) collective-permute-start(f32[32,128]{1,0:T(8,128)S(1)} %get-tuple-element.34), channel_id=1, source_target_pairs={{0,1},{1,2},{2,3},{3,4},{4,5},{5,6},{6,7},{7,0},{8,9},{9,10},{10,1... | collective-permute-start | bytes 49160 | tf_op jit(solution)/shard_map/base/ppermute | solution.py:414
  24.2 0.0 collective-permute-start.1
  24.2 0.9 %collective-permute-done.left = f32[32,128]{1,0:T(8,128)S(1)} collective-permute-done((f32[32,128]{1,0:T(8,128)S(1)}, f32[32,128]{1,0:T(8,128)S(1)}, u32[]{:S(2)}, u32[]{:S(2)}) %collective-permute-start) | collective-permute-done | bytes 16416 | tf_op jit(solution)/shard_map/base/ppermute | solution.py:414
  25.1 2.6 %collective-permute-done.1.right = f32[32,128]{1,0:T(8,128)S(1)} collective-permute-done((f32[32,128]{1,0:T(8,128)S(1)}, f32[32,128]{1,0:T(8,128)S(1)}, u32[]{:S(2)}, u32[]{:S(2)}) %collective-permute-start.1) | collective-permute-done | bytes 16416 | tf_op jit(solution)/shard_map/base/ppermute | solution.py:415
  27.7 0.5 base.3
  28.2 9.0 %all-to-all-done = f32[64,16,128]{2,1,0:T(8,128)S(1)} async-done(((f32[64,16,128]{2,1,0:T(8,128)}), f32[64,16,128]{2,1,0:T(8,128)S(1)}, u32[]{:S(2)}, u32[]{:S(2)}) %all-to-all-start) | async-done | bytes 524320 | tf_op jit(solution)/shard_map/to_points/all_to_all | solution.py:409
  37.2 1.3 %advection.1 = f32[1024,128]{1,0:T(8,128)S(1)} custom-call(f32[1024,128]{1,0:T(8,128)S(1)} %bitcast.14, f32[2,128]{1,0:T(2,128)S(1)} %get-tuple-element.41.factors, f32[256,128]{1,0:T(8,128)S(1)} %get-tuple-element.42.melting, bf16[128,256]{1,0:T(8,128)(2,1)S(1)} %get-tuple-element.43.deriv_h, bf16[128,256]{1,0:T(8,128)(2,1)S(1)} %get-tuple-element.44.deriv_l, ...), custom_call_target="tpu_custom_call" | custom-call | flops 1000000000 | bytes 1049600 | tf_op jit(solution)/shard_map/advection/pallas_call | solution.py:67
  38.5 22.4 %all_to_all.15 = f32[64,16,128]{2,1,0:T(8,128)S(1)} all-to-all(f32[64,16,128]{2,1,0:T(8,128)S(1)} %bitcast.15), channel_id=1, replica_groups=mesh['plane'=64,'dom'=8] {'plane'}, dimensions={0} | all-to-all | bytes 1048576 | tf_op jit(solution)/shard_map/advection/all_to_all | solution.py:481
  60.9 0.9 %solve.4 = (f32[256,128]{1,0:T(8,128)S(1)}, f32[256,128]{1,0:T(8,128)S(1)}, f32[32,128]{1,0:T(8,128)S(1)}, f32[32,128]{1,0:T(8,128)S(1)}, f32[256,128]{1,0:T(8,128)S(1)}) custom-call(f32[1024,128]{1,0:T(8,128)S(1)} %bitcast.12, f32[256,128]{1,0:T(8,128)S(1)} %get-tuple-element.46.base, bf16[128,768]{1,0:T(8,128)(2,1)S(1)} %get-tuple-element.47.weights_h, ...), custom_call_target="tpu_custom_call" | custom-call | flops 10000000 | bytes 1378304 | tf_op jit(solution)/shard_map/solve/pallas_call | solution.py:67
  61.9 5.8 %collective-permute-start.2 = (f32[32,128]{1,0:T(8,128)S(1)}, f32[32,128]{1,0:T(8,128)S(1)}, u32[]{:S(2)}, u32[]{:S(2)}) collective-permute-start(f32[32,128]{1,0:T(8,128)S(1)} %get-tuple-element.53), channel_id=1, source_target_pairs={{0,1},{1,2},{2,3},{3,4},{4,5},{5,6},{6,7},{7,0},{8,9},{9,10},{10,1... | collective-permute-start | bytes 49160 | tf_op jit(solution)/shard_map/solve/ppermute | solution.py:414
  67.6 0.0 collective-permute-start.3
  67.6 0.9 %solve.5 = f32[3,4,64,128]{3,2,1,0:T(8,128)} custom-call(f32[1024,128]{1,0:T(8,128)S(1)} %bitcast.13), custom_call_target="tpu_custom_call" | custom-call | flops 10000000 | bytes 524288 | tf_op jit(solution)/shard_map/solve/pallas_call | solution.py:67
  68.5 0.0 collective-permute-done.2.left
  68.5 2.3 %collective-permute-done.3.right = f32[32,128]{1,0:T(8,128)S(1)} collective-permute-done((f32[32,128]{1,0:T(8,128)S(1)}, f32[32,128]{1,0:T(8,128)S(1)}, u32[]{:S(2)}, u32[]{:S(2)}) %collective-permute-start.3) | collective-permute-done | bytes 16416 | tf_op jit(solution)/shard_map/solve/ppermute | solution.py:415
  70.8 1.0 %solve.6 = (f32[256,128]{1,0:T(8,128)S(1)}, f32[8,128]{1,0:T(8,128)S(1)}) custom-call(f32[256,128]{1,0:T(8,128)S(1)} %get-tuple-element.56.residual_ref.residual, f32[256,128]{1,0:T(8,128)S(1)} %get-tuple-element.57.part, f32[32,128]{1,0:T(8,128)S(1)} %collective-permute-done.2.left, f32[32,128]{1,0:T(8,128)S(1)} %collective-permute-done.3.right, ...), custom_call_target="tpu_custom_call" | custom-call | flops 10000000 | bytes 1181696 | tf_op jit(solution)/shard_map/solve/pallas_call | solution.py:67
  71.8 8.7 %all_to_all.16 = f32[8,1,128]{2,1,0:T(1,128)S(1)} all-to-all(f32[8,1,128]{2,1,0:T(1,128)S(1)} %bitcast.17), channel_id=1, replica_groups=mesh['plane'=64,'dom'=8] {'dom'}, dimensions={0} | all-to-all | bytes 8192 | tf_op jit(solution)/shard_map/solve/all_to_all | solution.py:519
  80.5 0.9 %solve.7 = f32[4,64,128]{2,1,0:T(8,128)} custom-call(f32[8,128]{1,0:T(8,128)S(1)} %bitcast.16, f32[4,4,64,128]{3,2,1,0:T(8,128)S(1)} %copy-done.1, f32[256,128]{1,0:T(8,128)S(1)} %get-tuple-element.56.residual_ref.residual, f32[256,128]{1,0:T(8,128)S(1)} %get-tuple-element.63.image), custom_call_target="tpu_custom_call" | custom-call | flops 10000000 | bytes 790528 | tf_op jit(solution)/shard_map/solve/pallas_call | solution.py:67
  (10 shorter events, 0.0 us)
Async XLA Ops:
  0.6 1.0 %copy-start = (f32[4,4,64,128]{3,2,1,0:T(8,128)S(1)}, f32[4,4,64,128]{3,2,1,0:T(8,128)}, u32[]{:S(2)}) copy-start(f32[4,4,64,128]{3,2,1,0:T(8,128)} %fields.7) | copy-start | bytes 1572868
  2.7 17.4 %copy-start.1 = (f32[4,4,64,128]{3,2,1,0:T(8,128)S(1)}, f32[4,4,64,128]{3,2,1,0:T(8,128)}, u32[]{:S(2)}) copy-start(f32[4,4,64,128]{3,2,1,0:T(8,128)} %fields.7) | copy-start | bytes 1572868
  2.7 17.4 %copy-start.3 = (f32[2,128,128]{2,1,0:T(8,128)S(1)}, f32[2,128,128]{2,1,0:T(8,128)}, u32[]{:S(2)}) copy-start(f32[2,128,128]{2,1,0:T(8,128)} %deriv.1) | copy-start | bytes 393220
  2.7 17.4 %copy-start.4 = (f32[128,128]{1,0:T(8,128)S(1)}, f32[128,128]{1,0:T(8,128)}, u32[]{:S(2)}) copy-start(f32[128,128]{1,0:T(8,128)} %stiffness.1) | copy-start | bytes 196612
  2.7 17.4 %copy-start.5 = (f32[2,64,128]{2,1,0:T(8,128)S(1)}, f32[2,64,128]{2,1,0:T(8,128)}, u32[]{:S(2)}) copy-start(f32[2,64,128]{2,1,0:T(8,128)} %geom.1) | copy-start | bytes 196612
  2.7 17.4 %copy-start.6 = (f32[4,16,128]{2,1,0:T(8,128)S(1)}, f32[4,16,128]{2,1,0:T(8,128)}, u32[]{:S(2)}) copy-start(f32[4,16,128]{2,1,0:T(8,128)} %traces.1) | copy-start | bytes 98308
  2.7 17.4 %copy-start.9 = (s32[256,1]{0,1:T(1,128)S(1)}, s32[256,1]{0,1:T(1,128)}, u32[]{:S(2)}) copy-start(s32[256,1]{0,1:T(1,128)} %param.18) | copy-start | bytes 3076
  2.7 34.5 %all-to-all-start = ((f32[64,16,128]{2,1,0:T(8,128)}), f32[64,16,128]{2,1,0:T(8,128)S(1)}, u32[]{:S(2)}, u32[]{:S(2)}) async-start(f32[64,16,128]{2,1,0:T(8,128)} %bitcast), calls=%async_computation | async-start | bytes 1048576 | tf_op jit(solution)/shard_map/to_points/all_to_all | solution.py:409
  20.0 0.7 copy-start.7
  20.0 0.7 copy-start.8
  20.1 0.7 copy-start.10
  20.7 6.9 %copy-start.2 = (bf16[512,256]{1,0:T(8,128)(2,1)S(1)}, bf16[512,256]{1,0:T(8,128)(2,1)}, u32[]{:S(2)}) copy-start(bf16[512,256]{1,0:T(8,128)(2,1)} %constant.2.clone.table) | copy-start | bytes 786436
  22.2 2.9 %collective-permute-start = (f32[32,128]{1,0:T(8,128)S(1)}, f32[32,128]{1,0:T(8,128)S(1)}, u32[]{:S(2)}, u32[]{:S(2)}) collective-permute-start(f32[32,128]{1,0:T(8,128)S(1)} %get-tuple-element.34), channel_id=1, source_target_pairs={{0,1},{1,2},{2,3},{3,4},{4,5},{5,6},{6,7},{7,0},{8,9},{9,10},{10,1... | collective-permute-start | bytes 49160 | tf_op jit(solution)/shard_map/base/ppermute | solution.py:414
  24.2 3.5 %collective-permute-start.1 = (f32[32,128]{1,0:T(8,128)S(1)}, f32[32,128]{1,0:T(8,128)S(1)}, u32[]{:S(2)}, u32[]{:S(2)}) collective-permute-start(f32[32,128]{1,0:T(8,128)S(1)} %get-tuple-element.35), channel_id=1, source_target_pairs={{1,0},{2,1},{3,2},{4,3},{5,4},{6,5},{7,6},{0,7},{9,8},{10,9},{11,1... | collective-permute-start | bytes 49160 | tf_op jit(solution)/shard_map/base/ppermute | solution.py:415
  61.9 6.6 %collective-permute-start.2 = (f32[32,128]{1,0:T(8,128)S(1)}, f32[32,128]{1,0:T(8,128)S(1)}, u32[]{:S(2)}, u32[]{:S(2)}) collective-permute-start(f32[32,128]{1,0:T(8,128)S(1)} %get-tuple-element.53), channel_id=1, source_target_pairs={{0,1},{1,2},{2,3},{3,4},{4,5},{5,6},{6,7},{7,0},{8,9},{9,10},{10,1... | collective-permute-start | bytes 49160 | tf_op jit(solution)/shard_map/solve/ppermute | solution.py:414
  67.6 3.2 %collective-permute-start.3 = (f32[32,128]{1,0:T(8,128)S(1)}, f32[32,128]{1,0:T(8,128)S(1)}, u32[]{:S(2)}, u32[]{:S(2)}) collective-permute-start(f32[32,128]{1,0:T(8,128)S(1)} %get-tuple-element.54), channel_id=1, source_target_pairs={{1,0},{2,1},{3,2},{4,3},{5,4},{6,5},{7,6},{0,7},{9,8},{10,9},{11,1... | collective-permute-start | bytes 49160 | tf_op jit(solution)/shard_map/solve/ppermute | solution.py:415

commit v4 on v3

--- a/solution.py
+++ b/solution.py
@@ -63,12 +63,11 @@
     return (lane % (EDGES * TRACE)) // TRACE
 
 
-def call(kernel, outs, *args, flops=0, specs=None):
+def call(kernel, outs, *args, flops=0):
     return pl.pallas_call(
         kernel,
-        grid=(1,) if specs else (),
         out_shape=[jax.ShapeDtypeStruct(shape, kind) for shape, kind in outs],
-        in_specs=specs or [pl.BlockSpec(memory_space=pltpu.VMEM)] * len(args),
+        in_specs=[pl.BlockSpec(memory_space=pltpu.VMEM)] * len(args),
         out_specs=[pl.BlockSpec(memory_space=pltpu.VMEM)] * len(outs),
         compiler_params=pltpu.CompilerParams(vmem_limit_bytes=24 * 1024 * 1024),
         cost_estimate=pl.CostEstimate(
@@ -187,12 +186,18 @@
     )
 
 
+def squared_waves(number):
+    plane = lax.axis_index("plane") * OWN + number
+    wave = jnp.where(plane == 1, PLANES // 2, plane // 2).astype(F32) * AXIAL_WAVE
+    return wave * wave
+
+
 def by_element(rows):
     return jnp.concatenate([rows] * OWN, axis=0)
 
 
-def start_helmholtz(vector, weights_h, weights_l, back, gather, to_rim, scale_one, scale_two):
-    scale_one, scale_two = by_plane(scale_one), by_element(scale_two)
+def start_helmholtz(vector, weights_h, weights_l, back, gather, to_rim, scale):
+    scale = by_element(scale)
     images = product_stacked(vector, weights_h, weights_l)
     stiff, own, doubled, crossing, stiff_trace, own_trace = (
         images[:, k * POINTS : (k + 1) * POINTS] for k in range(6)
@@ -200,8 +205,8 @@
     traces_split = two_halves(doubled)
     facing = facing_local(traces_split, gather).astype(BF16)
     coupling = product(jnp.concatenate([facing, facing], axis=1), back)
-    part = scale_one * vector + scale_two * stiff + own - coupling[:, :POINTS]
-    part_trace = scale_one * doubled + scale_two * stiff_trace + own_trace - coupling[:, POINTS:]
+    part = scale * stiff + own - coupling[:, :POINTS]
+    part_trace = scale * stiff_trace + own_trace - coupling[:, POINTS:]
     split = jnp.concatenate([traces_split, two_halves(part_trace)], axis=1).astype(BF16)
     rims = product(to_rim, split)
     first, second = doubled_sum(rims[:, :POINTS]), doubled_sum(rims[:, POINTS:])
@@ -225,18 +230,33 @@
 
 def prepare_kernel(
     stiffness, traces, scale_row, near_rows, rim_rows, flags, deriv, geom, fields,
-    weights_h, weights_l, back, gather, to_rim, from_rim, rim_mask, scale_one, scale_two,
-    melting, factors, deriv_h, deriv_l, part_out, left_out, right_out,
+    weights_h, weights_l, back, gather, to_rim, from_rim, rim_mask, scale,
+    size, melting, factors, deriv_h, deriv_l, part_out, left_out, right_out,
 ):
     plane_rank = lax.axis_index("plane")
     dom_rank = lax.axis_index("dom")
     edges = traces[...].reshape(EDGES * TRACE, POINTS)
+    stiff = stiffness[...]
+    sums = jnp.sum(jnp.abs(stiff), axis=0, keepdims=True)
+    bound = 3.0 * jnp.max(sums, axis=1, keepdims=True) + 2.0 * jnp.sum(
+        jnp.sum(edges * edges, axis=0, keepdims=True), axis=1, keepdims=True
+    )
+    bound = jnp.broadcast_to(bound, (1, POINTS))
+    root = jnp.ones((1, POINTS), F32)
+    for power in (32, 16, 8, 4, 2, 1):
+        large = bound >= 4.0**power
+        bound = jnp.where(large, bound * 4.0**-power, bound)
+        root = jnp.where(large, root * 2.0**power, root)
+    root = jnp.where(bound > 1.0, root * 2.0, root)
+    size[...] = root * root
+    inverse = 1.0 / root
+    edges = edges * inverse
+    stiff = stiff * inverse * inverse
     turned = jnp.concatenate([edges[2 * TRACE :], edges[: 2 * TRACE]], axis=0)
     edges = jnp.concatenate([edges, edges], axis=0)
     turned = jnp.concatenate([turned, turned], axis=0)
     edges_up = jnp.transpose(edges)
     turned_up = jnp.transpose(turned)
-    stiff = stiffness[...]
     own = 0.5 * exact(edges_up, edges)
     down = lax.broadcasted_iota(jnp.int32, (POINTS, POINTS), 0)
     along = lanes(POINTS)
@@ -275,13 +295,8 @@
     edge = edge_of(lane)
     beyond = ((edge == 1) & (near[1] == -2)) | ((edge == 3) & (near[3] == -2))
     mask = jnp.where(beyond & (lane >= lower), 1.0, 0.0)
-    scale = jnp.broadcast_to(upright(scale_row[...]), (ELEMS, POINTS))
-    plane = plane_rank * OWN + lax.broadcasted_iota(jnp.int32, (OWN, POINTS), 0)
-    wave = jnp.where(plane == 1, PLANES // 2, plane // 2).astype(F32) * AXIAL_WAVE
-    one = INVERSE_STEP + wave * wave
     rim_mask[...] = mask
-    scale_one[...] = one
-    scale_two[...] = scale
+    scale[...] = jnp.broadcast_to(upright(scale_row[...]), (ELEMS, POINTS))
 
     melted = upright(flags[...].astype(F32))
     melting[...] = jnp.broadcast_to(1.0 / (1.0 + LATENT * melted), (PLANES, POINTS))
@@ -291,24 +306,25 @@
     deriv_h[...] = high
     deriv_l[...] = low
 
-    vector = fields[0].reshape(ROWS, POINTS)
+    vector = fields[3].reshape(ROWS, POINTS)
     part, left, right, _ = start_helmholtz(
-        vector, weights_h[...], weights_l[...], back[...], gather[...], to_rim[...], one, scale
+        vector, weights_h[...], weights_l[...], back[...], gather[...], to_rim[...], scale[...]
     )
     part_out[...] = part
     left_out[...] = left
     right_out[...] = right
 
 
-def base_kernel(fields, part, left, right, from_rim, back, table, out, table_out):
+def base_kernel(fields, part, left, right, from_rim, back, size, table, out, table_out):
     table_out[...] = table[...]
     high, low = arrived(left, right, from_rim)
     image = part[...] - rim_coupling(high, low, back[...])
-    out[...] = INVERSE_STEP * fields[0].reshape(ROWS, POINTS) - image
+    squares = by_plane(squared_waves(lax.broadcasted_iota(jnp.int32, (OWN, POINTS), 0)))
+    out[...] = -(squares * fields[3].reshape(ROWS, POINTS) + size[...] * image)
 
 
 def residual_kernel(
-    modal, base, weights_h, weights_l, back, gather, to_rim, scale_one, scale_two,
+    modal, base, weights_h, weights_l, back, gather, to_rim, scale,
     residual_out, part_out, left_out, right_out, crossing_out,
 ):
     heat = [modal[pl.ds(plane * 4 + 3, ELEMS, stride=16), :] for plane in range(OWN)]
@@ -320,8 +336,7 @@
         back[...],
         gather[...],
         to_rim[...],
-        scale_one[...],
-        scale_two[...],
+        scale[...],
     )
     left_out[...] = left
     right_out[...] = right
@@ -338,7 +353,7 @@
 
 def moments_kernel(
     residual_ref, part, left, right, crossing, from_rim, weights_h, weights_l, back, gather,
-    rim_mask, scale_one, scale_two, image_out, sums_out,
+    rim_mask, scale, image_out, sums_out,
 ):
     high, low = arrived(left, right, from_rim)
     image = part[...] - rim_coupling(high, low, back[...])
@@ -355,7 +370,7 @@
     own = pltpu.roll(doubled, 2 * TRACE, 1)
     jumps = jnp.where(lanes(ROWS) >= EDGES * TRACE, own * (own - facing), 0.0)
     square = image * image
-    cubic = by_plane(scale_one[...]) * square + by_element(scale_two[...]) * (image * stiff) + jumps
+    cubic = by_element(scale[...]) * (image * stiff) + jumps
     rows = [
         jnp.sum(value[plane * ELEMS : (plane + 1) * ELEMS], axis=0, keepdims=True)
         for value in (residual * residual, residual * image, square, cubic)
@@ -367,20 +382,25 @@
     sums_out[...] = jnp.broadcast_to(row, sums_out.shape)
 
 
-def final_kernel(sums, fields, residual, image, out):
+def final_kernel(sums, size, fields, residual, image, out):
     total = jnp.sum(sums[...], axis=0, keepdims=True)
-    m0, m1, m2, m3 = (pltpu.roll(total, (-k * OWN) % POINTS, 1) for k in range(4))
-    step = m0 / m1
-    after = m0 + step * (step * m2 - 2.0 * m1)
-    after_image = m1 + step * (step * m3 - 2.0 * m2)
-    ratio = after / m0
-    second = after / (after_image - ratio * after / step)
-    on_residual = step + second * (1.0 + ratio)
-    on_image = -second * step
+    k0, k1, k2, k3 = (pltpu.roll(total, (-k * OWN) % POINTS, 1) for k in range(4))
+    diagonal = INVERSE_STEP + squared_waves(lanes(1))
+    size = size[...]
+    step = k0 / (diagonal * k0 + size * k1)
+    theta = k1 / k0
+    norm = k2 - theta * k1
+    bent = k3 + theta * (theta * k1 - 2.0 * k2)
+    length = step * size
+    share = length * (norm / k0)
+    ratio = length * share
+    second = norm / (diagonal * norm + size * (bent - share * norm))
+    on_residual = step + second * (length * theta + ratio)
+    on_image = -second * length
     for plane in range(OWN):
         rows = pl.ds(plane * ELEMS, ELEMS)
         out[plane] = (
-            fields[0, plane]
+            fields[3, plane]
             + on_residual[:, plane : plane + 1] * residual[rows, :]
             + on_image[:, plane : plane + 1] * image[rows, :]
         )
@@ -401,8 +421,6 @@
     groups = lax.axis_size("plane")
     whole = ((ROWS, POINTS), F32)
     rims = ((RIM, POINTS), F32)
-    plain = pl.BlockSpec(memory_space=pltpu.VMEM)
-    heat_only = pl.BlockSpec((1, OWN, ELEMS, POINTS), lambda *_: (3, 0, 0, 0), memory_space=pltpu.VMEM)
 
     with jax.named_scope("to_points"):
         (packed,) = call(pack_kernel, [((ELEMS * 16, POINTS), F32)], spectral_fields)
@@ -417,8 +435,8 @@
 
     with jax.named_scope("base"):
         (
-            weights_h, weights_l, back, gather, to_rim, from_rim, rim_mask, scale_one, scale_two,
-            melting, factors, deriv_h, deriv_l, part, left, right,
+            weights_h, weights_l, back, gather, to_rim, from_rim, rim_mask, scale,
+            size, melting, factors, deriv_h, deriv_l, part, left, right,
         ) = call(
             prepare_kernel,
             [
@@ -429,8 +447,8 @@
                 ((ROWS, ROWS), BF16),
                 ((ROWS, ROWS), BF16),
                 ((ELEMS, POINTS), F32),
-                ((OWN, POINTS), F32),
                 ((ELEMS, POINTS), F32),
+                ((1, POINTS), F32),
                 whole,
                 ((2, POINTS), F32),
                 ((POINTS, 2 * POINTS), BF16),
@@ -448,7 +466,6 @@
             deriv_ops,
             geom,
             spectral_fields,
-            specs=[plain] * 8 + [heat_only],
         )
         left, right = exchange(left, right)
         table = jnp.asarray(axial_table())
@@ -461,8 +478,8 @@
             right,
             from_rim,
             back,
+            size,
             table,
-            specs=[heat_only] + [plain] * 6,
         )
 
     with jax.named_scope("advection"):
@@ -493,8 +510,7 @@
             back,
             gather,
             to_rim,
-            scale_one,
-            scale_two,
+            scale,
         )
         left, right = exchange(left, right)
         (momentum,) = call(momentum_kernel, [((3, OWN, ELEMS, POINTS), F32)], returned)
@@ -513,8 +529,7 @@
             back,
             gather,
             rim_mask,
-            scale_one,
-            scale_two,
+            scale,
         )
         sums = lax.all_to_all(
             sums.reshape(count, 1, POINTS), "dom", split_axis=0, concat_axis=0, tiled=True
@@ -523,10 +538,10 @@
             final_kernel,
             [((OWN, ELEMS, POINTS), F32)],
             sums,
+            size,
             spectral_fields,
             residual,
             image,
-            specs=[plain, heat_only, plain, plain],
         )
     return momentum, temperature
 

time: 81.7 us -> 81.7 us (level)
  transfers between devices with their start and end apart: 5 -> 5, of which waited for: 4 -> 4; matrix products, arithmetic and copies ran while one was open for 0% -> 0% of each run, Pallas kernels for 3% -> 4%
where the time goes in v4:
time: 81.7 us; the launch traced here: 81.4 us
  blocking collectives  31.2 us (38%)
  starting transfers between devices  25.1 us (31%)
  waiting for transfers between devices  14.6 us (18%)
  Pallas kernels  8.01 us (10%)
  local copies, waits for them, and re-layouts  1.68 us (2%)
    all_to_all x1, blocking collectives, per_device(): lax.all_to_all(modal.reshape(groups, 16, POINTS), 'plane', split_axis=0,...  22.4 us
    all_to_all x1, starting transfers between devices, per_device(): lax.all_to_all(packed.reshape(groups, 16, POINTS), 'plane', split_axis=0,...  17.3 us
    all_to_all x1, waiting for transfers between devices, per_device(): lax.all_to_all(packed.reshape(groups, 16, POINTS), 'plane', split_axis=0,...  8.9 us
    all_to_all x1, blocking collectives, per_device(): lax.all_to_all(sums.reshape(count, 1, POINTS), 'dom', split_axis=0, conca...  8.71 us
    pallas_call x8, Pallas kernels, call(): pl.pallas_call(kernel, out_shape=[jax.ShapeDtypeStruct(shape, kind) for s...  8.01 us
    ppermute x2, starting transfers between devices, exchange(): lax.ppermute(right, 'dom', [(i, (i + 1) % count) for i in range(count)])  7.84 us
    ppermute x2, waiting for transfers between devices, exchange(): lax.ppermute(left, 'dom', [((i + 1) % count, i) for i in range(count)])  4.88 us
    unnamed x22, local copies, waits for them, and re-layouts  1.68 us
  transfers between devices with their start and end apart: 5, of which 4 were waited for; matrix products, arithmetic and copies ran while one was open for 0% of the time, Pallas kernels for 4%

profile of v4, /device:TPU:1, one launch (start us, length us, event | category | flops | bytes accessed | tf_op | source)
XLA Modules:
  0.0 81.4 jit_solution(11419909824562058522)
XLA Ops:
  0.6 0.0 copy-start
  0.6 1.0 %copy-done = f32[4,4,64,128]{3,2,1,0:T(8,128)S(1)} copy-done((f32[4,4,64,128]{3,2,1,0:T(8,128)S(1)}, f32[4,4,64,128]{3,2,1,0:T(8,128)}, u32[]{:S(2)}) %copy-start) | copy-done | bytes 524312
  1.7 1.0 %to_points.1 = f32[1024,128]{1,0:T(8,128)} custom-call(f32[4,4,64,128]{3,2,1,0:T(8,128)S(1)} %copy-done), custom_call_target="tpu_custom_call" | custom-call | flops 10000000 | bytes 524288 | tf_op jit(solution)/shard_map/to_points/pallas_call | solution.py:67
  2.7 0.0 copy-start.6
  2.7 0.0 copy-start.9
  2.7 17.3 %all-to-all-start = ((f32[64,16,128]{2,1,0:T(8,128)}), f32[64,16,128]{2,1,0:T(8,128)S(1)}, u32[]{:S(2)}, u32[]{:S(2)}) async-start(f32[64,16,128]{2,1,0:T(8,128)} %bitcast), calls=%async_computation | async-start | bytes 1048576 | tf_op jit(solution)/shard_map/to_points/all_to_all | solution.py:427
  20.0 0.0 copy-start.7
  20.0 0.0 copy-start.8
  20.1 0.0 copy-start.10
  20.1 0.0 copy-done.1
  20.1 0.0 copy-done.3
  20.1 0.0 copy-done.4
  20.1 0.6 copy-done.7
  20.7 0.0 copy-done.8
  20.7 1.5 %base.2 = (bf16[128,768]{1,0:T(8,128)(2,1)S(1)}, bf16[128,768]{1,0:T(8,128)(2,1)S(1)}, bf16[256,256]{1,0:T(8,128)(2,1)S(1)}, bf16[64,256]{1,0:T(8,128)(2,1)S(1)}...) custom-call(f32[128,128]{1,0:T(8,128)S(1)} %copy-done.4, ...), custom_call_target="tpu_custom_call" | custom-call | flops 10000000 | bytes 821760 | tf_op jit(solution)/shard_map/base/pallas_call | solution.py:67
  22.3 2.1 %collective-permute-start = (f32[32,128]{1,0:T(8,128)S(1)}, f32[32,128]{1,0:T(8,128)S(1)}, u32[]{:S(2)}, u32[]{:S(2)}) collective-permute-start(f32[32,128]{1,0:T(8,128)S(1)} %get-tuple-element.34), channel_id=1, source_target_pairs={{0,1},{1,2},{2,3},{3,4},{4,5},{5,6},{6,7},{7,0},{8,9},{9,10},{10,1... | collective-permute-start | bytes 49160 | tf_op jit(solution)/shard_map/base/ppermute | solution.py:432
  24.3 0.0 collective-permute-start.1
  24.3 0.9 %collective-permute-done.left = f32[32,128]{1,0:T(8,128)S(1)} collective-permute-done((f32[32,128]{1,0:T(8,128)S(1)}, f32[32,128]{1,0:T(8,128)S(1)}, u32[]{:S(2)}, u32[]{:S(2)}) %collective-permute-start) | collective-permute-done | bytes 16416 | tf_op jit(solution)/shard_map/base/ppermute | solution.py:432
  25.2 2.6 %collective-permute-done.1.right = f32[32,128]{1,0:T(8,128)S(1)} collective-permute-done((f32[32,128]{1,0:T(8,128)S(1)}, f32[32,128]{1,0:T(8,128)S(1)}, u32[]{:S(2)}, u32[]{:S(2)}) %collective-permute-start.1) | collective-permute-done | bytes 16416 | tf_op jit(solution)/shard_map/base/ppermute | solution.py:433
  27.8 0.5 base.3
  28.3 8.9 %all-to-all-done = f32[64,16,128]{2,1,0:T(8,128)S(1)} async-done(((f32[64,16,128]{2,1,0:T(8,128)}), f32[64,16,128]{2,1,0:T(8,128)S(1)}, u32[]{:S(2)}, u32[]{:S(2)}) %all-to-all-start) | async-done | bytes 524320 | tf_op jit(solution)/shard_map/to_points/all_to_all | solution.py:427
  37.2 1.3 %advection.1 = f32[1024,128]{1,0:T(8,128)S(1)} custom-call(f32[1024,128]{1,0:T(8,128)S(1)} %bitcast.14, f32[2,128]{1,0:T(2,128)S(1)} %get-tuple-element.42.factors, f32[256,128]{1,0:T(8,128)S(1)} %get-tuple-element.43.melting, bf16[128,256]{1,0:T(8,128)(2,1)S(1)} %get-tuple-element.44.deriv_h, bf16[128,256]{1,0:T(8,128)(2,1)S(1)} %get-tuple-element.45.deriv_l, ...), custom_call_target="tpu_custom_call" | custom-call | flops 1000000000 | bytes 1049600 | tf_op jit(solution)/shard_map/advection/pallas_call | solution.py:67
  38.5 22.4 %all_to_all.15 = f32[64,16,128]{2,1,0:T(8,128)S(1)} all-to-all(f32[64,16,128]{2,1,0:T(8,128)S(1)} %bitcast.15), channel_id=1, replica_groups=mesh['plane'=64,'dom'=8] {'plane'}, dimensions={0} | all-to-all | bytes 1048576 | tf_op jit(solution)/shard_map/advection/all_to_all | solution.py:498
  60.9 0.9 %solve.4 = (f32[256,128]{1,0:T(8,128)S(1)}, f32[256,128]{1,0:T(8,128)S(1)}, f32[32,128]{1,0:T(8,128)S(1)}, f32[32,128]{1,0:T(8,128)S(1)}, f32[256,128]{1,0:T(8,128)S(1)}) custom-call(f32[1024,128]{1,0:T(8,128)S(1)} %bitcast.12, f32[256,128]{1,0:T(8,128)S(1)} %get-tuple-element.47.base, bf16[128,768]{1,0:T(8,128)(2,1)S(1)} %get-tuple-element.48.weights_h, ...), custom_call_target="tpu_custom_call" | custom-call | flops 10000000 | bytes 1376256 | tf_op jit(solution)/shard_map/solve/pallas_call | solution.py:67
  61.9 5.8 %collective-permute-start.2 = (f32[32,128]{1,0:T(8,128)S(1)}, f32[32,128]{1,0:T(8,128)S(1)}, u32[]{:S(2)}, u32[]{:S(2)}) collective-permute-start(f32[32,128]{1,0:T(8,128)S(1)} %get-tuple-element.53), channel_id=1, source_target_pairs={{0,1},{1,2},{2,3},{3,4},{4,5},{5,6},{6,7},{7,0},{8,9},{9,10},{10,1... | collective-permute-start | bytes 49160 | tf_op jit(solution)/shard_map/solve/ppermute | solution.py:432
  67.6 0.0 collective-permute-start.3
  67.6 0.9 %solve.5 = f32[3,4,64,128]{3,2,1,0:T(8,128)} custom-call(f32[1024,128]{1,0:T(8,128)S(1)} %bitcast.13), custom_call_target="tpu_custom_call" | custom-call | flops 10000000 | bytes 524288 | tf_op jit(solution)/shard_map/solve/pallas_call | solution.py:67
  68.5 0.0 collective-permute-done.2.left
  68.5 2.3 %collective-permute-done.3.right = f32[32,128]{1,0:T(8,128)S(1)} collective-permute-done((f32[32,128]{1,0:T(8,128)S(1)}, f32[32,128]{1,0:T(8,128)S(1)}, u32[]{:S(2)}, u32[]{:S(2)}) %collective-permute-start.3) | collective-permute-done | bytes 16416 | tf_op jit(solution)/shard_map/solve/ppermute | solution.py:433
  70.8 1.0 %solve.6 = (f32[256,128]{1,0:T(8,128)S(1)}, f32[8,128]{1,0:T(8,128)S(1)}) custom-call(f32[256,128]{1,0:T(8,128)S(1)} %get-tuple-element.56.residual_ref.residual, f32[256,128]{1,0:T(8,128)S(1)} %get-tuple-element.57.part, f32[32,128]{1,0:T(8,128)S(1)} %collective-permute-done.2.left, f32[32,128]{1,0:T(8,128)S(1)} %collective-permute-done.3.right, ...), custom_call_target="tpu_custom_call" | custom-call | flops 10000000 | bytes 1179648 | tf_op jit(solution)/shard_map/solve/pallas_call | solution.py:67
  71.8 8.7 %all_to_all.16 = f32[8,1,128]{2,1,0:T(1,128)S(1)} all-to-all(f32[8,1,128]{2,1,0:T(1,128)S(1)} %bitcast.17), channel_id=1, replica_groups=mesh['plane'=64,'dom'=8] {'dom'}, dimensions={0} | all-to-all | bytes 8192 | tf_op jit(solution)/shard_map/solve/all_to_all | solution.py:534
  80.5 0.9 %solve.7 = f32[4,64,128]{2,1,0:T(8,128)} custom-call(f32[8,128]{1,0:T(8,128)S(1)} %bitcast.16, f32[1,128]{1,0:T(1,128)S(1)} %get-tuple-element.38.size, f32[4,4,64,128]{3,2,1,0:T(8,128)S(1)} %copy-done.1, f32[256,128]{1,0:T(8,128)S(1)} %get-tuple-element.56.residual_ref.residual, f32[256,128]{1,0:T(8,128)S(1)} %get-tuple-element.63.image), custom_call_target="tpu_custom_call" | custom-call | flops 10000000 | bytes 791040 | tf_op jit(solution)/shard_map/solve/pallas_call | solution.py:67
  (10 shorter events, 0.0 us)
Async XLA Ops:
  0.6 1.0 %copy-start = (f32[4,4,64,128]{3,2,1,0:T(8,128)S(1)}, f32[4,4,64,128]{3,2,1,0:T(8,128)}, u32[]{:S(2)}) copy-start(f32[4,4,64,128]{3,2,1,0:T(8,128)} %fields.7) | copy-start | bytes 1572868
  2.7 17.4 %copy-start.1 = (f32[4,4,64,128]{3,2,1,0:T(8,128)S(1)}, f32[4,4,64,128]{3,2,1,0:T(8,128)}, u32[]{:S(2)}) copy-start(f32[4,4,64,128]{3,2,1,0:T(8,128)} %fields.7) | copy-start | bytes 1572868
  2.7 17.4 %copy-start.3 = (f32[2,128,128]{2,1,0:T(8,128)S(1)}, f32[2,128,128]{2,1,0:T(8,128)}, u32[]{:S(2)}) copy-start(f32[2,128,128]{2,1,0:T(8,128)} %deriv.1) | copy-start | bytes 393220
  2.7 17.4 %copy-start.4 = (f32[128,128]{1,0:T(8,128)S(1)}, f32[128,128]{1,0:T(8,128)}, u32[]{:S(2)}) copy-start(f32[128,128]{1,0:T(8,128)} %stiffness.1) | copy-start | bytes 196612
  2.7 17.4 %copy-start.5 = (f32[2,64,128]{2,1,0:T(8,128)S(1)}, f32[2,64,128]{2,1,0:T(8,128)}, u32[]{:S(2)}) copy-start(f32[2,64,128]{2,1,0:T(8,128)} %geom.1) | copy-start | bytes 196612
  2.7 17.4 %copy-start.6 = (f32[4,16,128]{2,1,0:T(8,128)S(1)}, f32[4,16,128]{2,1,0:T(8,128)}, u32[]{:S(2)}) copy-start(f32[4,16,128]{2,1,0:T(8,128)} %traces.1) | copy-start | bytes 98308
  2.7 17.4 %copy-start.9 = (s32[256,1]{0,1:T(1,128)S(1)}, s32[256,1]{0,1:T(1,128)}, u32[]{:S(2)}) copy-start(s32[256,1]{0,1:T(1,128)} %param.18) | copy-start | bytes 3076
  2.7 34.5 %all-to-all-start = ((f32[64,16,128]{2,1,0:T(8,128)}), f32[64,16,128]{2,1,0:T(8,128)S(1)}, u32[]{:S(2)}, u32[]{:S(2)}) async-start(f32[64,16,128]{2,1,0:T(8,128)} %bitcast), calls=%async_computation | async-start | bytes 1048576 | tf_op jit(solution)/shard_map/to_points/all_to_all | solution.py:427
  20.0 0.7 copy-start.7
  20.0 0.7 copy-start.8
  20.1 0.7 copy-start.10
  20.7 7.1 %copy-start.2 = (bf16[512,256]{1,0:T(8,128)(2,1)S(1)}, bf16[512,256]{1,0:T(8,128)(2,1)}, u32[]{:S(2)}) copy-start(bf16[512,256]{1,0:T(8,128)(2,1)} %constant.2.clone.table) | copy-start | bytes 786436
  22.3 2.9 %collective-permute-start = (f32[32,128]{1,0:T(8,128)S(1)}, f32[32,128]{1,0:T(8,128)S(1)}, u32[]{:S(2)}, u32[]{:S(2)}) collective-permute-start(f32[32,128]{1,0:T(8,128)S(1)} %get-tuple-element.34), channel_id=1, source_target_pairs={{0,1},{1,2},{2,3},{3,4},{4,5},{5,6},{6,7},{7,0},{8,9},{9,10},{10,1... | collective-permute-start | bytes 49160 | tf_op jit(solution)/shard_map/base/ppermute | solution.py:432
  24.3 3.5 %collective-permute-start.1 = (f32[32,128]{1,0:T(8,128)S(1)}, f32[32,128]{1,0:T(8,128)S(1)}, u32[]{:S(2)}, u32[]{:S(2)}) collective-permute-start(f32[32,128]{1,0:T(8,128)S(1)} %get-tuple-element.35), channel_id=1, source_target_pairs={{1,0},{2,1},{3,2},{4,3},{5,4},{6,5},{7,6},{0,7},{9,8},{10,9},{11,1... | collective-permute-start | bytes 49160 | tf_op jit(solution)/shard_map/base/ppermute | solution.py:433
  61.9 6.6 %collective-permute-start.2 = (f32[32,128]{1,0:T(8,128)S(1)}, f32[32,128]{1,0:T(8,128)S(1)}, u32[]{:S(2)}, u32[]{:S(2)}) collective-permute-start(f32[32,128]{1,0:T(8,128)S(1)} %get-tuple-element.53), channel_id=1, source_target_pairs={{0,1},{1,2},{2,3},{3,4},{4,5},{5,6},{6,7},{7,0},{8,9},{9,10},{10,1... | collective-permute-start | bytes 49160 | tf_op jit(solution)/shard_map/solve/ppermute | solution.py:432
  67.6 3.2 %collective-permute-start.3 = (f32[32,128]{1,0:T(8,128)S(1)}, f32[32,128]{1,0:T(8,128)S(1)}, u32[]{:S(2)}, u32[]{:S(2)}) collective-permute-start(f32[32,128]{1,0:T(8,128)S(1)} %get-tuple-element.54), channel_id=1, source_target_pairs={{1,0},{2,1},{3,2},{4,3},{5,4},{6,5},{7,6},{0,7},{9,8},{10,9},{11,1... | collective-permute-start | bytes 49160 | tf_op jit(solution)/shard_map/solve/ppermute | solution.py:433

commit v5 on v4

--- a/solution.py
+++ b/solution.py
@@ -212,7 +212,7 @@
     first, second = doubled_sum(rims[:, :POINTS]), doubled_sum(rims[:, POINTS:])
     rims = jnp.where(lanes(ROWS) < EDGES * TRACE, first, second)
     half = OWN * RIM
-    return part, packed_rims(rims[:half], 1), packed_rims(rims[half:], 3), crossing
+    return part, packed_rims(rims[:half], 1), packed_rims(rims[half:], 3), doubled, crossing
 
 
 def arrived(left, right, from_rim):
@@ -307,7 +307,7 @@
     deriv_l[...] = low
 
     vector = fields[3].reshape(ROWS, POINTS)
-    part, left, right, _ = start_helmholtz(
+    part, left, right, _, _ = start_helmholtz(
         vector, weights_h[...], weights_l[...], back[...], gather[...], to_rim[...], scale[...]
     )
     part_out[...] = part
@@ -325,11 +325,11 @@
 
 def residual_kernel(
     modal, base, weights_h, weights_l, back, gather, to_rim, scale,
-    residual_out, part_out, left_out, right_out, crossing_out,
+    residual_out, part_out, left_out, right_out, traces_out,
 ):
     heat = [modal[pl.ds(plane * 4 + 3, ELEMS, stride=16), :] for plane in range(OWN)]
     residual = base[...] + jnp.concatenate(heat, axis=0)
-    part, left, right, crossing = start_helmholtz(
+    part, left, right, doubled, crossing = start_helmholtz(
         residual,
         weights_h[...],
         weights_l[...],
@@ -342,67 +342,113 @@
     right_out[...] = right
     residual_out[...] = residual
     part_out[...] = part
-    crossing_out[...] = crossing
-
-
-def momentum_kernel(modal, out):
+    lower = lanes(ROWS) < EDGES * TRACE
+    traces_out[...] = jnp.where(lower, doubled, crossing)
+
+
+def momentum_kernel(modal, residual, part, out, quotients):
     for field in range(3):
         for plane in range(OWN):
             out[field, plane] = modal[pl.ds(plane * 4 + field, ELEMS, stride=16), :]
+    for plane in range(OWN):
+        rows = pl.ds(plane * ELEMS, ELEMS)
+        own = residual[rows, :]
+        above = jnp.sum(jnp.sum(own * part[rows, :], axis=0, keepdims=True), axis=1, keepdims=True)
+        below = jnp.sum(jnp.sum(own * own, axis=0, keepdims=True), axis=1, keepdims=True)
+        quotient = jnp.where(below > 0.0, above / below, 0.0)
+        quotients[plane : plane + 1, :] = jnp.broadcast_to(quotient, (1, POINTS))
+
+
+NUMBERS = 9
 
 
 def moments_kernel(
-    residual_ref, part, left, right, crossing, from_rim, weights_h, weights_l, back, gather,
-    rim_mask, scale, image_out, sums_out,
+    residual_ref, part, left, right, traces_ref, from_rim, weights_h, weights_l, back, gather,
+    rim_mask, scale, quotients, bend_out, sums_out,
 ):
     high, low = arrived(left, right, from_rim)
-    image = part[...] - rim_coupling(high, low, back[...])
-    image_out[...] = image
+    beyond = high + low
     residual = residual_ref[...]
+    bend = part[...] - rim_coupling(high, low, back[...]) - by_plane(quotients[...]) * residual
+    bend_out[...] = bend
     weights = [
         jnp.concatenate([w[:, :POINTS], w[:, 2 * POINTS : 3 * POINTS]], axis=1)
         for w in (weights_h, weights_l)
     ]
-    images = product_stacked(image, *weights)
+    images = product_stacked(bend, *weights)
     stiff, doubled = images[:, :POINTS], images[:, POINTS:]
+    traces = traces_ref[...]
     facing = doubled_sum(facing_local(two_halves(doubled), gather[...]))
-    facing = facing + (high + low) - crossing[...] * by_element(rim_mask[...])
+    facing = facing + beyond - traces * by_element(rim_mask[...])
     own = pltpu.roll(doubled, 2 * TRACE, 1)
-    jumps = jnp.where(lanes(ROWS) >= EDGES * TRACE, own * (own - facing), 0.0)
-    square = image * image
-    cubic = by_element(scale[...]) * (image * stiff) + jumps
+    upper = lanes(ROWS) >= EDGES * TRACE
+    cubic = by_element(scale[...]) * (bend * stiff) + jnp.where(upper, own * (own - facing), 0.0)
+    turned = jnp.where(
+        edge_of(lanes(ROWS)) == 3,
+        pltpu.roll(traces, 2 * TRACE, 1),
+        pltpu.roll(traces, POINTS - 2 * TRACE, 1),
+    )
+    across_rims = jnp.where(upper, own * pltpu.roll(beyond, EDGES * TRACE, 1), turned * beyond)
     rows = [
         jnp.sum(value[plane * ELEMS : (plane + 1) * ELEMS], axis=0, keepdims=True)
-        for value in (residual * residual, residual * image, square, cubic)
+        for value in (residual * residual, residual * bend, bend * bend, cubic, across_rims)
         for plane in range(OWN)
     ]
-    totals = jnp.sum(jnp.concatenate(rows, axis=0), axis=1, keepdims=True)
-    down = lax.broadcasted_iota(jnp.int32, (EDGES * OWN, POINTS), 0)
-    row = jnp.sum(jnp.where(down == lanes(EDGES * OWN), totals, 0.0), axis=0, keepdims=True)
+    whole, cut = jnp.concatenate(rows[: 4 * OWN], axis=0), jnp.concatenate(rows[4 * OWN :], axis=0)
+    lane = lanes(OWN)
+    cuts = [
+        jnp.where((edge_of(lane) == edge) & ((lane >= EDGES * TRACE) == above), cut, 0.0)
+        for above in (True, False)
+        for edge in (3, 1)
+    ]
+    totals = jnp.sum(jnp.concatenate([whole, *cuts], axis=0), axis=1, keepdims=True)
+    totals = jnp.concatenate([totals, quotients[:, 0:1], jnp.zeros((OWN, 1), F32)], axis=0)
+    down = lax.broadcasted_iota(jnp.int32, ((NUMBERS + 1) * OWN, POINTS), 0)
+    row = jnp.sum(jnp.where(down == lanes((NUMBERS + 1) * OWN), totals, 0.0), axis=0, keepdims=True)
     sums_out[...] = jnp.broadcast_to(row, sums_out.shape)
 
 
-def final_kernel(sums, size, fields, residual, image, out):
-    total = jnp.sum(sums[...], axis=0, keepdims=True)
-    k0, k1, k2, k3 = (pltpu.roll(total, (-k * OWN) % POINTS, 1) for k in range(4))
+def final_kernel(sums, size, fields, residual, bend, out):
     diagonal = INVERSE_STEP + squared_waves(lanes(1))
     size = size[...]
+    numbers = [pltpu.roll(sums[...], (-k * OWN) % POINTS, 1) for k in range(NUMBERS)]
+    square, slant, bends, cubic, bend_left, bend_right, own_left, own_right, quotient = numbers
+
+    def total(value):
+        return jnp.sum(value, axis=0, keepdims=True)
+
+    def beside(value):
+        return pltpu.roll(value, 1, 0), pltpu.roll(value, value.shape[0] - 1, 0)
+
+    k0 = total(square)
+    k1 = total(quotient * square + slant)
+    theta = k1 / k0
+    apart = theta - quotient
+    left, right = (apart - value for value in beside(apart))
+    quotient_left, quotient_right = beside(quotient)
+    norm = total(bends + apart * (apart * square - 2.0 * slant))
+    bent = total(
+        cubic
+        + quotient_left * bend_left
+        + quotient_right * bend_right
+        - 2.0 * (apart * (bends + quotient * slant) + left * bend_left + right * bend_right)
+        + apart * (apart * (slant + quotient * square) + left * own_left + right * own_right)
+    )
     step = k0 / (diagonal * k0 + size * k1)
-    theta = k1 / k0
-    norm = k2 - theta * k1
-    bent = k3 + theta * (theta * k1 - 2.0 * k2)
     length = step * size
     share = length * (norm / k0)
     ratio = length * share
     second = norm / (diagonal * norm + size * (bent - share * norm))
-    on_residual = step + second * (length * theta + ratio)
-    on_image = -second * length
+    second = jnp.where(norm > 0.0, second, 0.0)
+    here = lax.broadcasted_iota(jnp.int32, apart.shape, 0) == lax.axis_index("dom")
+    on_residual = step + second * (length * total(jnp.where(here, apart, 0.0)) + ratio)
+    on_bend = -second * length
     for plane in range(OWN):
         rows = pl.ds(plane * ELEMS, ELEMS)
         out[plane] = (
             fields[3, plane]
             + on_residual[:, plane : plane + 1] * residual[rows, :]
-            + on_image[:, plane : plane + 1] * image[rows, :]
+            + on_bend[:, plane : plane + 1] * bend[rows, :]
         )
 
 
@@ -500,7 +546,7 @@
         ).reshape(ELEMS * 16, POINTS)
 
     with jax.named_scope("solve"):
-        residual, part, left, right, crossing = call(
+        residual, part, left, right, edge_traces = call(
             residual_kernel,
             [whole, whole, rims, rims, whole],
             returned,
@@ -513,16 +559,22 @@
             scale,
         )
         left, right = exchange(left, right)
-        (momentum,) = call(momentum_kernel, [((3, OWN, ELEMS, POINTS), F32)], returned)
+        momentum, quotients = call(
+            momentum_kernel,
+            [((3, OWN, ELEMS, POINTS), F32), ((OWN, POINTS), F32)],
+            returned,
+            residual,
+            part,
+        )
         left, right, momentum = lax.optimization_barrier((left, right, momentum))
-        image, sums = call(
+        bend, sums = call(
             moments_kernel,
             [whole, ((count, POINTS), F32)],
             residual,
             part,
             left,
             right,
-            crossing,
+            edge_traces,
             from_rim,
             weights_h,
             weights_l,
@@ -530,6 +582,7 @@
             gather,
             rim_mask,
             scale,
+            quotients,
         )
         sums = lax.all_to_all(
             sums.reshape(count, 1, POINTS), "dom", split_axis=0, concat_axis=0, tiled=True
@@ -541,7 +594,7 @@
             size,
             spectral_fields,
             residual,
-            image,
+            bend,
         )
     return momentum, temperature
 

time: 81.7 us -> 81.8 us (level)
  no operation moved by 1% of the time
where the time goes in v5:
time: 81.8 us; the launch traced here: 81.5 us
  blocking collectives  31.2 us (38%)
  starting transfers between devices  25.1 us (31%)
  waiting for transfers between devices  14.6 us (18%)
  Pallas kernels  8.12 us (10%)
  local copies, waits for them, and re-layouts  1.68 us (2%)
    all_to_all x1, blocking collectives, per_device(): lax.all_to_all(modal.reshape(groups, 16, POINTS), 'plane', split_axis=0,...  22.5 us
    all_to_all x1, starting transfers between devices, per_device(): lax.all_to_all(packed.reshape(groups, 16, POINTS), 'plane', split_axis=0,...  17.3 us
    all_to_all x1, waiting for transfers between devices, per_device(): lax.all_to_all(packed.reshape(groups, 16, POINTS), 'plane', split_axis=0,...  8.89 us
    all_to_all x1, blocking collectives, per_device(): lax.all_to_all(sums.reshape(count, 1, POINTS), 'dom', split_axis=0, conca...  8.71 us
    pallas_call x8, Pallas kernels, call(): pl.pallas_call(kernel, out_shape=[jax.ShapeDtypeStruct(shape, kind) for s...  8.12 us
    ppermute x2, starting transfers between devices, exchange(): lax.ppermute(right, 'dom', [(i, (i + 1) % count) for i in range(count)])  7.84 us
    ppermute x2, waiting for transfers between devices, exchange(): lax.ppermute(left, 'dom', [((i + 1) % count, i) for i in range(count)])  4.85 us
    unnamed x22, local copies, waits for them, and re-layouts  1.68 us
  transfers between devices with their start and end apart: 5, of which 4 were waited for; matrix products, arithmetic and copies ran while one was open for 0% of the time, Pallas kernels for 4%

profile of v5, /device:TPU:1, one launch (start us, length us, event | category | flops | bytes accessed | tf_op | source)
XLA Modules:
  0.0 81.5 jit_solution(3616763285697463222)
XLA Ops:
  0.6 0.0 copy-start
  0.6 1.0 %copy-done = f32[4,4,64,128]{3,2,1,0:T(8,128)S(1)} copy-done((f32[4,4,64,128]{3,2,1,0:T(8,128)S(1)}, f32[4,4,64,128]{3,2,1,0:T(8,128)}, u32[]{:S(2)}) %copy-start) | copy-done | bytes 524312
  1.7 1.1 %to_points.1 = f32[1024,128]{1,0:T(8,128)} custom-call(f32[4,4,64,128]{3,2,1,0:T(8,128)S(1)} %copy-done), custom_call_target="tpu_custom_call" | custom-call | flops 10000000 | bytes 524288 | tf_op jit(solution)/shard_map/to_points/pallas_call | solution.py:67
  2.7 0.0 copy-start.6
  2.8 0.0 copy-start.9
  2.8 17.3 %all-to-all-start = ((f32[64,16,128]{2,1,0:T(8,128)}), f32[64,16,128]{2,1,0:T(8,128)S(1)}, u32[]{:S(2)}, u32[]{:S(2)}) async-start(f32[64,16,128]{2,1,0:T(8,128)} %bitcast), calls=%async_computation | async-start | bytes 1048576 | tf_op jit(solution)/shard_map/to_points/all_to_all | solution.py:473
  20.1 0.0 copy-start.7
  20.1 0.0 copy-start.8
  20.1 0.0 copy-start.10
  20.1 0.0 copy-done.1
  20.1 0.0 copy-done.3
  20.1 0.0 copy-done.4
  20.1 0.6 copy-done.7
  20.7 0.0 copy-done.8
  20.8 1.5 %base.2 = (bf16[128,768]{1,0:T(8,128)(2,1)S(1)}, bf16[128,768]{1,0:T(8,128)(2,1)S(1)}, bf16[256,256]{1,0:T(8,128)(2,1)S(1)}, bf16[64,256]{1,0:T(8,128)(2,1)S(1)}...) custom-call(f32[128,128]{1,0:T(8,128)S(1)} %copy-done.4, ...), custom_call_target="tpu_custom_call" | custom-call | flops 10000000 | bytes 821760 | tf_op jit(solution)/shard_map/base/pallas_call | solution.py:67
  22.3 2.1 %collective-permute-start = (f32[32,128]{1,0:T(8,128)S(1)}, f32[32,128]{1,0:T(8,128)S(1)}, u32[]{:S(2)}, u32[]{:S(2)}) collective-permute-start(f32[32,128]{1,0:T(8,128)S(1)} %get-tuple-element.36), channel_id=1, source_target_pairs={{0,1},{1,2},{2,3},{3,4},{4,5},{5,6},{6,7},{7,0},{8,9},{9,10},{10,1... | collective-permute-start | bytes 49160 | tf_op jit(solution)/shard_map/base/ppermute | solution.py:478
  24.4 0.0 collective-permute-start.1
  24.4 0.9 %collective-permute-done.left = f32[32,128]{1,0:T(8,128)S(1)} collective-permute-done((f32[32,128]{1,0:T(8,128)S(1)}, f32[32,128]{1,0:T(8,128)S(1)}, u32[]{:S(2)}, u32[]{:S(2)}) %collective-permute-start) | collective-permute-done | bytes 16416 | tf_op jit(solution)/shard_map/base/ppermute | solution.py:478
  25.2 2.6 %collective-permute-done.1.right = f32[32,128]{1,0:T(8,128)S(1)} collective-permute-done((f32[32,128]{1,0:T(8,128)S(1)}, f32[32,128]{1,0:T(8,128)S(1)}, u32[]{:S(2)}, u32[]{:S(2)}) %collective-permute-start.1) | collective-permute-done | bytes 16416 | tf_op jit(solution)/shard_map/base/ppermute | solution.py:479
  27.8 0.5 base.3
  28.3 8.9 %all-to-all-done = f32[64,16,128]{2,1,0:T(8,128)S(1)} async-done(((f32[64,16,128]{2,1,0:T(8,128)}), f32[64,16,128]{2,1,0:T(8,128)S(1)}, u32[]{:S(2)}, u32[]{:S(2)}) %all-to-all-start) | async-done | bytes 524320 | tf_op jit(solution)/shard_map/to_points/all_to_all | solution.py:473
  37.2 1.3 %advection.1 = f32[1024,128]{1,0:T(8,128)S(1)} custom-call(f32[1024,128]{1,0:T(8,128)S(1)} %bitcast.14, f32[2,128]{1,0:T(2,128)S(1)} %get-tuple-element.44.factors, f32[256,128]{1,0:T(8,128)S(1)} %get-tuple-element.45.melting, bf16[128,256]{1,0:T(8,128)(2,1)S(1)} %get-tuple-element.46.deriv_h, bf16[128,256]{1,0:T(8,128)(2,1)S(1)} %get-tuple-element.47.deriv_l, ...), custom_call_target="tpu_custom_call" | custom-call | flops 1000000000 | bytes 1049600 | tf_op jit(solution)/shard_map/advection/pallas_call | solution.py:67
  38.5 22.5 %all_to_all.15 = f32[64,16,128]{2,1,0:T(8,128)S(1)} all-to-all(f32[64,16,128]{2,1,0:T(8,128)S(1)} %bitcast.15), channel_id=1, replica_groups=mesh['plane'=64,'dom'=8] {'plane'}, dimensions={0} | all-to-all | bytes 1048576 | tf_op jit(solution)/shard_map/advection/all_to_all | solution.py:544
  61.0 0.9 %solve.4 = (f32[256,128]{1,0:T(8,128)S(1)}, f32[256,128]{1,0:T(8,128)S(1)}, f32[32,128]{1,0:T(8,128)S(1)}, f32[32,128]{1,0:T(8,128)S(1)}, f32[256,128]{1,0:T(8,128)S(1)}) custom-call(f32[1024,128]{1,0:T(8,128)S(1)} %bitcast.12, f32[256,128]{1,0:T(8,128)S(1)} %get-tuple-element.49.base, bf16[128,768]{1,0:T(8,128)(2,1)S(1)} %get-tuple-element.50.weights_h, ...), custom_call_target="tpu_custom_call" | custom-call | flops 10000000 | bytes 1376256 | tf_op jit(solution)/shard_map/solve/pallas_call | solution.py:67
  61.9 5.8 %collective-permute-start.2 = (f32[32,128]{1,0:T(8,128)S(1)}, f32[32,128]{1,0:T(8,128)S(1)}, u32[]{:S(2)}, u32[]{:S(2)}) collective-permute-start(f32[32,128]{1,0:T(8,128)S(1)} %get-tuple-element.55), channel_id=1, source_target_pairs={{0,1},{1,2},{2,3},{3,4},{4,5},{5,6},{6,7},{7,0},{8,9},{9,10},{10,1... | collective-permute-start | bytes 49160 | tf_op jit(solution)/shard_map/solve/ppermute | solution.py:478
  67.7 0.0 collective-permute-start.3
  67.7 0.9 %solve.5 = (f32[3,4,64,128]{3,2,1,0:T(8,128)}, f32[4,128]{1,0:T(4,128)S(1)}) custom-call(f32[1024,128]{1,0:T(8,128)S(1)} %bitcast.13, f32[256,128]{1,0:T(8,128)S(1)} %get-tuple-element.57.residual.residual_ref, f32[256,128]{1,0:T(8,128)S(1)} %get-tuple-element.58.part), custom_call_target="tpu_custom_call" | custom-call | flops 10000000 | bytes 786432 | tf_op jit(solution)/shard_map/solve/pallas_call | solution.py:67
  68.5 0.0 collective-permute-done.2.left
  68.6 2.3 %collective-permute-done.3.right = f32[32,128]{1,0:T(8,128)S(1)} collective-permute-done((f32[32,128]{1,0:T(8,128)S(1)}, f32[32,128]{1,0:T(8,128)S(1)}, u32[]{:S(2)}, u32[]{:S(2)}) %collective-permute-start.3) | collective-permute-done | bytes 16416 | tf_op jit(solution)/shard_map/solve/ppermute | solution.py:479
  70.8 1.1 %solve.6 = (f32[256,128]{1,0:T(8,128)S(1)}, f32[8,128]{1,0:T(8,128)S(1)}) custom-call(f32[256,128]{1,0:T(8,128)S(1)} %get-tuple-element.57.residual.residual_ref, f32[256,128]{1,0:T(8,128)S(1)} %get-tuple-element.58.part, f32[32,128]{1,0:T(8,128)S(1)} %collective-permute-done.2.left, f32[32,128]{1,0:T(8,128)S(1)} %collective-permute-done.3.right, ...), custom_call_target="tpu_custom_call" | custom-call | flops 10000000 | bytes 1181696 | tf_op jit(solution)/shard_map/solve/pallas_call | solution.py:67
  71.9 8.7 %all_to_all.16 = f32[8,1,128]{2,1,0:T(1,128)S(1)} all-to-all(f32[8,1,128]{2,1,0:T(1,128)S(1)} %bitcast.17), channel_id=1, replica_groups=mesh['plane'=64,'dom'=8] {'dom'}, dimensions={0} | all-to-all | bytes 8192 | tf_op jit(solution)/shard_map/solve/all_to_all | solution.py:587
  80.6 0.9 %solve.7 = f32[4,64,128]{2,1,0:T(8,128)} custom-call(f32[8,128]{1,0:T(8,128)S(1)} %bitcast.16, f32[1,128]{1,0:T(1,128)S(1)} %get-tuple-element.40.size, f32[4,4,64,128]{3,2,1,0:T(8,128)S(1)} %copy-done.1, f32[256,128]{1,0:T(8,128)S(1)} %get-tuple-element.57.residual.residual_ref, f32[256,128]{1,0:T(8,128)S(1)} %get-tuple-element.67.bend), custom_call_target="tpu_custom_call" | custom-call | flops 10000000 | bytes 791040 | tf_op jit(solution)/shard_map/solve/pallas_call | solution.py:67
  (10 shorter events, 0.0 us)
Async XLA Ops:
  0.6 1.0 %copy-start = (f32[4,4,64,128]{3,2,1,0:T(8,128)S(1)}, f32[4,4,64,128]{3,2,1,0:T(8,128)}, u32[]{:S(2)}) copy-start(f32[4,4,64,128]{3,2,1,0:T(8,128)} %fields.7) | copy-start | bytes 1572868
  2.7 17.4 %copy-start.1 = (f32[4,4,64,128]{3,2,1,0:T(8,128)S(1)}, f32[4,4,64,128]{3,2,1,0:T(8,128)}, u32[]{:S(2)}) copy-start(f32[4,4,64,128]{3,2,1,0:T(8,128)} %fields.7) | copy-start | bytes 1572868
  2.7 17.4 %copy-start.3 = (f32[2,128,128]{2,1,0:T(8,128)S(1)}, f32[2,128,128]{2,1,0:T(8,128)}, u32[]{:S(2)}) copy-start(f32[2,128,128]{2,1,0:T(8,128)} %deriv.1) | copy-start | bytes 393220
  2.7 17.4 %copy-start.4 = (f32[128,128]{1,0:T(8,128)S(1)}, f32[128,128]{1,0:T(8,128)}, u32[]{:S(2)}) copy-start(f32[128,128]{1,0:T(8,128)} %stiffness.1) | copy-start | bytes 196612
  2.7 17.4 %copy-start.5 = (f32[2,64,128]{2,1,0:T(8,128)S(1)}, f32[2,64,128]{2,1,0:T(8,128)}, u32[]{:S(2)}) copy-start(f32[2,64,128]{2,1,0:T(8,128)} %geom.1) | copy-start | bytes 196612
  2.7 17.4 %copy-start.6 = (f32[4,16,128]{2,1,0:T(8,128)S(1)}, f32[4,16,128]{2,1,0:T(8,128)}, u32[]{:S(2)}) copy-start(f32[4,16,128]{2,1,0:T(8,128)} %traces.1) | copy-start | bytes 98308
  2.8 17.4 %copy-start.9 = (s32[256,1]{0,1:T(1,128)S(1)}, s32[256,1]{0,1:T(1,128)}, u32[]{:S(2)}) copy-start(s32[256,1]{0,1:T(1,128)} %param.18) | copy-start | bytes 3076
  2.8 34.5 %all-to-all-start = ((f32[64,16,128]{2,1,0:T(8,128)}), f32[64,16,128]{2,1,0:T(8,128)S(1)}, u32[]{:S(2)}, u32[]{:S(2)}) async-start(f32[64,16,128]{2,1,0:T(8,128)} %bitcast), calls=%async_computation | async-start | bytes 1048576 | tf_op jit(solution)/shard_map/to_points/all_to_all | solution.py:473
  20.1 0.7 copy-start.7
  20.1 0.7 copy-start.8
  20.1 0.7 copy-start.10
  20.8 7.1 %copy-start.2 = (bf16[512,256]{1,0:T(8,128)(2,1)S(1)}, bf16[512,256]{1,0:T(8,128)(2,1)}, u32[]{:S(2)}) copy-start(bf16[512,256]{1,0:T(8,128)(2,1)} %constant.2.clone.table) | copy-start | bytes 786436
  22.3 2.9 %collective-permute-start = (f32[32,128]{1,0:T(8,128)S(1)}, f32[32,128]{1,0:T(8,128)S(1)}, u32[]{:S(2)}, u32[]{:S(2)}) collective-permute-start(f32[32,128]{1,0:T(8,128)S(1)} %get-tuple-element.36), channel_id=1, source_target_pairs={{0,1},{1,2},{2,3},{3,4},{4,5},{5,6},{6,7},{7,0},{8,9},{9,10},{10,1... | collective-permute-start | bytes 49160 | tf_op jit(solution)/shard_map/base/ppermute | solution.py:478
  24.4 3.5 %collective-permute-start.1 = (f32[32,128]{1,0:T(8,128)S(1)}, f32[32,128]{1,0:T(8,128)S(1)}, u32[]{:S(2)}, u32[]{:S(2)}) collective-permute-start(f32[32,128]{1,0:T(8,128)S(1)} %get-tuple-element.37), channel_id=1, source_target_pairs={{1,0},{2,1},{3,2},{4,3},{5,4},{6,5},{7,6},{0,7},{9,8},{10,9},{11,1... | collective-permute-start | bytes 49160 | tf_op jit(solution)/shard_map/base/ppermute | solution.py:479
  61.9 6.7 %collective-permute-start.2 = (f32[32,128]{1,0:T(8,128)S(1)}, f32[32,128]{1,0:T(8,128)S(1)}, u32[]{:S(2)}, u32[]{:S(2)}) collective-permute-start(f32[32,128]{1,0:T(8,128)S(1)} %get-tuple-element.55), channel_id=1, source_target_pairs={{0,1},{1,2},{2,3},{3,4},{4,5},{5,6},{6,7},{7,0},{8,9},{9,10},{10,1... | collective-permute-start | bytes 49160 | tf_op jit(solution)/shard_map/solve/ppermute | solution.py:478
  67.7 3.2 %collective-permute-start.3 = (f32[32,128]{1,0:T(8,128)S(1)}, f32[32,128]{1,0:T(8,128)S(1)}, u32[]{:S(2)}, u32[]{:S(2)}) collective-permute-start(f32[32,128]{1,0:T(8,128)S(1)} %get-tuple-element.56), channel_id=1, source_target_pairs={{1,0},{2,1},{3,2},{4,3},{5,4},{6,5},{7,6},{0,7},{9,8},{10,9},{11,1... | collective-permute-start | bytes 49160 | tf_op jit(solution)/shard_map/solve/ppermute | solution.py:479

commit v6 on v5

--- a/solution.py
+++ b/solution.py
@@ -88,10 +88,49 @@
     return product(pair, twice) + product(pair[:, : low.shape[0]], low)
 
 
-def pack_kernel(fields, out):
-    for plane in range(OWN):
-        for field in range(4):
-            out[pl.ds(plane * 4 + field, ELEMS, stride=16), :] = fields[field, plane]
+SLICES = 4
+
+
+def pack_kernel(fields, out, taken, packed, arrivals, departures):
+    width = ELEMS // SLICES
+    into, back = [], []
+    for part in range(SLICES):
+        elements = pl.ds(part * width, width)
+        rows = pl.ds(part * width * 16, width * 16)
+        into.append(
+            pltpu.make_async_copy(fields.at[:, :, elements, :], taken.at[:, :, elements, :], arrivals.at[part])
+        )
+        back.append(pltpu.make_async_copy(packed.at[rows, :], out.at[rows, :], departures.at[part]))
+    for copy in into:
+        copy.start()
+    for part in range(SLICES):
+        into[part].wait()
+        for plane in range(OWN):
+            for field in range(4):
+                start = part * width * 16 + plane * 4 + field
+                packed[pl.ds(start, width, stride=16), :] = taken[
+                    field, plane, part * width : (part + 1) * width, :
+                ]
+        back[part].start()
+    for copy in back:
+        copy.wait()
+
+
+def pack(fields):
+    return pl.pallas_call(
+        pack_kernel,
+        out_shape=jax.ShapeDtypeStruct((ELEMS * 16, POINTS), F32),
+        in_specs=[pl.BlockSpec(memory_space=pltpu.HBM)],
+        out_specs=pl.BlockSpec(memory_space=pltpu.HBM),
+        scratch_shapes=[
+            pltpu.VMEM((4, OWN, ELEMS, POINTS), F32),
+            pltpu.VMEM((ELEMS * 16, POINTS), F32),
+            pltpu.SemaphoreType.DMA((SLICES,)),
+            pltpu.SemaphoreType.DMA((SLICES,)),
+        ],
+        compiler_params=pltpu.CompilerParams(vmem_limit_bytes=60 * 1024 * 1024),
+        cost_estimate=pl.CostEstimate(flops=10**6, bytes_accessed=2**20, transcendentals=0),
+    )(fields)
 
 
 def physical_kernel(fields, factors, melting, deriv_h, deriv_l, table, out):
@@ -110,7 +149,7 @@
     axial = [points[:, c * POINTS : (c + 1) * POINTS] for c in range(4, 8)]
     first = values[0] * factors[0:1, :]
     second = values[1] * factors[1:2, :]
-    third = values[2]
+    third = values[2] * (-2.0 / PLANES)
     terms = []
     for c in range(4):
         slopes = product_stacked(values[c], deriv_h[...], deriv_l[...])
@@ -119,7 +158,7 @@
     terms = halves(jnp.concatenate(terms, axis=1))
     modal = across(basis[0], terms[0]) + (across(basis[1], terms[0]) + across(basis[0], terms[1]))
     row = lax.broadcasted_iota(jnp.int32, (PLANES, 4 * POINTS), 0)
-    modal = modal * jnp.where(row % half == 0, -1.0 / PLANES, -2.0 / PLANES)
+    modal = jnp.where(row % half == 0, 0.5 * modal, modal)
     for c in range(4):
         out[pl.ds(c, half, stride=8), :] = modal[:half, c * POINTS : (c + 1) * POINTS]
         out[pl.ds(4 + c, half, stride=8), :] = modal[half:, c * POINTS : (c + 1) * POINTS]
@@ -301,7 +340,7 @@
     melted = upright(flags[...].astype(F32))
     melting[...] = jnp.broadcast_to(1.0 / (1.0 + LATENT * melted), (PLANES, POINTS))
     for side in range(2):
-        factors[side : side + 1, :] = geom[side, pl.ds(plane_rank, 1), :]
+        factors[side : side + 1, :] = geom[side, pl.ds(plane_rank, 1), :] * (-2.0 / PLANES)
     high, low = halves(jnp.concatenate([jnp.transpose(deriv[0]), jnp.transpose(deriv[1])], axis=1))
     deriv_h[...] = high
     deriv_l[...] = low
@@ -469,7 +508,7 @@
     rims = ((RIM, POINTS), F32)
 
     with jax.named_scope("to_points"):
-        (packed,) = call(pack_kernel, [((ELEMS * 16, POINTS), F32)], spectral_fields)
+        packed = pack(spectral_fields)
         gathered = lax.all_to_all(
             packed.reshape(groups, 16, POINTS), "plane", split_axis=0, concat_axis=0, tiled=True
         ).reshape(groups * 16, POINTS)

time: 81.8 us -> 81.6 us (level)
  local copies, waits for them, and re-layouts: 1.68 us -> 0.66 us
  Pallas kernels: 8.12 us -> 8.98 us
    pallas_call x0 -> x1, Pallas kernels: none -> 1.86 us  [pack(): pl.pallas_call(pack_kernel, out_shape=jax.ShapeDtypeStruct((ELEMS * 16, P...]
    unnamed x22 -> x20, local copies, waits for them, and re-layouts: 1.68 us -> 0.66 us
    pallas_call x8 -> x7, Pallas kernels: 8.12 us -> 7.12 us  [call(): pl.pallas_call(kernel, out_shape=[jax.ShapeDtypeStruct(shape, kind) for s...]
where the time goes in v6:
time: 81.6 us; the launch traced here: 81.3 us
  blocking collectives  31.2 us (38%)
  starting transfers between devices  25.1 us (31%)
  waiting for transfers between devices  14.6 us (18%)
  Pallas kernels  8.98 us (11%)
    all_to_all x1, blocking collectives, per_device(): lax.all_to_all(modal.reshape(groups, 16, POINTS), 'plane', split_axis=0,...  22.5 us
    all_to_all x1, starting transfers between devices, per_device(): lax.all_to_all(packed.reshape(groups, 16, POINTS), 'plane', split_axis=0,...  17.3 us
    all_to_all x1, waiting for transfers between devices, per_device(): lax.all_to_all(packed.reshape(groups, 16, POINTS), 'plane', split_axis=0,...  8.89 us
    all_to_all x1, blocking collectives, per_device(): lax.all_to_all(sums.reshape(count, 1, POINTS), 'dom', split_axis=0, conca...  8.71 us
    ppermute x2, starting transfers between devices, exchange(): lax.ppermute(right, 'dom', [(i, (i + 1) % count) for i in range(count)])  7.81 us
    pallas_call x7, Pallas kernels, call(): pl.pallas_call(kernel, out_shape=[jax.ShapeDtypeStruct(shape, kind) for s...  7.12 us
    ppermute x2, waiting for transfers between devices, exchange(): lax.ppermute(left, 'dom', [((i + 1) % count, i) for i in range(count)])  4.85 us
    pallas_call x1, Pallas kernels, pack(): pl.pallas_call(pack_kernel, out_shape=jax.ShapeDtypeStruct((ELEMS * 16, P...  1.86 us
  transfers between devices with their start and end apart: 5, of which 4 were waited for; matrix products, arithmetic and copies ran while one was open for 0% of the time, Pallas kernels for 4%

profile of v6, /device:TPU:1, one launch (start us, length us, event | category | flops | bytes accessed | tf_op | source)
XLA Modules:
  0.0 81.3 jit_solution(15934540377283463176)
XLA Ops:
  0.6 1.9 %to_points.1 = f32[1024,128]{1,0:T(8,128)} custom-call(f32[4,4,64,128]{3,2,1,0:T(8,128)} %fields.7), custom_call_target="tpu_custom_call" | custom-call | flops 1000000 | bytes 1048576 | tf_op jit(solution)/shard_map/to_points/pallas_call | solution.py:120
  2.5 0.0 copy-start
  2.5 0.0 copy-start.2
  2.5 0.0 copy-start.3
  2.5 0.0 copy-start.4
  2.5 0.0 copy-start.5
  2.6 0.0 copy-start.8
  2.6 17.3 %all-to-all-start = ((f32[64,16,128]{2,1,0:T(8,128)}), f32[64,16,128]{2,1,0:T(8,128)S(1)}, u32[]{:S(2)}, u32[]{:S(2)}) async-start(f32[64,16,128]{2,1,0:T(8,128)} %bitcast.22), calls=%async_computation | async-start | bytes 1048576 | tf_op jit(solution)/shard_map/to_points/all_to_all | solution.py:512
  19.9 0.0 copy-start.6
  19.9 0.0 copy-start.7
  19.9 0.0 copy-start.9
  19.9 0.0 copy-done
  20.0 0.6 copy-done.6
  20.5 0.0 copy-done.7
  20.6 1.5 %base.2 = (bf16[128,768]{1,0:T(8,128)(2,1)S(1)}, bf16[128,768]{1,0:T(8,128)(2,1)S(1)}, bf16[256,256]{1,0:T(8,128)(2,1)S(1)}, bf16[64,256]{1,0:T(8,128)(2,1)S(1)}...) custom-call(f32[128,128]{1,0:T(8,128)S(1)} %copy-done.3, ...), custom_call_target="tpu_custom_call" | custom-call | flops 10000000 | bytes 821760 | tf_op jit(solution)/shard_map/base/pallas_call | solution.py:67
  22.1 2.1 %collective-permute-start = (f32[32,128]{1,0:T(8,128)S(1)}, f32[32,128]{1,0:T(8,128)S(1)}, u32[]{:S(2)}, u32[]{:S(2)}) collective-permute-start(f32[32,128]{1,0:T(8,128)S(1)} %get-tuple-element.36), channel_id=1, source_target_pairs={{0,1},{1,2},{2,3},{3,4},{4,5},{5,6},{6,7},{7,0},{8,9},{9,10},{10,1... | collective-permute-start | bytes 49160 | tf_op jit(solution)/shard_map/base/ppermute | solution.py:517
  24.2 0.0 collective-permute-start.1
  24.2 0.9 %collective-permute-done.left = f32[32,128]{1,0:T(8,128)S(1)} collective-permute-done((f32[32,128]{1,0:T(8,128)S(1)}, f32[32,128]{1,0:T(8,128)S(1)}, u32[]{:S(2)}, u32[]{:S(2)}) %collective-permute-start) | collective-permute-done | bytes 16416 | tf_op jit(solution)/shard_map/base/ppermute | solution.py:517
  25.0 2.6 %collective-permute-done.1.right = f32[32,128]{1,0:T(8,128)S(1)} collective-permute-done((f32[32,128]{1,0:T(8,128)S(1)}, f32[32,128]{1,0:T(8,128)S(1)}, u32[]{:S(2)}, u32[]{:S(2)}) %collective-permute-start.1) | collective-permute-done | bytes 16416 | tf_op jit(solution)/shard_map/base/ppermute | solution.py:518
  27.6 0.5 base.3
  28.1 8.9 %all-to-all-done = f32[64,16,128]{2,1,0:T(8,128)S(1)} async-done(((f32[64,16,128]{2,1,0:T(8,128)}), f32[64,16,128]{2,1,0:T(8,128)S(1)}, u32[]{:S(2)}, u32[]{:S(2)}) %all-to-all-start) | async-done | bytes 524320 | tf_op jit(solution)/shard_map/to_points/all_to_all | solution.py:512
  37.0 1.3 %advection.1 = f32[1024,128]{1,0:T(8,128)S(1)} custom-call(f32[1024,128]{1,0:T(8,128)S(1)} %bitcast.14, f32[2,128]{1,0:T(2,128)S(1)} %get-tuple-element.44.factors, f32[256,128]{1,0:T(8,128)S(1)} %get-tuple-element.45.melting, bf16[128,256]{1,0:T(8,128)(2,1)S(1)} %get-tuple-element.46.deriv_h, bf16[128,256]{1,0:T(8,128)(2,1)S(1)} %get-tuple-element.47.deriv_l, ...), custom_call_target="tpu_custom_call" | custom-call | flops 1000000000 | bytes 1049600 | tf_op jit(solution)/shard_map/advection/pallas_call | solution.py:67
  38.3 22.5 %all_to_all.15 = f32[64,16,128]{2,1,0:T(8,128)S(1)} all-to-all(f32[64,16,128]{2,1,0:T(8,128)S(1)} %bitcast.15), channel_id=1, replica_groups=mesh['plane'=64,'dom'=8] {'plane'}, dimensions={0} | all-to-all | bytes 1048576 | tf_op jit(solution)/shard_map/advection/all_to_all | solution.py:583
  60.8 0.9 %solve.4 = (f32[256,128]{1,0:T(8,128)S(1)}, f32[256,128]{1,0:T(8,128)S(1)}, f32[32,128]{1,0:T(8,128)S(1)}, f32[32,128]{1,0:T(8,128)S(1)}, f32[256,128]{1,0:T(8,128)S(1)}) custom-call(f32[1024,128]{1,0:T(8,128)S(1)} %bitcast.12, f32[256,128]{1,0:T(8,128)S(1)} %get-tuple-element.49.base, bf16[128,768]{1,0:T(8,128)(2,1)S(1)} %get-tuple-element.50.weights_h, ...), custom_call_target="tpu_custom_call" | custom-call | flops 10000000 | bytes 1376256 | tf_op jit(solution)/shard_map/solve/pallas_call | solution.py:67
  61.7 5.8 %collective-permute-start.2 = (f32[32,128]{1,0:T(8,128)S(1)}, f32[32,128]{1,0:T(8,128)S(1)}, u32[]{:S(2)}, u32[]{:S(2)}) collective-permute-start(f32[32,128]{1,0:T(8,128)S(1)} %get-tuple-element.55), channel_id=1, source_target_pairs={{0,1},{1,2},{2,3},{3,4},{4,5},{5,6},{6,7},{7,0},{8,9},{9,10},{10,1... | collective-permute-start | bytes 49160 | tf_op jit(solution)/shard_map/solve/ppermute | solution.py:517
  67.5 0.0 collective-permute-start.3
  67.5 0.9 %solve.5 = (f32[3,4,64,128]{3,2,1,0:T(8,128)}, f32[4,128]{1,0:T(4,128)S(1)}) custom-call(f32[1024,128]{1,0:T(8,128)S(1)} %bitcast.13, f32[256,128]{1,0:T(8,128)S(1)} %get-tuple-element.57.residual.residual_ref, f32[256,128]{1,0:T(8,128)S(1)} %get-tuple-element.58.part), custom_call_target="tpu_custom_call" | custom-call | flops 10000000 | bytes 786432 | tf_op jit(solution)/shard_map/solve/pallas_call | solution.py:67
  68.4 0.0 collective-permute-done.2.left
  68.4 2.3 %collective-permute-done.3.right = f32[32,128]{1,0:T(8,128)S(1)} collective-permute-done((f32[32,128]{1,0:T(8,128)S(1)}, f32[32,128]{1,0:T(8,128)S(1)}, u32[]{:S(2)}, u32[]{:S(2)}) %collective-permute-start.3) | collective-permute-done | bytes 16416 | tf_op jit(solution)/shard_map/solve/ppermute | solution.py:518
  70.7 1.1 %solve.6 = (f32[256,128]{1,0:T(8,128)S(1)}, f32[8,128]{1,0:T(8,128)S(1)}) custom-call(f32[256,128]{1,0:T(8,128)S(1)} %get-tuple-element.57.residual.residual_ref, f32[256,128]{1,0:T(8,128)S(1)} %get-tuple-element.58.part, f32[32,128]{1,0:T(8,128)S(1)} %collective-permute-done.2.left, f32[32,128]{1,0:T(8,128)S(1)} %collective-permute-done.3.right, ...), custom_call_target="tpu_custom_call" | custom-call | flops 10000000 | bytes 1181696 | tf_op jit(solution)/shard_map/solve/pallas_call | solution.py:67
  71.7 8.7 %all_to_all.16 = f32[8,1,128]{2,1,0:T(1,128)S(1)} all-to-all(f32[8,1,128]{2,1,0:T(1,128)S(1)} %bitcast.17), channel_id=1, replica_groups=mesh['plane'=64,'dom'=8] {'dom'}, dimensions={0} | all-to-all | bytes 8192 | tf_op jit(solution)/shard_map/solve/all_to_all | solution.py:626
  80.5 0.9 %solve.7 = f32[4,64,128]{2,1,0:T(8,128)} custom-call(f32[8,128]{1,0:T(8,128)S(1)} %bitcast.16, f32[1,128]{1,0:T(1,128)S(1)} %get-tuple-element.40.size, f32[4,4,64,128]{3,2,1,0:T(8,128)S(1)} %copy-done, f32[256,128]{1,0:T(8,128)S(1)} %get-tuple-element.57.residual.residual_ref, f32[256,128]{1,0:T(8,128)S(1)} %get-tuple-element.67.bend), custom_call_target="tpu_custom_call" | custom-call | flops 10000000 | bytes 791040 | tf_op jit(solution)/shard_map/solve/pallas_call | solution.py:67
  (8 shorter events, 0.0 us)
Async XLA Ops:
  2.5 17.4 %copy-start = (f32[4,4,64,128]{3,2,1,0:T(8,128)S(1)}, f32[4,4,64,128]{3,2,1,0:T(8,128)}, u32[]{:S(2)}) copy-start(f32[4,4,64,128]{3,2,1,0:T(8,128)} %fields.7) | copy-start | bytes 1572868
  2.5 17.4 %copy-start.2 = (f32[2,128,128]{2,1,0:T(8,128)S(1)}, f32[2,128,128]{2,1,0:T(8,128)}, u32[]{:S(2)}) copy-start(f32[2,128,128]{2,1,0:T(8,128)} %deriv.1) | copy-start | bytes 393220
  2.5 17.4 %copy-start.3 = (f32[128,128]{1,0:T(8,128)S(1)}, f32[128,128]{1,0:T(8,128)}, u32[]{:S(2)}) copy-start(f32[128,128]{1,0:T(8,128)} %stiffness.1) | copy-start | bytes 196612
  2.5 17.4 %copy-start.4 = (f32[2,64,128]{2,1,0:T(8,128)S(1)}, f32[2,64,128]{2,1,0:T(8,128)}, u32[]{:S(2)}) copy-start(f32[2,64,128]{2,1,0:T(8,128)} %geom.1) | copy-start | bytes 196612
  2.5 17.4 %copy-start.5 = (f32[4,16,128]{2,1,0:T(8,128)S(1)}, f32[4,16,128]{2,1,0:T(8,128)}, u32[]{:S(2)}) copy-start(f32[4,16,128]{2,1,0:T(8,128)} %traces.1) | copy-start | bytes 98308
  2.6 17.4 %copy-start.8 = (s32[256,1]{0,1:T(1,128)S(1)}, s32[256,1]{0,1:T(1,128)}, u32[]{:S(2)}) copy-start(s32[256,1]{0,1:T(1,128)} %param.18) | copy-start | bytes 3076
  2.6 34.5 %all-to-all-start = ((f32[64,16,128]{2,1,0:T(8,128)}), f32[64,16,128]{2,1,0:T(8,128)S(1)}, u32[]{:S(2)}, u32[]{:S(2)}) async-start(f32[64,16,128]{2,1,0:T(8,128)} %bitcast.22), calls=%async_computation | async-start | bytes 1048576 | tf_op jit(solution)/shard_map/to_points/all_to_all | solution.py:512
  19.9 0.7 copy-start.6
  19.9 0.7 copy-start.7
  19.9 0.7 copy-start.9
  20.6 7.1 %copy-start.1 = (bf16[512,256]{1,0:T(8,128)(2,1)S(1)}, bf16[512,256]{1,0:T(8,128)(2,1)}, u32[]{:S(2)}) copy-start(bf16[512,256]{1,0:T(8,128)(2,1)} %constant.2.clone.table) | copy-start | bytes 786436
  22.1 2.9 %collective-permute-start = (f32[32,128]{1,0:T(8,128)S(1)}, f32[32,128]{1,0:T(8,128)S(1)}, u32[]{:S(2)}, u32[]{:S(2)}) collective-permute-start(f32[32,128]{1,0:T(8,128)S(1)} %get-tuple-element.36), channel_id=1, source_target_pairs={{0,1},{1,2},{2,3},{3,4},{4,5},{5,6},{6,7},{7,0},{8,9},{9,10},{10,1... | collective-permute-start | bytes 49160 | tf_op jit(solution)/shard_map/base/ppermute | solution.py:517
  24.2 3.5 %collective-permute-start.1 = (f32[32,128]{1,0:T(8,128)S(1)}, f32[32,128]{1,0:T(8,128)S(1)}, u32[]{:S(2)}, u32[]{:S(2)}) collective-permute-start(f32[32,128]{1,0:T(8,128)S(1)} %get-tuple-element.37), channel_id=1, source_target_pairs={{1,0},{2,1},{3,2},{4,3},{5,4},{6,5},{7,6},{0,7},{9,8},{10,9},{11,1... | collective-permute-start | bytes 49160 | tf_op jit(solution)/shard_map/base/ppermute | solution.py:518
  61.7 6.7 %collective-permute-start.2 = (f32[32,128]{1,0:T(8,128)S(1)}, f32[32,128]{1,0:T(8,128)S(1)}, u32[]{:S(2)}, u32[]{:S(2)}) collective-permute-start(f32[32,128]{1,0:T(8,128)S(1)} %get-tuple-element.55), channel_id=1, source_target_pairs={{0,1},{1,2},{2,3},{3,4},{4,5},{5,6},{6,7},{7,0},{8,9},{9,10},{10,1... | collective-permute-start | bytes 49160 | tf_op jit(solution)/shard_map/solve/ppermute | solution.py:517
  67.5 3.2 %collective-permute-start.3 = (f32[32,128]{1,0:T(8,128)S(1)}, f32[32,128]{1,0:T(8,128)S(1)}, u32[]{:S(2)}, u32[]{:S(2)}) collective-permute-start(f32[32,128]{1,0:T(8,128)S(1)} %get-tuple-element.56), channel_id=1, source_target_pairs={{1,0},{2,1},{3,2},{4,3},{5,4},{6,5},{7,6},{0,7},{9,8},{10,9},{11,1... | collective-permute-start | bytes 49160 | tf_op jit(solution)/shard_map/solve/ppermute | solution.py:518

commit v7 on v6

--- a/solution.py
+++ b/solution.py
@@ -243,7 +243,7 @@
     )
     traces_split = two_halves(doubled)
     facing = facing_local(traces_split, gather).astype(BF16)
-    coupling = product(jnp.concatenate([facing, facing], axis=1), back)
+    coupling = product(jnp.concatenate([facing, facing], axis=1), back[:, : 2 * POINTS])
     part = scale * stiff + own - coupling[:, :POINTS]
     part_trace = scale * stiff_trace + own_trace - coupling[:, POINTS:]
     split = jnp.concatenate([traces_split, two_halves(part_trace)], axis=1).astype(BF16)
@@ -264,7 +264,7 @@
     facing = jnp.where(
         lanes(ROWS) < EDGES * TRACE, high, pltpu.roll(low, EDGES * TRACE, 1)
     ).astype(BF16)
-    return product(jnp.concatenate([facing, facing], axis=1), back[:, :POINTS])
+    return product(jnp.concatenate([facing, facing], axis=1), back)
 
 
 def prepare_kernel(
@@ -313,7 +313,7 @@
     high, low = halves(weights)
     weights_h[...] = high
     weights_l[...] = low
-    high, low = halves(jnp.concatenate([edges, exact(edges, turned_up)], axis=1))
+    high, low = halves(jnp.concatenate([edges, exact(edges, turned_up), exact(edges, stiff)], axis=1))
     back[...] = jnp.concatenate([high, low], axis=0)
 
     rows = near_rows[...]
@@ -357,7 +357,7 @@
 def base_kernel(fields, part, left, right, from_rim, back, size, table, out, table_out):
     table_out[...] = table[...]
     high, low = arrived(left, right, from_rim)
-    image = part[...] - rim_coupling(high, low, back[...])
+    image = part[...] - rim_coupling(high, low, back[:, :POINTS])
     squares = by_plane(squared_waves(lax.broadcasted_iota(jnp.int32, (OWN, POINTS), 0)))
     out[...] = -(squares * fields[3].reshape(ROWS, POINTS) + size[...] * image)
 
@@ -385,39 +385,53 @@
     traces_out[...] = jnp.where(lower, doubled, crossing)
 
 
-def momentum_kernel(modal, residual, part, out, quotients):
-    for field in range(3):
-        for plane in range(OWN):
-            out[field, plane] = modal[pl.ds(plane * 4 + field, ELEMS, stride=16), :]
+def momentum_kernel(
+    modal, residual_ref, part, weights_h, weights_l, gather, out, quotients, bend_out, stiff_out, doubled_out, facing_out
+):
+    residual = residual_ref[...]
+    rows = []
     for plane in range(OWN):
-        rows = pl.ds(plane * ELEMS, ELEMS)
-        own = residual[rows, :]
-        above = jnp.sum(jnp.sum(own * part[rows, :], axis=0, keepdims=True), axis=1, keepdims=True)
+        own = residual[plane * ELEMS : (plane + 1) * ELEMS]
+        image = part[plane * ELEMS : (plane + 1) * ELEMS, :]
+        above = jnp.sum(jnp.sum(own * image, axis=0, keepdims=True), axis=1, keepdims=True)
         below = jnp.sum(jnp.sum(own * own, axis=0, keepdims=True), axis=1, keepdims=True)
-        quotient = jnp.where(below > 0.0, above / below, 0.0)
-        quotients[plane : plane + 1, :] = jnp.broadcast_to(quotient, (1, POINTS))
-
-
-NUMBERS = 9
-
-
-def moments_kernel(
-    residual_ref, part, left, right, traces_ref, from_rim, weights_h, weights_l, back, gather,
-    rim_mask, scale, quotients, bend_out, sums_out,
-):
-    high, low = arrived(left, right, from_rim)
-    beyond = high + low
-    residual = residual_ref[...]
-    bend = part[...] - rim_coupling(high, low, back[...]) - by_plane(quotients[...]) * residual
-    bend_out[...] = bend
+        rows.append(jnp.broadcast_to(jnp.where(below > 0.0, above / below, 0.0), (1, POINTS)))
+    rows = jnp.concatenate(rows, axis=0)
+    quotients[...] = rows
+    bend = part[...] - by_plane(rows) * residual
     weights = [
         jnp.concatenate([w[:, :POINTS], w[:, 2 * POINTS : 3 * POINTS]], axis=1)
         for w in (weights_h, weights_l)
     ]
     images = product_stacked(bend, *weights)
     stiff, doubled = images[:, :POINTS], images[:, POINTS:]
+    bend_out[...] = bend
+    stiff_out[...] = stiff
+    doubled_out[...] = doubled
+    facing_out[...] = doubled_sum(facing_local(two_halves(doubled), gather[...]))
+    for field in range(3):
+        for plane in range(OWN):
+            out[field, plane] = modal[pl.ds(plane * 4 + field, ELEMS, stride=16), :]
+
+
+NUMBERS = 9
+
+
+def moments_kernel(
+    residual_ref, bend_ref, stiff_ref, doubled_ref, facing_ref, left, right, traces_ref, from_rim, back, gather,
+    rim_mask, scale, quotients, bend_out, sums_out,
+):
+    high, low = arrived(left, right, from_rim)
+    beyond = high + low
+    residual = residual_ref[...]
+    coupling = rim_coupling(high, low, back[...])
+    bend = bend_ref[...] - coupling[:, :POINTS]
+    bend_out[...] = bend
+    stiff = stiff_ref[...] - coupling[:, 2 * POINTS :]
+    more = coupling[:, POINTS : 2 * POINTS]
+    doubled = doubled_ref[...] - more
     traces = traces_ref[...]
-    facing = doubled_sum(facing_local(two_halves(doubled), gather[...]))
+    facing = facing_ref[...] - doubled_sum(facing_local(two_halves(more), gather[...]))
     facing = facing + beyond - traces * by_element(rim_mask[...])
     own = pltpu.roll(doubled, 2 * TRACE, 1)
     upper = lanes(ROWS) >= EDGES * TRACE
@@ -527,7 +541,7 @@
             [
                 ((POINTS, 6 * POINTS), BF16),
                 ((POINTS, 6 * POINTS), BF16),
-                ((2 * POINTS, 2 * POINTS), BF16),
+                ((2 * POINTS, 3 * POINTS), BF16),
                 ((ELEMS, EDGES * ELEMS), BF16),
                 ((ROWS, ROWS), BF16),
                 ((ROWS, ROWS), BF16),
@@ -598,25 +612,29 @@
             scale,
         )
         left, right = exchange(left, right)
-        momentum, quotients = call(
+        momentum, quotients, bend, stiff, doubled, facing = call(
             momentum_kernel,
-            [((3, OWN, ELEMS, POINTS), F32), ((OWN, POINTS), F32)],
+            [((3, OWN, ELEMS, POINTS), F32), ((OWN, POINTS), F32), whole, whole, whole, whole],
             returned,
             residual,
             part,
+            weights_h,
+            weights_l,
+            gather,
         )
         left, right, momentum = lax.optimization_barrier((left, right, momentum))
         bend, sums = call(
             moments_kernel,
             [whole, ((count, POINTS), F32)],
             residual,
-            part,
+            bend,
+            stiff,
+            doubled,
+            facing,
             left,
             right,
             edge_traces,
             from_rim,
-            weights_h,
-            weights_l,
             back,
             gather,
             rim_mask,

time: 81.6 us -> 81.5 us (level)
  no operation moved by 1% of the time
where the time goes in v7:
time: 81.5 us; the launch traced here: 81.2 us
  blocking collectives  31.2 us (38%)
  starting transfers between devices  25.1 us (31%)
  waiting for transfers between devices  14.1 us (17%)
  Pallas kernels  9.37 us (11%)
    all_to_all x1, blocking collectives, per_device(): lax.all_to_all(modal.reshape(groups, 16, POINTS), 'plane', split_axis=0,...  22.5 us
    all_to_all x1, starting transfers between devices, per_device(): lax.all_to_all(packed.reshape(groups, 16, POINTS), 'plane', split_axis=0,...  17.3 us
    all_to_all x1, waiting for transfers between devices, per_device(): lax.all_to_all(packed.reshape(groups, 16, POINTS), 'plane', split_axis=0,...  8.83 us
    all_to_all x1, blocking collectives, per_device(): lax.all_to_all(sums.reshape(count, 1, POINTS), 'dom', split_axis=0, conca...  8.71 us
    ppermute x2, starting transfers between devices, exchange(): lax.ppermute(right, 'dom', [(i, (i + 1) % count) for i in range(count)])  7.82 us
    pallas_call x7, Pallas kernels, call(): pl.pallas_call(kernel, out_shape=[jax.ShapeDtypeStruct(shape, kind) for s...  7.5 us
    ppermute x2, waiting for transfers between devices, exchange(): lax.ppermute(left, 'dom', [((i + 1) % count, i) for i in range(count)])  4.38 us
    pallas_call x1, Pallas kernels, pack(): pl.pallas_call(pack_kernel, out_shape=jax.ShapeDtypeStruct((ELEMS * 16, P...  1.86 us
  transfers between devices with their start and end apart: 5, of which 4 were waited for; matrix products, arithmetic and copies ran while one was open for 0% of the time, Pallas kernels for 4%

profile of v7, /device:TPU:1, one launch (start us, length us, event | category | flops | bytes accessed | tf_op | source)
XLA Modules:
  0.0 81.2 jit_solution(6801095327461094918)
XLA Ops:
  0.6 1.9 %to_points.1 = f32[1024,128]{1,0:T(8,128)} custom-call(f32[4,4,64,128]{3,2,1,0:T(8,128)} %fields.7), custom_call_target="tpu_custom_call" | custom-call | flops 1000000 | bytes 1048576 | tf_op jit(solution)/shard_map/to_points/pallas_call | solution.py:120
  2.5 0.0 copy-start
  2.5 0.0 copy-start.2
  2.5 0.0 copy-start.3
  2.5 0.0 copy-start.4
  2.5 0.0 copy-start.5
  2.6 0.0 copy-start.8
  2.6 17.3 %all-to-all-start = ((f32[64,16,128]{2,1,0:T(8,128)}), f32[64,16,128]{2,1,0:T(8,128)S(1)}, u32[]{:S(2)}, u32[]{:S(2)}) async-start(f32[64,16,128]{2,1,0:T(8,128)} %bitcast.22), calls=%async_computation | async-start | bytes 1048576 | tf_op jit(solution)/shard_map/to_points/all_to_all | solution.py:526
  19.9 0.0 copy-start.6
  19.9 0.0 copy-start.7
  19.9 0.0 copy-start.9
  19.9 0.0 copy-done
  20.0 0.6 copy-done.6
  20.5 0.0 copy-done.7
  20.6 1.6 %base.2 = (bf16[128,768]{1,0:T(8,128)(2,1)S(1)}, bf16[128,768]{1,0:T(8,128)(2,1)S(1)}, bf16[256,384]{1,0:T(8,128)(2,1)S(1)}, bf16[64,256]{1,0:T(8,128)(2,1)S(1)}...) custom-call(f32[128,128]{1,0:T(8,128)S(1)} %copy-done.3, ...), custom_call_target="tpu_custom_call" | custom-call | flops 10000000 | bytes 821760 | tf_op jit(solution)/shard_map/base/pallas_call | solution.py:67
  22.2 2.1 %collective-permute-start = (f32[32,128]{1,0:T(8,128)S(1)}, f32[32,128]{1,0:T(8,128)S(1)}, u32[]{:S(2)}, u32[]{:S(2)}) collective-permute-start(f32[32,128]{1,0:T(8,128)S(1)} %get-tuple-element.40), channel_id=1, source_target_pairs={{0,1},{1,2},{2,3},{3,4},{4,5},{5,6},{6,7},{7,0},{8,9},{9,10},{10,1... | collective-permute-start | bytes 49160 | tf_op jit(solution)/shard_map/base/ppermute | solution.py:531
  24.2 0.0 collective-permute-start.1
  24.2 0.9 %collective-permute-done.left = f32[32,128]{1,0:T(8,128)S(1)} collective-permute-done((f32[32,128]{1,0:T(8,128)S(1)}, f32[32,128]{1,0:T(8,128)S(1)}, u32[]{:S(2)}, u32[]{:S(2)}) %collective-permute-start) | collective-permute-done | bytes 16416 | tf_op jit(solution)/shard_map/base/ppermute | solution.py:531
  25.1 2.6 %collective-permute-done.1.right = f32[32,128]{1,0:T(8,128)S(1)} collective-permute-done((f32[32,128]{1,0:T(8,128)S(1)}, f32[32,128]{1,0:T(8,128)S(1)}, u32[]{:S(2)}, u32[]{:S(2)}) %collective-permute-start.1) | collective-permute-done | bytes 16416 | tf_op jit(solution)/shard_map/base/ppermute | solution.py:532
  27.7 0.5 base.3
  28.2 8.8 %all-to-all-done = f32[64,16,128]{2,1,0:T(8,128)S(1)} async-done(((f32[64,16,128]{2,1,0:T(8,128)}), f32[64,16,128]{2,1,0:T(8,128)S(1)}, u32[]{:S(2)}, u32[]{:S(2)}) %all-to-all-start) | async-done | bytes 524320 | tf_op jit(solution)/shard_map/to_points/all_to_all | solution.py:526
  37.0 1.3 %advection.1 = f32[1024,128]{1,0:T(8,128)S(1)} custom-call(f32[1024,128]{1,0:T(8,128)S(1)} %bitcast.14, f32[2,128]{1,0:T(2,128)S(1)} %get-tuple-element.48.factors, f32[256,128]{1,0:T(8,128)S(1)} %get-tuple-element.49.melting, bf16[128,256]{1,0:T(8,128)(2,1)S(1)} %get-tuple-element.50.deriv_h, bf16[128,256]{1,0:T(8,128)(2,1)S(1)} %get-tuple-element.51.deriv_l, ...), custom_call_target="tpu_custom_call" | custom-call | flops 1000000000 | bytes 1049600 | tf_op jit(solution)/shard_map/advection/pallas_call | solution.py:67
  38.3 22.5 %all_to_all.15 = f32[64,16,128]{2,1,0:T(8,128)S(1)} all-to-all(f32[64,16,128]{2,1,0:T(8,128)S(1)} %bitcast.15), channel_id=1, replica_groups=mesh['plane'=64,'dom'=8] {'plane'}, dimensions={0} | all-to-all | bytes 1048576 | tf_op jit(solution)/shard_map/advection/all_to_all | solution.py:597
  60.8 0.9 %solve.4 = (f32[256,128]{1,0:T(8,128)S(1)}, f32[256,128]{1,0:T(8,128)S(1)}, f32[32,128]{1,0:T(8,128)S(1)}, f32[32,128]{1,0:T(8,128)S(1)}, f32[256,128]{1,0:T(8,128)S(1)}) custom-call(f32[1024,128]{1,0:T(8,128)S(1)} %bitcast.12, f32[256,128]{1,0:T(8,128)S(1)} %get-tuple-element.53.base, bf16[128,768]{1,0:T(8,128)(2,1)S(1)} %get-tuple-element.54.weights_h, ...), custom_call_target="tpu_custom_call" | custom-call | flops 10000000 | bytes 1441792 | tf_op jit(solution)/shard_map/solve/pallas_call | solution.py:67
  61.7 5.8 %collective-permute-start.2 = (f32[32,128]{1,0:T(8,128)S(1)}, f32[32,128]{1,0:T(8,128)S(1)}, u32[]{:S(2)}, u32[]{:S(2)}) collective-permute-start(f32[32,128]{1,0:T(8,128)S(1)} %get-tuple-element.59), channel_id=1, source_target_pairs={{0,1},{1,2},{2,3},{3,4},{4,5},{5,6},{6,7},{7,0},{8,9},{9,10},{10,1... | collective-permute-start | bytes 49160 | tf_op jit(solution)/shard_map/solve/ppermute | solution.py:531
  67.5 0.0 collective-permute-start.3
  67.5 1.4 %solve.5 = (f32[3,4,64,128]{3,2,1,0:T(8,128)}, f32[4,128]{1,0:T(4,128)S(1)}, f32[256,128]{1,0:T(8,128)S(1)}, f32[256,128]{1,0:T(8,128)S(1)}, f32[256,128]{1,0:T(8,128)S(1)}, /*index=5*/f32[256,128]{1,0:T(8,128)S(1)}) custom-call(f32[1024,128]{1,0:T(8,128)S(1)} %bitcast.13, f32[256,128]{1,0:T(8,128)S(1)} %get-tuple-element.61.residual_ref.residual, ...), custom_call_target="tpu_custom_call" | custom-call | flops 10000000 | bytes 1212416 | tf_op jit(solution)/shard_map/solve/pallas_call | solution.py:67
  68.9 0.0 collective-permute-done.2.left
  68.9 1.8 %collective-permute-done.3.right = f32[32,128]{1,0:T(8,128)S(1)} collective-permute-done((f32[32,128]{1,0:T(8,128)S(1)}, f32[32,128]{1,0:T(8,128)S(1)}, u32[]{:S(2)}, u32[]{:S(2)}) %collective-permute-start.3) | collective-permute-done | bytes 16416 | tf_op jit(solution)/shard_map/solve/ppermute | solution.py:532
  70.7 0.9 %solve.6 = (f32[256,128]{1,0:T(8,128)S(1)}, f32[8,128]{1,0:T(8,128)S(1)}) custom-call(f32[256,128]{1,0:T(8,128)S(1)} %get-tuple-element.61.residual_ref.residual, f32[256,128]{1,0:T(8,128)S(1)} %get-tuple-element.65.bend_ref, f32[256,128]{1,0:T(8,128)S(1)} %get-tuple-element.66.stiff_ref, f32[256,128]{1,0:T(8,128)S(1)} %get-tuple-element.67.doubled_ref, ...), custom_call_target="tpu_custom_call" | custom-call | flops 10000000 | bytes 1247232 | tf_op jit(solution)/shard_map/solve/pallas_call | solution.py:67
  71.6 8.7 %all_to_all.16 = f32[8,1,128]{2,1,0:T(1,128)S(1)} all-to-all(f32[8,1,128]{2,1,0:T(1,128)S(1)} %bitcast.17), channel_id=1, replica_groups=mesh['plane'=64,'dom'=8] {'dom'}, dimensions={0} | all-to-all | bytes 8192 | tf_op jit(solution)/shard_map/solve/all_to_all | solution.py:644
  80.3 0.9 %solve.7 = f32[4,64,128]{2,1,0:T(8,128)} custom-call(f32[8,128]{1,0:T(8,128)S(1)} %bitcast.16, f32[1,128]{1,0:T(1,128)S(1)} %get-tuple-element.44.size, f32[4,4,64,128]{3,2,1,0:T(8,128)S(1)} %copy-done, f32[256,128]{1,0:T(8,128)S(1)} %get-tuple-element.61.residual_ref.residual, f32[256,128]{1,0:T(8,128)S(1)} %get-tuple-element.75.bend), custom_call_target="tpu_custom_call" | custom-call | flops 10000000 | bytes 791040 | tf_op jit(solution)/shard_map/solve/pallas_call | solution.py:67
  (8 shorter events, 0.0 us)
Async XLA Ops:
  2.5 17.4 %copy-start = (f32[4,4,64,128]{3,2,1,0:T(8,128)S(1)}, f32[4,4,64,128]{3,2,1,0:T(8,128)}, u32[]{:S(2)}) copy-start(f32[4,4,64,128]{3,2,1,0:T(8,128)} %fields.7) | copy-start | bytes 1572868
  2.5 17.4 %copy-start.2 = (f32[2,128,128]{2,1,0:T(8,128)S(1)}, f32[2,128,128]{2,1,0:T(8,128)}, u32[]{:S(2)}) copy-start(f32[2,128,128]{2,1,0:T(8,128)} %deriv.1) | copy-start | bytes 393220
  2.5 17.4 %copy-start.3 = (f32[128,128]{1,0:T(8,128)S(1)}, f32[128,128]{1,0:T(8,128)}, u32[]{:S(2)}) copy-start(f32[128,128]{1,0:T(8,128)} %stiffness.1) | copy-start | bytes 196612
  2.5 17.4 %copy-start.4 = (f32[2,64,128]{2,1,0:T(8,128)S(1)}, f32[2,64,128]{2,1,0:T(8,128)}, u32[]{:S(2)}) copy-start(f32[2,64,128]{2,1,0:T(8,128)} %geom.1) | copy-start | bytes 196612
  2.5 17.4 %copy-start.5 = (f32[4,16,128]{2,1,0:T(8,128)S(1)}, f32[4,16,128]{2,1,0:T(8,128)}, u32[]{:S(2)}) copy-start(f32[4,16,128]{2,1,0:T(8,128)} %traces.1) | copy-start | bytes 98308
  2.6 17.4 %copy-start.8 = (s32[256,1]{0,1:T(1,128)S(1)}, s32[256,1]{0,1:T(1,128)}, u32[]{:S(2)}) copy-start(s32[256,1]{0,1:T(1,128)} %param.18) | copy-start | bytes 3076
  2.6 34.5 %all-to-all-start = ((f32[64,16,128]{2,1,0:T(8,128)}), f32[64,16,128]{2,1,0:T(8,128)S(1)}, u32[]{:S(2)}, u32[]{:S(2)}) async-start(f32[64,16,128]{2,1,0:T(8,128)} %bitcast.22), calls=%async_computation | async-start | bytes 1048576 | tf_op jit(solution)/shard_map/to_points/all_to_all | solution.py:526
  19.9 0.7 copy-start.6
  19.9 0.7 copy-start.7
  19.9 0.7 copy-start.9
  20.6 7.1 %copy-start.1 = (bf16[512,256]{1,0:T(8,128)(2,1)S(1)}, bf16[512,256]{1,0:T(8,128)(2,1)}, u32[]{:S(2)}) copy-start(bf16[512,256]{1,0:T(8,128)(2,1)} %constant.2.clone.table) | copy-start | bytes 786436
  22.2 2.9 %collective-permute-start = (f32[32,128]{1,0:T(8,128)S(1)}, f32[32,128]{1,0:T(8,128)S(1)}, u32[]{:S(2)}, u32[]{:S(2)}) collective-permute-start(f32[32,128]{1,0:T(8,128)S(1)} %get-tuple-element.40), channel_id=1, source_target_pairs={{0,1},{1,2},{2,3},{3,4},{4,5},{5,6},{6,7},{7,0},{8,9},{9,10},{10,1... | collective-permute-start | bytes 49160 | tf_op jit(solution)/shard_map/base/ppermute | solution.py:531
  24.2 3.5 %collective-permute-start.1 = (f32[32,128]{1,0:T(8,128)S(1)}, f32[32,128]{1,0:T(8,128)S(1)}, u32[]{:S(2)}, u32[]{:S(2)}) collective-permute-start(f32[32,128]{1,0:T(8,128)S(1)} %get-tuple-element.41), channel_id=1, source_target_pairs={{1,0},{2,1},{3,2},{4,3},{5,4},{6,5},{7,6},{0,7},{9,8},{10,9},{11,1... | collective-permute-start | bytes 49160 | tf_op jit(solution)/shard_map/base/ppermute | solution.py:532
  61.7 7.1 %collective-permute-start.2 = (f32[32,128]{1,0:T(8,128)S(1)}, f32[32,128]{1,0:T(8,128)S(1)}, u32[]{:S(2)}, u32[]{:S(2)}) collective-permute-start(f32[32,128]{1,0:T(8,128)S(1)} %get-tuple-element.59), channel_id=1, source_target_pairs={{0,1},{1,2},{2,3},{3,4},{4,5},{5,6},{6,7},{7,0},{8,9},{9,10},{10,1... | collective-permute-start | bytes 49160 | tf_op jit(solution)/shard_map/solve/ppermute | solution.py:531
  67.5 3.2 %collective-permute-start.3 = (f32[32,128]{1,0:T(8,128)S(1)}, f32[32,128]{1,0:T(8,128)S(1)}, u32[]{:S(2)}, u32[]{:S(2)}) collective-permute-start(f32[32,128]{1,0:T(8,128)S(1)} %get-tuple-element.60), channel_id=1, source_target_pairs={{1,0},{2,1},{3,2},{4,3},{5,4},{6,5},{7,6},{0,7},{9,8},{10,9},{11,1... | collective-permute-start | bytes 49160 | tf_op jit(solution)/shard_map/solve/ppermute | solution.py:532
